TPU v7x, 32 devices: a whole 2x2x4 slice. The times are simulated.
32 devices in a mesh: groups: 1, ctx: 16 (over z, y, x), tp: 2 (over core).
Axes of the slice: x: 2, y: 2, z: 4, core: 2. Of those that a mesh axis runs over, the one named last changes fastest.
Arguments:
- queries: bfloat16 [4, 32, 64, 128], P('groups', 'ctx', 'tp'), may hold values from -100 to 100
- cand_keys: bfloat16 [4, 32, 8, 128], P('groups', 'ctx', 'tp'), may hold values from -4 to 4
- candidate_values: bfloat16 [4, 32, 8, 128], P('groups', 'ctx', 'tp'), may hold values from -5 to 5
- cached_prompt_keys: bfloat16 [256, 128, 8, 128], P(('groups', 'ctx'), None, 'tp'), may hold values from -4 to 4
- cached_prompt_values: bfloat16 [256, 128, 8, 128], P(('groups', 'ctx'), None, 'tp'), may hold values from -5 to 5
- block_lists: int32 [4, 128], P('groups'), may hold values from 0 to 255, as said below
- out_weight: bfloat16 [8192, 8192], P('tp', 'ctx'), may hold values from -0.0625 to 0.0625
Outputs:
- verified: bfloat16 [4, 32, 8192], P('groups', 'tp', 'ctx')
Inputs may be any that keep to these rules, and one draw needn't show every extreme that they name: `block_lists`: each row holds 128 distinct block numbers in increasing order; among blocks 16 * c to 16 * (c + 1) - 1 a row has at most 16 entries, exactly 16 for some c in every row; all rows together have at most 40 entries in one such range, exactly 40 in some.
All inputs are finite; a program needn't handle non-finite values.
Results may differ from a plain program's by a relative error of at most 0.022.
Values may be sent and summed in bfloat16 or wider, within the bound.
No kernel may reach another device: no remote copies, remote signals or barrier semaphores. Data moves between devices by JAX's collectives and lax.ppermute only.
A program may use at most 128 MiB of HBM per device.

v0:
```python
import jax
import jax.numpy as jnp
from jax import lax
from jax.sharding import PartitionSpec as P

NEGATIVE = -1e30


def masked_softmax(scores, visible):
    scores = jnp.where(visible, scores, NEGATIVE)
    maxima = jnp.max(scores, axis=-1)
    weights = jnp.where(visible, jnp.exp(scores - maxima[..., None]), 0.0)
    return (weights, maxima, jnp.sum(weights, axis=-1))


def heads_last(stats):
    kv_count, query_group_width, row_count = stats.shape
    return jnp.transpose(stats, (2, 0, 1)).reshape(row_count, kv_count * query_group_width)


def block_terms(query_matrix, block_keys, block_values, visible, factor):
    row_count, kv_count, query_group_width, head_size = query_matrix.shape
    scores = (
        jnp.einsum("nkgd,mkd->kgnm", query_matrix, block_keys, preferred_element_type=jnp.float32)
        * factor
    )
    weights, maxima, denominator = masked_softmax(scores, visible)
    numerator = jnp.einsum(
        "kgnm,mkd->nkgd",
        weights.astype(jnp.bfloat16),
        block_values,
        preferred_element_type=jnp.float32,
    )
    return (
        numerator.reshape(row_count, kv_count * query_group_width, head_size),
        heads_last(maxima),
        heads_last(denominator),
    )


def join_parts(first, second):
    maxima = jnp.maximum(first[1], second[1])
    left_scale = jnp.exp(first[1] - maxima)
    right_scale = jnp.exp(second[1] - maxima)
    numerator = first[0] * left_scale[..., None] + second[0] * right_scale[..., None]
    return (numerator, maxima, first[2] * left_scale + second[2] * right_scale)


def sources_merge(parts):
    numerator, maxima, denominator = parts
    highest = jnp.max(maxima, axis=2)
    rescale = jnp.exp(maxima - highest[:, :, None])
    return (
        jnp.sum(numerator * rescale[..., None], axis=2),
        highest,
        jnp.sum(denominator * rescale, axis=2),
    )


def on_device(
    queries,
    cand_keys,
    candidate_values,
    cached_prompt_keys,
    cached_prompt_values,
    block_lists,
    out_weight,
):
    cand_count, tok_rows, head_local, head_size = queries.shape
    kv_local = cand_keys.shape[2]
    query_group_width = head_local // kv_local
    blocks_here, block_tokens = (cached_prompt_keys.shape[0], cached_prompt_keys.shape[1])
    selected = block_lists.shape[1]
    ranges = lax.axis_size("ctx")
    device = lax.axis_index("ctx")
    cand_length = tok_rows * ranges
    factor = head_size ** (-0.5)
    capacity = min(blocks_here, 4 * selected // ranges)
    lowest = device * blocks_here
    below = jnp.sum((block_lists < lowest).astype(jnp.int32), axis=1)
    inside = jnp.sum((block_lists < lowest + blocks_here).astype(jnp.int32), axis=1) - below
    slot_ids = jnp.arange(capacity)
    where_listed = jnp.clip(below[:, None] + slot_ids[None, :], 0, selected - 1)
    slot_live = slot_ids[None, :] < inside[:, None]
    local_index = jnp.where(
        slot_live, jnp.take_along_axis(block_lists, where_listed, axis=1) - lowest, 0
    )
    gathered_keys = jnp.take(cached_prompt_keys, local_index, axis=0).reshape(
        cand_count, capacity * block_tokens, kv_local, head_size
    )
    gathered_values = jnp.take(cached_prompt_values, local_index, axis=0).reshape(
        cand_count, capacity * block_tokens, kv_local, head_size
    )
    key_live = jnp.repeat(slot_live, block_tokens, axis=1)
    shard_rows = lax.all_gather(queries, "ctx", axis=1, tiled=True)
    row_count = shard_rows.shape[1]
    grouped_queries = shard_rows.reshape(
        cand_count, row_count, kv_local, query_group_width, head_size
    )
    terms = lax.map(
        lambda parts: block_terms(parts[0], parts[1], parts[2], parts[3], factor),
        (grouped_queries, gathered_keys, gathered_values, key_live),
    )
    prompt_parts = tuple((fresh for fresh in terms))
    candidate_own_keys, own_values = (
        lax.all_gather(cand_keys, "ctx", axis=1, tiled=True),
        lax.all_gather(candidate_values, "ctx", axis=1, tiled=True),
    )
    query_pos = device * tok_rows + jnp.arange(tok_rows)
    causal = jnp.arange(cand_length)[None, :] <= query_pos[:, None]
    grouped_local = queries.reshape(cand_count, tok_rows, kv_local, query_group_width, head_size)
    own_scores = (
        jnp.einsum(
            "jnkgd,jmkd->jkgnm",
            grouped_local,
            candidate_own_keys,
            preferred_element_type=jnp.float32,
        )
        * factor
    )
    own_weights, own_max, own_sum = masked_softmax(own_scores, causal)
    own_numer = jnp.einsum(
        "jkgnm,jmkd->jnkgd",
        own_weights.astype(jnp.bfloat16),
        own_values,
        preferred_element_type=jnp.float32,
    )
    own_part = (
        own_numer.reshape(cand_count, tok_rows, head_local, head_size),
        jnp.transpose(own_max, (0, 3, 1, 2)).reshape(cand_count, tok_rows, head_local),
        jnp.transpose(own_sum, (0, 3, 1, 2)).reshape(cand_count, tok_rows, head_local),
    )
    merged = sources_merge(
        (
            lax.all_to_all(
                prompt_parts[0][:, :, None].astype(jnp.bfloat16),
                "ctx",
                split_axis=1,
                concat_axis=2,
                tiled=True,
            ).astype(jnp.float32),
            lax.all_to_all(
                prompt_parts[1][:, :, None].astype(jnp.bfloat16),
                "ctx",
                split_axis=1,
                concat_axis=2,
                tiled=True,
            ).astype(jnp.float32),
            lax.all_to_all(
                prompt_parts[2][:, :, None].astype(jnp.bfloat16),
                "ctx",
                split_axis=1,
                concat_axis=2,
                tiled=True,
            ).astype(jnp.float32),
        )
    )
    numerator, unused_max, denominator = join_parts(merged, own_part)
    attention = (
        (numerator / denominator[..., None])
        .reshape(cand_count, tok_rows, head_local * head_size)
        .astype(jnp.bfloat16)
    )
    partial_value = jnp.einsum(
        "jnf,fc->jnc",
        lax.all_gather(attention, "ctx", axis=1, tiled=True),
        out_weight,
        preferred_element_type=jnp.float32,
    )
    return lax.psum_scatter(
        partial_value.astype(jnp.bfloat16), "tp", scatter_dimension=1, tiled=True
    )


def solution(mesh):
    placed = (
        P("groups", "ctx", "tp", None),
        P("groups", "ctx", "tp", None),
        P("groups", "ctx", "tp", None),
        P(("groups", "ctx"), None, "tp", None),
        P(("groups", "ctx"), None, "tp", None),
        P("groups", None),
        P("tp", "ctx"),
    )
    return jax.shard_map(
        on_device, mesh=mesh, in_specs=placed, out_specs=P("groups", "tp", "ctx"), check_vma=False
    )
```

profile of v0, /device:TPU:0, one launch (start us, length us, event | category | flops | bytes accessed | tf_op | source)
XLA Modules:
  0.0 322.9 jit_solution(12083824224312323788)
XLA Ops:
  6.5 0.7 all-gather.3.cloned.1.call-update
  7.3 0.8 convert_reduce_fusion.1
  8.3 1.6 gather_fusion
  9.9 0.1 reshape.205
  10.0 0.1 compare_and_fusion
  10.1 9.3 %gather_fusion.1 = bf16[64,128,4,128]{3,2,1,0:T(4,128)(2,1)} fusion(bf16[16,128,4,128]{3,2,1,0:T(4,128)(2,1)S(1)} %copy-done, s32[1024]{0:T(1024)S(1)} %pad_clamp_fusion), kind=kCustom, calls=%fused_computation.clone | custom fusion | bytes 16777472 | tf_op jit(solution)/shard_map/jit(_take)/gather | solution.py:91
  19.4 10.9 %gather_fusion.2 = bf16[64,128,4,128]{3,2,1,0:T(4,128)(2,1)} fusion(bf16[16,128,4,128]{3,2,1,0:T(4,128)(2,1)} %param.14, s32[1024]{0:T(1024)S(1)} %pad_clamp_fusion), kind=kCustom, calls=%fused_computation.1.clone | custom fusion | bytes 16777472 | tf_op jit(solution)/shard_map/jit(_take)/gather | solution.py:88
  30.4 14.7 %copy_select_fusion = (bf16[4,16,128,4,128]{4,2,1,3,0:T(8,128)(2,1)}, bf16[4,16,128,4,128]{4,2,1,3,0:T(8,128)(2,1)}) fusion(bf16[4,16,128,4,128]{4,3,2,1,0:T(4,128)(2,1)} %bitcast.150, pred[4,16]{1,0:T(4,128)(4,1)S(1)} %get-tuple-element.82, bf16[4,16,128,4,128]{4,3,2,1,0:T(4,128)(2,1)} %bitcast.149), kind=kLoop, calls=%fused_computation.27 | loop fusion | flops 8388608 | bytes 33554496 | tf_op jit(solution)/shard_map/jit(_take)/select_n | solution.py:88
  45.1 22.7 %all-gather.3.cloned.1.call-done = bf16[4,32,32,128]{3,2,1,0:T(8,128)(2,1)} async-done(((bf16[4,2,32,128]{3,2,1,0:T(8,128)(2,1)}), bf16[4,32,32,128]{3,2,1,0:T(8,128)(2,1)}) %all-gather.3.cloned.1.call-update) | async-done | bytes 1048592 | tf_op jit(solution)/shard_map/all_gather | solution.py:95
  67.8 1.6 copy.71
  69.5 61.6 %while.14 = (s32[]{:T(128)}, bf16[4,32,32,128]{3,2,0,1:T(8,128)(2,1)}, bf16[4,32,32]{2,0,1:T(4,128)(2,1)S(1)}, bf16[4,32,32]{2,0,1:T(4,128)(2,1)S(1)}, bf16[4,20...) while((s32[]{:T(128)}, ...), condition=%wide.region_5.7_spmd, body=%wide.region_2.6_spmd.sunk | while | flops 1101002752 | bytes 64022668 | solution.py:100
  69.5 3.0 bitcast_reduce_fusion.2
  72.5 3.2 copy-done.1
  75.7 2.2 fusion.59
  77.9 0.1 copy.132
  78.0 0.1 dynamic_update_slice.17
  78.1 5.7 %fusion.58 = bf16[4,128,8,32]{1,3,2,0:T(8,128)(2,1)S(1)} fusion(f32[4,2048,32,8]{1,2,3,0:T(8,128)} %copy-done.1, f32[4,8,32]{2,1,0:T(8,128)S(1)} %get-tuple-element.148, pred[2048]{0:T(1024)(128)(4,1)S(1)} %dynamic-slice_reduce_fusion.2, bf16[4,2048,4,128]{3,1,2,0:T(8,128)(2,1)} %get-tuple-element.173, s32[]{:T(128)} %get-tuple-element.159), kind=kOutput, calls=%fused_computation.10.clone.1 | convolution fusion | flops 547356672 | bytes 10768896 | tf_op jit(solution)/shard_map/while/body/eval_jaxpr/kgnm,mkd->nkgd/dot_general | solution.py:28
  83.8 0.9 copy_dynamic-update-slice_fusion.2
  84.9 3.0 bitcast_reduce_fusion.2
  87.9 3.2 copy-done.1
  91.1 2.2 fusion.59
  93.3 0.1 copy.132
  93.4 0.1 dynamic_update_slice.17
  93.5 5.7 %fusion.58 = bf16[4,128,8,32]{1,3,2,0:T(8,128)(2,1)S(1)} fusion(f32[4,2048,32,8]{1,2,3,0:T(8,128)} %copy-done.1, f32[4,8,32]{2,1,0:T(8,128)S(1)} %get-tuple-element.148, pred[2048]{0:T(1024)(128)(4,1)S(1)} %dynamic-slice_reduce_fusion.2, bf16[4,2048,4,128]{3,1,2,0:T(8,128)(2,1)} %get-tuple-element.173, s32[]{:T(128)} %get-tuple-element.159), kind=kOutput, calls=%fused_computation.10.clone.1 | convolution fusion | flops 547356672 | bytes 10768896 | tf_op jit(solution)/shard_map/while/body/eval_jaxpr/kgnm,mkd->nkgd/dot_general | solution.py:28
  99.3 0.9 copy_dynamic-update-slice_fusion.2
  100.3 3.0 bitcast_reduce_fusion.2
  103.3 3.2 copy-done.1
  106.6 2.2 fusion.59
  108.8 0.1 copy.132
  108.8 0.1 dynamic_update_slice.17
  108.9 5.7 %fusion.58 = bf16[4,128,8,32]{1,3,2,0:T(8,128)(2,1)S(1)} fusion(f32[4,2048,32,8]{1,2,3,0:T(8,128)} %copy-done.1, f32[4,8,32]{2,1,0:T(8,128)S(1)} %get-tuple-element.148, pred[2048]{0:T(1024)(128)(4,1)S(1)} %dynamic-slice_reduce_fusion.2, bf16[4,2048,4,128]{3,1,2,0:T(8,128)(2,1)} %get-tuple-element.173, s32[]{:T(128)} %get-tuple-element.159), kind=kOutput, calls=%fused_computation.10.clone.1 | convolution fusion | flops 547356672 | bytes 10768896 | tf_op jit(solution)/shard_map/while/body/eval_jaxpr/kgnm,mkd->nkgd/dot_general | solution.py:28
  114.7 0.9 copy_dynamic-update-slice_fusion.2
  115.7 3.0 bitcast_reduce_fusion.2
  118.7 3.2 copy-done.1
  122.0 2.2 fusion.59
  124.2 0.1 copy.132
  124.3 0.1 dynamic_update_slice.17
  124.3 5.7 %fusion.58 = bf16[4,128,8,32]{1,3,2,0:T(8,128)(2,1)S(1)} fusion(f32[4,2048,32,8]{1,2,3,0:T(8,128)} %copy-done.1, f32[4,8,32]{2,1,0:T(8,128)S(1)} %get-tuple-element.148, pred[2048]{0:T(1024)(128)(4,1)S(1)} %dynamic-slice_reduce_fusion.2, bf16[4,2048,4,128]{3,1,2,0:T(8,128)(2,1)} %get-tuple-element.173, s32[]{:T(128)} %get-tuple-element.159), kind=kOutput, calls=%fused_computation.10.clone.1 | convolution fusion | flops 547356672 | bytes 10768896 | tf_op jit(solution)/shard_map/while/body/eval_jaxpr/kgnm,mkd->nkgd/dot_general | solution.py:28
  130.1 0.8 copy_dynamic-update-slice_fusion.2
  131.1 0.7 reshape.228
  131.8 4.7 %all-to-all-start.2 = ((bf16[16,2,128]{2,1,0:T(2,128)(2,1)}), bf16[16,2,128]{2,1,0:T(2,128)(2,1)S(1)}, u32[]{:S(2)}, u32[]{:S(2)}) async-start(bf16[16,2,128]{2,1,0:T(2,128)(2,1)} %reshape.228), calls=%async_computation.2 | async-start | bytes 16384 | tf_op jit(solution)/shard_map/all_to_all | solution.py:149
  136.5 0.1 reshape.226
  136.6 7.1 %all-to-all-done.2 = bf16[16,2,128]{2,1,0:T(2,128)(2,1)S(1)} async-done(((bf16[16,2,128]{2,1,0:T(2,128)(2,1)}), bf16[16,2,128]{2,1,0:T(2,128)(2,1)S(1)}, u32[]{:S(2)}, u32[]{:S(2)}) %all-to-all-start.2) | async-done | bytes 8224 | tf_op jit(solution)/shard_map/all_to_all | solution.py:149
  143.7 9.8 %all_to_all.33 = bf16[16,2,128]{2,1,0:T(2,128)(2,1)S(1)} all-to-all(bf16[16,2,128]{2,1,0:T(2,128)(2,1)S(1)} %reshape.226), channel_id=1, replica_groups=mesh['groups'=1,'ctx'=16,'tp'=2] {'ctx'}, dimensions={0} | all-to-all | bytes 16384 | tf_op jit(solution)/shard_map/all_to_all | solution.py:142
  153.5 3.7 %all-to-all-start = ((bf16[4,32,1,32,128]{4,3,0,2,1:T(8,128)(2,1)}), bf16[4,32,1,32,128]{4,3,0,2,1:T(8,128)(2,1)S(1)}, u32[]{:S(2)}, u32[]{:S(2)}) async-start(bf16[4,32,1,32,128]{4,3,0,2,1:T(8,128)(2,1)} %bitcast.156), calls=%async_computation | async-start | bytes 2097152 | tf_op jit(solution)/shard_map/all_to_all | solution.py:135
  157.2 47.3 %all_gather.13 = bf16[4,32,4,128]{3,2,0,1:T(4,128)(2,1)S(1)} all-gather(bf16[4,2,4,128]{3,2,0,1:T(4,128)(2,1)S(1)} %copy.77), channel_id=1, replica_groups=mesh['groups'=1,'ctx'=16,'tp'=2] {'ctx'}, dimensions={1}, use_global_device_ids=true | all-gather | bytes 139264 | tf_op jit(solution)/shard_map/all_gather | solution.py:106
  204.6 0.3 fusion.50
  204.9 0.2 fusion.33
  205.1 0.1 reshape.180
  205.2 0.1 reshape.178
  205.3 38.1 %all_gather.14 = bf16[4,32,4,128]{3,2,0,1:T(4,128)(2,1)S(1)} all-gather(bf16[4,2,4,128]{3,2,0,1:T(4,128)(2,1)S(1)} %copy.82), channel_id=1, replica_groups=mesh['groups'=1,'ctx'=16,'tp'=2] {'ctx'}, dimensions={1}, use_global_device_ids=true | all-gather | bytes 139264 | tf_op jit(solution)/shard_map/all_gather | solution.py:107
  243.5 0.2 convolution_bitcast_fusion
  244.1 1.5 copy.76
  245.6 0.1 div.11
  245.8 0.7 mul.77
  246.5 1.0 mul.78
  247.5 0.7 copy.81
  248.2 0.3 convert.23
  248.5 3.9 %fusion.22 = f32[4,2,32,128]{3,1,2,0:T(2,128)S(1)} fusion(f32[4,16,2,1,32,128]{5,4,0,2,1,3:T(8,128)S(1)} %convert.23, f32[4,2,16,32]{1,2,3,0:T(8,128)} %copy.76), kind=kLoop, calls=%fused_computation.32 | loop fusion | flops 1015808 | bytes 2244608 | tf_op jit(solution)/shard_map/reduce_sum | solution.py:54
  252.4 1.1 fusion.32
  253.5 0.7 copy.88
  254.2 51.3 %all-gather.5.cloned.1.call-done = bf16[4,32,4096]{2,0,1:T(4,128)(2,1)} async-done(((bf16[4,2,4096]{2,0,1:T(4,128)(2,1)}), bf16[4,32,4096]{2,0,1:T(4,128)(2,1)}) %all-gather.5.cloned.1.call-update) | async-done | bytes 1048592 | tf_op jit(solution)/shard_map/all_gather | solution.py:166
  305.5 4.4 %fusion.23 = bf16[4,32,512]{2,1,0:T(8,128)(2,1)} fusion(bf16[4096,512]{1,0:T(8,128)(2,1)} %param.17, bf16[4,32,4096]{2,0,1:T(4,128)(2,1)} %all-gather.5.cloned.1.call-done), kind=kOutput, calls=%fused_computation.33 | convolution fusion | flops 536936448 | bytes 5373952 | tf_op jit(solution)/shard_map/jnf,fc->jnc/dot_general | solution.py:164
  309.9 6.5 %reduce-scatter.2.cloned.1.call-done = bf16[4,16,512]{2,1,0:T(8,128)(2,1)} async-done(((bf16[4,32,512]{2,1,0:T(8,128)(2,1)}), bf16[4,16,512]{2,1,0:T(8,128)(2,1)}) %reduce-scatter.2.cloned.1.call-update) | async-done | bytes 65552 | tf_op jit(solution)/shard_map/reduce_scatter | solution.py:170
  (59 shorter events, 1.9 us)
Async XLA Ops:
  6.5 3.6 %copy-start = (bf16[16,128,4,128]{3,2,1,0:T(4,128)(2,1)S(1)}, bf16[16,128,4,128]{3,2,1,0:T(4,128)(2,1)}, u32[]{:S(2)}) copy-start(bf16[16,128,4,128]{3,2,1,0:T(4,128)(2,1)} %param.15) | copy-start | bytes 6291460
  6.5 61.3 %all-gather.3.cloned.1.call-start = ((), (), s32[]{:S(2)}) async-start(), calls=%async_computation.4 | async-start | bytes 1114112 | tf_op jit(solution)/shard_map/all_gather | solution.py:95
  69.4 87.8 %copy-start.3 = (bf16[4,2,4,128]{3,2,1,0:T(4,128)(2,1)S(1)}, bf16[4,2,4,128]{3,2,1,0:T(4,128)(2,1)}, u32[]{:S(2)}) copy-start(bf16[4,2,4,128]{3,2,1,0:T(4,128)(2,1)} %param.12) | copy-start | bytes 24580
  69.4 135.1 %copy-start.2 = (bf16[4,2,32,128]{3,2,1,0:T(8,128)(2,1)S(1)}, bf16[4,2,32,128]{3,2,1,0:T(8,128)(2,1)}, u32[]{:S(2)}) copy-start(bf16[4,2,32,128]{3,2,1,0:T(8,128)(2,1)} %param.11) | copy-start | bytes 196612
  69.5 135.8 %copy-start.4 = (bf16[4,2,4,128]{3,2,1,0:T(4,128)(2,1)S(1)}, bf16[4,2,4,128]{3,2,1,0:T(4,128)(2,1)}, u32[]{:S(2)}) copy-start(bf16[4,2,4,128]{3,2,1,0:T(4,128)(2,1)} %param.13) | copy-start | bytes 24580
  72.5 3.2 copy-start.1
  87.9 3.2 copy-start.1
  103.3 3.2 copy-start.1
  118.7 3.2 copy-start.1
  131.8 11.9 %all-to-all-start.2 = ((bf16[16,2,128]{2,1,0:T(2,128)(2,1)}), bf16[16,2,128]{2,1,0:T(2,128)(2,1)S(1)}, u32[]{:S(2)}, u32[]{:S(2)}) async-start(bf16[16,2,128]{2,1,0:T(2,128)(2,1)} %reshape.228), calls=%async_computation.2 | async-start | bytes 16384 | tf_op jit(solution)/shard_map/all_to_all | solution.py:149
  153.5 94.7 %all-to-all-start = ((bf16[4,32,1,32,128]{4,3,0,2,1:T(8,128)(2,1)}), bf16[4,32,1,32,128]{4,3,0,2,1:T(8,128)(2,1)S(1)}, u32[]{:S(2)}, u32[]{:S(2)}) async-start(bf16[4,32,1,32,128]{4,3,0,2,1:T(8,128)(2,1)} %bitcast.156), calls=%async_computation | async-start | bytes 2097152 | tf_op jit(solution)/shard_map/all_to_all | solution.py:135
  157.2 148.3 %all-gather.5.cloned.1.call-start = ((), (), s32[]{:S(2)}) async-start(), calls=%async_computation.5 | async-start | bytes 1114112 | tf_op jit(solution)/shard_map/all_gather | solution.py:166
  254.2 62.1 %reduce-scatter.2.cloned.1.call-start = ((), (), s32[]{:S(2)}) async-start(), calls=%async_computation.6 | async-start | bytes 196608 | tf_op jit(solution)/shard_map/reduce_scatter | solution.py:170
Sparse Core Ops, SparseCore 0:
  10.1 57.6 all-gather.2
  254.3 51.1 all-gather.4
  310.0 6.2 reduce-scatter.1
where the time goes:
time: 324 us; the launch traced here: 323 us
  blocking collectives  95.3 us (29%)
  waiting for transfers between devices  88.2 us (27%)
  local copies, waits for them, and re-layouts  47.6 us (15%)
  matrix products  39.7 us (12%)
  other arithmetic  30.1 us (9%)
  between operations  13.4 us (4%)
  starting transfers between devices  8.39 us (3%)
    all_gather x1, waiting for transfers between devices, on_device(): lax.all_gather(attention, 'ctx', axis=1, tiled=True)  51.3 us
    all_gather x1, blocking collectives, on_device(): lax.all_gather(cand_keys, 'ctx', axis=1, tiled=True)  47.3 us
    all_gather x1, blocking collectives, on_device(): lax.all_gather(candidate_values, 'ctx', axis=1, tiled=True)  38.1 us
    dot_general x4, matrix products, block_terms(): jnp.einsum('kgnm,mkd->nkgd', weights.astype(jnp.bfloat16), block_values,...  22.9 us
    all_gather x1, waiting for transfers between devices, on_device(): shard_rows = lax.all_gather(queries, 'ctx', axis=1, tiled=True)  22.7 us
    select_n x1, other arithmetic, on_device(): jnp.take(cached_prompt_keys, local_index, axis=0)  14.7 us
    while x8, local copies, waits for them, and re-layouts  12.9 us
    dot_general x4, matrix products, block_terms(): jnp.einsum('nkgd,mkd->kgnm', query_matrix, block_keys, preferred_element_...  12 us
  transfers between devices with their start and end apart: 5, of which 4 were waited for; matrix products, arithmetic and copies ran while one was open for 13% of the time, Pallas kernels for 0%

commit v1 on v0

v1 whole, which is shorter than its diff:
```python
import functools
import math

import jax
import jax.numpy as jnp
from jax import lax
from jax.experimental import pallas as pl
from jax.experimental.pallas import tpu as pltpu
from jax.sharding import PartitionSpec as P

NEGATIVE = -1e30
POSITIVE = 1e30
STATS = 3
OWN_ROWS = 16
GROUP = 4
LIMIT = 48 * 1024 * 1024

NT = (((1,), (1,)), ((), ()))
TN = (((0,), (0,)), ((), ()))


def whole(space=pltpu.VMEM):
    return pl.BlockSpec(memory_space=space)


def in_bf16(value):
    return value.astype(jnp.bfloat16).astype(jnp.float32)


def stat_rows(units):
    return -(-units * STATS // 16) * 16


class Sizes:
    def __init__(self, ranges, queries, cached, kv):
        self.n = ranges
        self.cand, self.toks, self.heads, self.width = queries
        self.kv = kv
        self.group = self.heads // kv
        self.blocks, self.block_tokens = cached[0], cached[1]
        self.lines = ranges // kv
        self.row_groups = self.lines // self.cand
        self.tokens = self.toks * ranges
        self.group_tokens = self.tokens // self.row_groups
        self.rows = self.group_tokens * self.group
        if kv != 4 or self.row_groups * self.cand * kv != ranges:
            raise ValueError("shape")


def place(size, line, first, second):
    me, core = lax.axis_index("ctx"), lax.axis_index("tp")
    other = (me // size.kv) ^ line
    return other * size.kv + ((me % size.kv) ^ (first * (1 + core)) ^ (second * (2 - core)))


def hop(size, value, stage):
    pairs = []
    cores = lax.axis_size("tp")
    for c in range(size.n):
        for core in range(cores):
            if stage == "first":
                other = c ^ (1 + core)
            elif stage == "second":
                other = c ^ (2 - core)
            else:
                other = c ^ (stage * size.kv)
            pairs.append((c * cores + core, other * cores + core))
    return lax.ppermute(value, ("ctx", "tp"), pairs)


def gather_lines(size, value):
    return jnp.stack([value] + [hop(size, value, k) for k in range(1, size.lines)])


def attention_kernel(
    size, first, lists, counts, q0, q1, q2, q3, keys, values, own_keys, own_values, out, rows, acc, stats
):
    units = 2 * size.lines
    scale = size.width ** (-0.5) * math.log2(math.e)
    me = lax.axis_index("ctx")
    for index, ref in enumerate((q0, q1, q2, q3)):
        for line in range(size.lines):
            chip = place(size, line, index % 2, index // 2)
            for j in range(size.cand):
                parts = [ref[line, j, t].astype(jnp.float32) for t in range(size.toks)]
                for kv in range(size.kv):
                    cut = [p[kv * size.group : (kv + 1) * size.group] for p in parts]
                    rows[j, kv, chip] = jnp.concatenate(cut).astype(jnp.bfloat16)
    chip_rows = size.toks * size.group
    chips = size.rows // chip_rows

    def one(step, carry):
        line = step
        j, part = line % size.cand, line // size.cand
        count = counts[j]
        matrices, held = [], []
        token = lax.broadcasted_iota(jnp.int32, (OWN_ROWS, size.rows), 1) // size.group
        token = token + part * size.group_tokens
        own = lax.broadcasted_iota(jnp.int32, (OWN_ROWS, size.rows), 0)
        seen = (own < size.toks) & (own + me * size.toks <= token)
        heads = [place(size, 0, first, second) % size.kv for second in range(2)]
        for second in range(2):
            q = rows[j, heads[second], pl.ds(part * chips, chips)].reshape(size.rows, size.width)
            matrices.append(q)
            s = lax.dot_general(
                own_keys[j, heads[second]], q, NT, preferred_element_type=jnp.float32
            )
            s = jnp.where(seen, s * scale, NEGATIVE)
            m = in_bf16(jnp.max(s, axis=0, keepdims=True))
            p = jnp.where(seen, jnp.exp2(s - m), 0.0)
            acc[second] = lax.dot_general(
                own_values[j, heads[second]],
                p.astype(jnp.bfloat16),
                TN,
                preferred_element_type=jnp.float32,
            )
            held += [m, jnp.sum(p, axis=0, keepdims=True)]

        def over(g, held):
            held = list(held)
            for second in range(2):
                m, l = held[2 * second], held[2 * second + 1]
                head, q = heads[second], matrices[second]
                scores, tops, live, cut = [], [], [], []
                for b in range(GROUP):
                    slot = g * GROUP + b
                    block = lists[j, slot]
                    alive = slot < count
                    s = lax.dot_general(
                        keys[head, block], q, NT, preferred_element_type=jnp.float32
                    )
                    top = jnp.max(s, axis=0, keepdims=True) * scale
                    scores.append(s)
                    live.append(alive)
                    tops.append(jnp.where(alive, top, NEGATIVE))
                    cut.append(values[head, block])
                top = functools.reduce(jnp.maximum, tops)
                high = jnp.maximum(m, in_bf16(top))
                fade = jnp.exp2(m - high)
                weights = []
                total = l * fade
                for b in range(GROUP):
                    shift = jnp.where(live[b], high, POSITIVE)
                    p = jnp.exp2(scores[b] * scale - shift)
                    total = total + jnp.sum(p, axis=0, keepdims=True)
                    weights.append(p.astype(jnp.bfloat16))
                acc[second] = acc[second] * fade + jnp.dot(
                    jnp.concatenate(cut, axis=1),
                    jnp.concatenate(weights, axis=0),
                    preferred_element_type=jnp.float32,
                )
                held[2 * second], held[2 * second + 1] = high, total
            return tuple(held)

        held = lax.fori_loop(0, (count + GROUP - 1) // GROUP, over, tuple(held))
        for second in range(2):
            unit = second * size.lines + line
            at = pl.multiple_of(unit * size.width, size.width)
            out[pl.ds(at, size.width), :] = acc[second].astype(jnp.bfloat16)
            m, l = held[2 * second], held[2 * second + 1]
            whole_l = in_bf16(l)
            stats[pl.ds(unit, 1), :] = m
            stats[pl.ds(units + unit, 1), :] = whole_l
            stats[pl.ds(2 * units + unit, 1), :] = l - whole_l
        return carry

    stats[...] = jnp.zeros_like(stats)
    lax.fori_loop(0, size.lines, one, 0)
    out[pl.ds(units * size.width, stat_rows(units)), :] = stats[...].astype(jnp.bfloat16)


def attention_part(size, first, lists, counts, gathered, keys, values, own_keys, own_values):
    units = 2 * size.lines
    length = units * size.width + stat_rows(units)
    return pl.pallas_call(
        functools.partial(attention_kernel, size, first),
        out_shape=jax.ShapeDtypeStruct((length, size.rows), jnp.bfloat16),
        in_specs=[whole(pltpu.SMEM)] * 2 + [whole()] * 8,
        out_specs=whole(),
        scratch_shapes=[
            pltpu.VMEM(
                (size.cand, size.kv, size.n, size.toks * size.group, size.width), jnp.bfloat16
            ),
            pltpu.VMEM((2, size.width, size.rows), jnp.float32),
            pltpu.VMEM((stat_rows(units), size.rows), jnp.float32),
        ],
        compiler_params=pltpu.CompilerParams(vmem_limit_bytes=LIMIT),
        name="attention",
    )(lists, counts, *gathered, keys, values, own_keys, own_values)


def merge_units(size, parts, unit_lists, units_of):
    stats = []
    for ref, units, unit in zip(parts, units_of, unit_lists):
        at = units * size.width
        block = ref[pl.ds(at, stat_rows(units)), :].astype(jnp.float32)
        m = block[unit : unit + 1]
        l = block[units + unit : units + unit + 1] + block[2 * units + unit : 2 * units + unit + 1]
        stats.append((m, l))
    high = functools.reduce(jnp.maximum, [m for m, _ in stats])
    fades = [jnp.exp2(m - high) for m, _ in stats]
    total = functools.reduce(jnp.add, [l * f for (_, l), f in zip(stats, fades)])
    sums = None
    for ref, unit, fade in zip(parts, unit_lists, fades):
        value = ref[pl.ds(unit * size.width, size.width), :].astype(jnp.float32) * fade
        sums = value if sums is None else sums + value
    return sums, high, total


def merge_kernel(size, start, units, units_in, mine, theirs, out):
    highs, totals = [], []
    for unit in range(units):
        sums, high, total = merge_units(size, (mine, theirs), (start + unit,) * 2, (units_in,) * 2)
        out[pl.ds(unit * size.width, size.width), :] = sums.astype(jnp.bfloat16)
        highs.append(high)
        totals.append(total)
    lengths = [in_bf16(t) for t in totals]
    rows = highs + lengths + [t - l for t, l in zip(totals, lengths)]
    left = stat_rows(units) - len(rows)
    if left:
        rows.append(jnp.zeros((left, size.rows), jnp.float32))
    out[pl.ds(units * size.width, stat_rows(units)), :] = jnp.concatenate(rows).astype(jnp.bfloat16)


def merge(size, start, units, units_in, mine, theirs):
    length = units * size.width + stat_rows(units)
    return pl.pallas_call(
        functools.partial(merge_kernel, size, start, units, units_in),
        out_shape=jax.ShapeDtypeStruct((length, size.rows), jnp.bfloat16),
        in_specs=[whole()] * 2,
        out_specs=whole(),
        compiler_params=pltpu.CompilerParams(vmem_limit_bytes=LIMIT),
        name="merge",
    )(mine, theirs)


def split_kernel(size, mine, theirs, own, *outs):
    here = lax.axis_index("ctx") // size.kv
    lines = size.lines
    parts = []
    for unit in range(lines):
        sums, high, total = merge_units(size, (mine, theirs), (unit, unit), (lines, lines))
        length = in_bf16(total)
        tail = jnp.concatenate(
            [high, length, total - length, jnp.zeros((16 - STATS, size.rows), jnp.float32)]
        )
        parts.append((sums.astype(jnp.bfloat16), tail.astype(jnp.bfloat16)))
    for line, out in enumerate((own,) + outs):
        for unit in range(lines):

            @pl.when((here ^ line) == unit)
            def _():
                out[: size.width, :] = parts[unit][0]
                out[size.width :, :] = parts[unit][1]


def split_merge(size, mine, theirs):
    shape = jax.ShapeDtypeStruct((size.width + 16, size.rows), jnp.bfloat16)
    return pl.pallas_call(
        functools.partial(split_kernel, size),
        out_shape=[shape] * size.lines,
        in_specs=[whole()] * 2,
        out_specs=[whole()] * size.lines,
        compiler_params=pltpu.CompilerParams(vmem_limit_bytes=LIMIT),
        name="split",
    )(mine, theirs)


def finish_kernel(size, *refs):
    parts, out, turned = refs[:-2], refs[-2], refs[-1]
    count = len(parts)
    sums, _, total = merge_units(size, parts, (0,) * count, (1,) * count)
    turned[...] = (sums / total).T
    for g in range(size.group):
        piece = turned[pl.ds(g, size.group_tokens, stride=size.group), :]
        out[pl.ds(g * size.group_tokens, size.group_tokens), :] = piece.astype(jnp.bfloat16)


def finish(size, parts):
    return pl.pallas_call(
        functools.partial(finish_kernel, size),
        out_shape=jax.ShapeDtypeStruct((size.rows, size.width), jnp.bfloat16),
        in_specs=[whole()] * len(parts),
        out_specs=whole(),
        scratch_shapes=[pltpu.VMEM((size.rows, size.width), jnp.float32)],
        compiler_params=pltpu.CompilerParams(vmem_limit_bytes=LIMIT),
        name="finish",
    )(*parts)


def project_kernel(size, a0, a1, a2, a3, weight, kept, sent, whole_rows, product):
    core = lax.axis_index("tp")
    for index, ref in enumerate((a0, a1, a2, a3)):
        for line in range(size.lines):
            chip = place(size, line, index % 2, index // 2)
            kv, other = chip % size.kv, chip // size.kv
            j, part = other % size.cand, other // size.cand
            at = pl.multiple_of(j * size.tokens + part * size.group_tokens, size.group_tokens)
            for g in range(size.group):
                piece = ref[line, pl.ds(g * size.group_tokens, size.group_tokens), :]
                whole_rows[kv * size.group + g, pl.ds(at, size.group_tokens), :] = piece
    total = None
    for h in range(0, size.heads, 2):
        pair = jnp.concatenate([whole_rows[h], whole_rows[h + 1]], axis=1)
        term = jnp.dot(
            pair,
            weight[pl.ds(h * size.width, 2 * size.width), :],
            preferred_element_type=jnp.float32,
        )
        total = term if total is None else total + term
    product[...] = total
    half = size.tokens // 2
    for j in range(size.cand):
        near = pl.multiple_of(j * size.tokens + core * half, half)
        far = pl.multiple_of(j * size.tokens + (1 - core) * half, half)
        kept[j] = product[pl.ds(near, half), :]
        sent[j] = product[pl.ds(far, half), :].astype(jnp.bfloat16)


def project(size, gathered, weight):
    columns = weight.shape[1]
    shape = (size.cand, size.tokens // 2, columns)
    return pl.pallas_call(
        functools.partial(project_kernel, size),
        out_shape=[
            jax.ShapeDtypeStruct(shape, jnp.float32),
            jax.ShapeDtypeStruct(shape, jnp.bfloat16),
        ],
        in_specs=[whole()] * 5,
        out_specs=[whole()] * 2,
        scratch_shapes=[
            pltpu.VMEM((size.heads, size.cand * size.tokens, size.width), jnp.bfloat16),
            pltpu.VMEM((size.cand * size.tokens, columns), jnp.float32),
        ],
        compiler_params=pltpu.CompilerParams(vmem_limit_bytes=LIMIT),
        name="project",
    )(*gathered, weight)


def gather_all(size, value):
    a0 = gather_lines(size, value)
    a1 = hop(size, a0, "first")
    a2 = hop(size, a0, "second")
    a3 = hop(size, a1, "second")
    return a0, a1, a2, a3


def listed_here(size, block_lists):
    lowest = lax.axis_index("ctx") * size.blocks
    local = block_lists - lowest
    below = jnp.sum((local < 0).astype(jnp.int32), axis=1)
    inside = jnp.sum((local < size.blocks).astype(jnp.int32), axis=1) - below
    slots = jnp.arange(-(-size.blocks // GROUP) * GROUP)
    entry = jnp.arange(block_lists.shape[1])
    hit = entry[None, None, :] == (below[:, None] + slots[None, :])[:, :, None]
    hit = hit & (slots[None, :] < inside[:, None])[:, :, None]
    return jnp.sum(jnp.where(hit, local[:, None, :], 0), axis=2), inside


def on_device(
    queries,
    cand_keys,
    candidate_values,
    cached_prompt_keys,
    cached_prompt_values,
    block_lists,
    out_weight,
):
    size = Sizes(
        lax.axis_size("ctx"), queries.shape, cached_prompt_keys.shape, cand_keys.shape[2]
    )
    gathered = gather_all(size, queries)
    lists, counts = listed_here(size, block_lists)
    keys = jnp.transpose(cached_prompt_keys, (2, 0, 1, 3))
    values = jnp.transpose(cached_prompt_values, (2, 0, 3, 1))
    room = ((0, 0), (0, 0), (0, OWN_ROWS - size.toks), (0, 0))
    own_keys = jnp.pad(jnp.transpose(cand_keys, (0, 2, 1, 3)), room)
    own_values = jnp.pad(jnp.transpose(candidate_values, (0, 2, 1, 3)), room)
    shared = (lists, counts, gathered, keys, values, own_keys, own_values)
    away = attention_part(size, 1, *shared)
    away = hop(size, away, "first")
    mine = attention_part(size, 0, *shared)
    lines = size.lines
    leaves = merge(size, lines, lines, 2 * lines, mine, away)
    leaves = hop(size, leaves, "second")
    stays = merge(size, 0, lines, 2 * lines, mine, away)
    parts = split_merge(size, stays, leaves)
    parts = [parts[0]] + [hop(size, parts[k], k) for k in range(1, lines)]
    attention = finish(size, parts)
    kept, sent = project(size, gather_all(size, attention), out_weight)
    cores = lax.axis_size("tp")
    sent = lax.ppermute(sent, "tp", [(i, cores - 1 - i) for i in range(cores)])
    return (kept + sent.astype(jnp.float32)).astype(jnp.bfloat16)


def solution(mesh):
    placed = (
        P("groups", "ctx", "tp", None),
        P("groups", "ctx", "tp", None),
        P("groups", "ctx", "tp", None),
        P(("groups", "ctx"), None, "tp", None),
        P(("groups", "ctx"), None, "tp", None),
        P("groups", None),
        P("tp", "ctx"),
    )
    return jax.shard_map(
        on_device, mesh=mesh, in_specs=placed, out_specs=P("groups", "tp", "ctx"), check_vma=False
    )
```

time: 324 us -> 98 us (0.30)
  blocking collectives: 95.3 us -> 0 us
  waiting for transfers between devices: 88.2 us -> 41.7 us
  matrix products: 39.7 us -> 0 us
  local copies, waits for them, and re-layouts: 47.6 us -> 9.46 us
  other arithmetic: 30.1 us -> 2.74 us
  Pallas kernels: 0 us -> 24.2 us
  between operations: 13.4 us -> 0.14 us
  starting transfers between devices: 8.39 us -> 20 us
    all_gather x2 -> x0, blocking collectives: 85.4 us -> none  [the longest x1 47.3 us: on_device(): lax.all_gather(cand_keys, 'ctx', axis=1, tiled=True)]
    all_gather x2 -> x0, waiting for transfers between devices: 73.9 us -> none  [the longest x1 51.3 us: on_device(): lax.all_gather(attention, 'ctx', axis=1, tiled=True)]
    ppermute x0 -> x18, waiting for transfers between devices: none -> 41.7 us  [the longest x17 40.4 us: hop(): return lax.ppermute(value, ('ctx', 'tp'), pairs)]
    dot_general x11 -> x0, matrix products: 39.7 us -> none  [the longest x4 22.9 us: block_terms(): jnp.einsum('kgnm,mkd->nkgd', weights.astype(jnp.bfloat16), block_values,...]
    pallas_call x0 -> x7, Pallas kernels: none -> 24.2 us  [the longest x2 22.6 us: attention_part(): pl.pallas_call(functools.partial(attention_kernel, size, first), out_shap...]
    gather x5 -> x0, local copies, waits for them, and re-layouts: 21.9 us -> none  [the longest x1 10.9 us: on_device(): jnp.take(cached_prompt_keys, local_index, axis=0)]
    ppermute x0 -> x18, starting transfers between devices: none -> 20 us  [the longest x17 19.9 us: hop(): return lax.ppermute(value, ('ctx', 'tp'), pairs)]
    select_n x1 -> x0, other arithmetic: 14.7 us -> none  [on_device(): jnp.take(cached_prompt_keys, local_index, axis=0)]
  transfers between devices with their start and end apart: 5 -> 18, of which waited for: 4 -> 12; matrix products, arithmetic and copies ran while one was open for 13% -> 9% of each run, Pallas kernels for 0% -> 12%
where the time goes in v1:
time: 98 us; the launch traced here: 98.2 us
  waiting for transfers between devices  41.7 us (43%)
  Pallas kernels  24.2 us (25%)
  starting transfers between devices  20 us (20%)
  local copies, waits for them, and re-layouts  9.46 us (10%)
  other arithmetic  2.74 us (3%)
    ppermute x17, waiting for transfers between devices, hop(): return lax.ppermute(value, ('ctx', 'tp'), pairs)  40.4 us
    pallas_call x2, Pallas kernels, attention_part(): pl.pallas_call(functools.partial(attention_kernel, size, first), out_shap...  22.6 us
    ppermute x17, starting transfers between devices, hop(): return lax.ppermute(value, ('ctx', 'tp'), pairs)  19.9 us
    unnamed x8, local copies, waits for them, and re-layouts  9.44 us
  transfers between devices with their start and end apart: 18, of which 12 were waited for; matrix products, arithmetic and copies ran while one was open for 9% of the time, Pallas kernels for 12%

profile of v1, /device:TPU:0, one launch (start us, length us, event | category | flops | bytes accessed | tf_op | source)
XLA Modules:
  0.0 98.2 jit_solution(1744391116366698618)
XLA Ops:
  0.0 3.0 %collective-permute-start = (bf16[4,2,32,128]{3,2,1,0:T(8,128)(2,1)}, bf16[4,2,32,128]{3,2,1,0:T(8,128)(2,1)S(1)}, u32[]{:S(2)}, u32[]{:S(2)}) collective-permute-start(bf16[4,2,32,128]{3,2,1,0:T(8,128)(2,1)} %param.7), channel_id=1, source_target_pairs={{0,8},{1,9},{2,10},{3,11},{4,12},{5,13},{6,14},{7,15},{8,0},{9,1},... | collective-permute-start | bytes 196616 | tf_op jit(solution)/shard_map/ppermute | solution.py:68
  3.0 2.5 %collective-permute-start.2 = (bf16[4,2,32,128]{3,2,1,0:T(8,128)(2,1)}, bf16[4,2,32,128]{3,2,1,0:T(8,128)(2,1)S(1)}, u32[]{:S(2)}, u32[]{:S(2)}) collective-permute-start(bf16[4,2,32,128]{3,2,1,0:T(8,128)(2,1)} %param.7), channel_id=1, source_target_pairs={{0,24},{1,25},{2,26},{3,27},{4,28},{5,29},{6,30},{7,31},{8,16},{9,... | collective-permute-start | bytes 196616 | tf_op jit(solution)/shard_map/ppermute | solution.py:68
  5.5 0.1 collective-permute-start.1
  5.6 0.0 collective-permute-done
  5.6 4.5 %collective-permute-done.2 = bf16[4,2,32,128]{3,2,1,0:T(8,128)(2,1)S(1)} collective-permute-done((bf16[4,2,32,128]{3,2,1,0:T(8,128)(2,1)}, bf16[4,2,32,128]{3,2,1,0:T(8,128)(2,1)S(1)}, u32[]{:S(2)}, u32[]{:S(2)}) %collective-permute-start.2) | collective-permute-done | bytes 65568 | tf_op jit(solution)/shard_map/ppermute | solution.py:68
  10.1 2.1 %collective-permute-done.1 = bf16[4,2,32,128]{3,2,1,0:T(8,128)(2,1)S(1)} collective-permute-done((bf16[4,2,32,128]{3,2,1,0:T(8,128)(2,1)}, bf16[4,2,32,128]{3,2,1,0:T(8,128)(2,1)S(1)}, u32[]{:S(2)}, u32[]{:S(2)}) %collective-permute-start.1) | collective-permute-done | bytes 65568 | tf_op jit(solution)/shard_map/ppermute | solution.py:68
  12.2 0.9 pad_maximum_fusion.q0
  13.1 1.6 %collective-permute-start.3 = (bf16[4,4,2,32,128]{4,3,2,1,0:T(8,128)(2,1)S(1)}, bf16[4,4,2,32,128]{4,3,2,1,0:T(8,128)(2,1)S(1)}, u32[]{:S(2)}, u32[]{:S(2)}) collective-permute-start(bf16[4,4,2,32,128]{4,3,2,1,0:T(8,128)(2,1)S(1)} %pad_maximum_fusion.q0), channel_id=1, source_target_pairs={{0,2},{1,5},{2,0},{3,7},{4,6},{5,1},{6,4},{7,3},{8,10},{9,13},{10,... | collective-permute-start | bytes 786440 | tf_op jit(solution)/shard_map/ppermute | solution.py:68
  14.6 0.8 convert_reduce_fusion
  15.4 0.7 copy.21
  16.1 0.7 copy.20
  16.9 2.1 %copy.19 = bf16[16,128,4,128]{3,1,0,2:T(8,128)(2,1)S(1)} copy(bf16[16,128,4,128]{3,2,1,0:T(4,128)(2,1)} %param.10) | data formatting | bytes 4194304 | tf_op args[3]
  19.0 4.3 %copy.13 = bf16[16,128,4,128]{1,3,0,2:T(8,128)(2,1)} copy(bf16[16,128,4,128]{3,2,1,0:T(4,128)(2,1)} %param.11) | data formatting | bytes 4194304 | tf_op args[4]
  23.3 0.1 iota_add_fusion
  23.4 1.5 %collective-permute-start.4 = (bf16[4,4,2,32,128]{4,3,2,1,0:T(8,128)(2,1)S(1)}, bf16[4,4,2,32,128]{4,3,2,1,0:T(8,128)(2,1)S(1)}, u32[]{:S(2)}, u32[]{:S(2)}) collective-permute-start(bf16[4,4,2,32,128]{4,3,2,1,0:T(8,128)(2,1)S(1)} %pad_maximum_fusion.q0), channel_id=1, source_target_pairs={{0,4},{1,3},{2,6},{3,1},{4,0},{5,7},{6,2},{7,5},{8,12},{9,11},{10,... | collective-permute-start | bytes 786440 | tf_op jit(solution)/shard_map/ppermute | solution.py:68
  24.9 0.0 collective-permute-done.3.q1
  24.9 0.5 collective-permute-start.5
  25.4 0.1 iota_compare_fusion.1
  25.5 0.2 select_reduce_fusion.lists
  25.7 4.0 %collective-permute-done.4.q2 = bf16[4,4,2,32,128]{4,3,2,1,0:T(8,128)(2,1)S(1)} collective-permute-done((bf16[4,4,2,32,128]{4,3,2,1,0:T(8,128)(2,1)S(1)}, bf16[4,4,2,32,128]{4,3,2,1,0:T(8,128)(2,1)S(1)}, u32[]{:S(2)}, u32[]{:S(2)}) %collective-permute-start.4) | collective-permute-done | bytes 262176 | tf_op jit(solution)/shard_map/ppermute | solution.py:68
  29.8 2.8 %collective-permute-done.5.q3 = bf16[4,4,2,32,128]{4,3,2,1,0:T(8,128)(2,1)S(1)} collective-permute-done((bf16[4,4,2,32,128]{4,3,2,1,0:T(8,128)(2,1)S(1)}, bf16[4,4,2,32,128]{4,3,2,1,0:T(8,128)(2,1)S(1)}, u32[]{:S(2)}, u32[]{:S(2)}) %collective-permute-start.5) | collective-permute-done | bytes 262176 | tf_op jit(solution)/shard_map/ppermute | solution.py:68
  32.6 0.0 copy-start
  32.6 1.6 %copy-done = bf16[16,128,4,128]{1,3,0,2:T(8,128)(2,1)S(1)} copy-done((bf16[16,128,4,128]{1,3,0,2:T(8,128)(2,1)S(1)}, bf16[16,128,4,128]{1,3,0,2:T(8,128)(2,1)}, u32[]{:S(2)}) %copy-start) | copy-done | bytes 2097176
  34.2 11.3 %attention.3 = bf16[1056,256]{1,0:T(8,128)(2,1)S(1)} custom-call(s32[4,16]{1,0:T(4,128)S(1)} %select_reduce_fusion.lists, s32[4]{0:T(128)S(1)} %sub.11.counts, bf16[4,4,2,32,128]{4,3,2,1,0:T(8,128)(2,1)S(1)} %pad_maximum_fusion.q0, bf16[4,4,2,32,128]{4,3,2,1,0:T(8,128)(2,1)S(1)} %collective-permute-done.3.q1, ...), custom_call_target="tpu_custom_call" | custom-call | tf_op jit(solution)/shard_map/attention/pallas_call | solution.py:175
  45.5 0.1 collective-permute-start.6
  45.6 0.0 copy-start.1
  45.6 11.3 %attention.2.mine = bf16[1056,256]{1,0:T(8,128)(2,1)S(1)} custom-call(s32[4,16]{1,0:T(4,128)S(1)} %select_reduce_fusion.lists, s32[4]{0:T(128)S(1)} %sub.11.counts, bf16[4,4,2,32,128]{4,3,2,1,0:T(8,128)(2,1)S(1)} %pad_maximum_fusion.q0, bf16[4,4,2,32,128]{4,3,2,1,0:T(8,128)(2,1)S(1)} %collective-permute-done.3.q1, ...), custom_call_target="tpu_custom_call" | custom-call | tf_op jit(solution)/shard_map/attention/pallas_call | solution.py:175
  56.9 0.0 collective-permute-done.6.theirs
  56.9 0.1 merge.3
  57.1 0.1 collective-permute-start.7
  57.1 0.1 merge.2.mine
  57.3 6.3 %collective-permute-done.7.theirs = bf16[528,256]{1,0:T(8,128)(2,1)S(1)} collective-permute-done((bf16[528,256]{1,0:T(8,128)(2,1)S(1)}, bf16[528,256]{1,0:T(8,128)(2,1)S(1)}, u32[]{:S(2)}, u32[]{:S(2)}) %collective-permute-start.7) | collective-permute-done | bytes 270368 | tf_op jit(solution)/shard_map/ppermute | solution.py:68
  63.6 0.2 split.1
  63.8 0.1 collective-permute-start.8
  63.9 1.7 %collective-permute-start.9 = (bf16[144,256]{1,0:T(8,128)(2,1)S(1)}, bf16[144,256]{1,0:T(8,128)(2,1)S(1)}, u32[]{:S(2)}, u32[]{:S(2)}) collective-permute-start(bf16[144,256]{1,0:T(8,128)(2,1)S(1)} %get-tuple-element.13), channel_id=1, source_target_pairs={{0,16},{1,17},{2,18},{3,19},{4,20},{5,21},{6,22},{7,23},{8,24},{9,... | collective-permute-start | bytes 221192 | tf_op jit(solution)/shard_map/ppermute | solution.py:68
  65.6 2.6 %collective-permute-start.10 = (bf16[144,256]{1,0:T(8,128)(2,1)S(1)}, bf16[144,256]{1,0:T(8,128)(2,1)S(1)}, u32[]{:S(2)}, u32[]{:S(2)}) collective-permute-start(bf16[144,256]{1,0:T(8,128)(2,1)S(1)} %get-tuple-element.14), channel_id=1, source_target_pairs={{0,24},{1,25},{2,26},{3,27},{4,28},{5,29},{6,30},{7,31},{8,16},{9,... | collective-permute-start | bytes 221192 | tf_op jit(solution)/shard_map/ppermute | solution.py:68
  68.2 0.0 collective-permute-done.8.refs_1_
  68.3 1.5 %collective-permute-done.9.refs_2_ = bf16[144,256]{1,0:T(8,128)(2,1)S(1)} collective-permute-done((bf16[144,256]{1,0:T(8,128)(2,1)S(1)}, bf16[144,256]{1,0:T(8,128)(2,1)S(1)}, u32[]{:S(2)}, u32[]{:S(2)}) %collective-permute-start.9) | collective-permute-done | bytes 73760 | tf_op jit(solution)/shard_map/ppermute | solution.py:68
  69.8 2.0 %collective-permute-done.10.refs_3_ = bf16[144,256]{1,0:T(8,128)(2,1)S(1)} collective-permute-done((bf16[144,256]{1,0:T(8,128)(2,1)S(1)}, bf16[144,256]{1,0:T(8,128)(2,1)S(1)}, u32[]{:S(2)}, u32[]{:S(2)}) %collective-permute-start.10) | collective-permute-done | bytes 73760 | tf_op jit(solution)/shard_map/ppermute | solution.py:68
  71.8 0.2 finish.1
  72.0 2.7 %collective-permute-start.13 = (bf16[256,128]{1,0:T(8,128)(2,1)S(1)}, bf16[256,128]{1,0:T(8,128)(2,1)S(1)}, u32[]{:S(2)}, u32[]{:S(2)}) collective-permute-start(bf16[256,128]{1,0:T(8,128)(2,1)S(1)} %finish.1), channel_id=1, source_target_pairs={{0,24},{1,25},{2,26},{3,27},{4,28},{5,29},{6,30},{7,31},{8,16},{9,... | collective-permute-start | bytes 196616 | tf_op jit(solution)/shard_map/ppermute | solution.py:68
  74.7 0.3 collective-permute-start.12
  74.9 1.5 %collective-permute-start.11 = (bf16[256,128]{1,0:T(8,128)(2,1)S(1)}, bf16[256,128]{1,0:T(8,128)(2,1)S(1)}, u32[]{:S(2)}, u32[]{:S(2)}) collective-permute-start(bf16[256,128]{1,0:T(8,128)(2,1)S(1)} %finish.1), channel_id=1, source_target_pairs={{0,8},{1,9},{2,10},{3,11},{4,12},{5,13},{6,14},{7,15},{8,0},{9,1},... | collective-permute-start | bytes 196616 | tf_op jit(solution)/shard_map/ppermute | solution.py:68
  76.4 1.7 %collective-permute-done.13 = bf16[256,128]{1,0:T(8,128)(2,1)S(1)} collective-permute-done((bf16[256,128]{1,0:T(8,128)(2,1)S(1)}, bf16[256,128]{1,0:T(8,128)(2,1)S(1)}, u32[]{:S(2)}, u32[]{:S(2)}) %collective-permute-start.13) | collective-permute-done | bytes 65568 | tf_op jit(solution)/shard_map/ppermute | solution.py:68
  78.1 1.8 %collective-permute-done.12 = bf16[256,128]{1,0:T(8,128)(2,1)S(1)} collective-permute-done((bf16[256,128]{1,0:T(8,128)(2,1)S(1)}, bf16[256,128]{1,0:T(8,128)(2,1)S(1)}, u32[]{:S(2)}, u32[]{:S(2)}) %collective-permute-start.12) | collective-permute-done | bytes 65568 | tf_op jit(solution)/shard_map/ppermute | solution.py:68
  79.9 0.0 collective-permute-done.11
  79.9 1.4 %collective-permute-start.14 = (bf16[4,256,128]{2,1,0:T(8,128)(2,1)S(1)}, bf16[4,256,128]{2,1,0:T(8,128)(2,1)S(1)}, u32[]{:S(2)}, u32[]{:S(2)}) collective-permute-start(bf16[4,256,128]{2,1,0:T(8,128)(2,1)S(1)} %pad_maximum_fusion.1.a0), channel_id=1, source_target_pairs={{0,2},{1,5},{2,0},{3,7},{4,6},{5,1},{6,4},{7,3},{8,10},{9,13},{10,... | collective-permute-start | bytes 786440 | tf_op jit(solution)/shard_map/ppermute | solution.py:68
  81.3 0.1 collective-permute-start.15
  81.4 7.5 %collective-permute-done.14.a1 = bf16[4,256,128]{2,1,0:T(8,128)(2,1)S(1)} collective-permute-done((bf16[4,256,128]{2,1,0:T(8,128)(2,1)S(1)}, bf16[4,256,128]{2,1,0:T(8,128)(2,1)S(1)}, u32[]{:S(2)}, u32[]{:S(2)}) %collective-permute-start.14) | collective-permute-done | bytes 262176 | tf_op jit(solution)/shard_map/ppermute | solution.py:68
  88.9 0.2 collective-permute-start.16
  89.1 0.0 collective-permute-done.15.a2
  89.1 6.2 %collective-permute-done.16.a3 = bf16[4,256,128]{2,1,0:T(8,128)(2,1)S(1)} collective-permute-done((bf16[4,256,128]{2,1,0:T(8,128)(2,1)S(1)}, bf16[4,256,128]{2,1,0:T(8,128)(2,1)S(1)}, u32[]{:S(2)}, u32[]{:S(2)}) %collective-permute-start.16) | collective-permute-done | bytes 262176 | tf_op jit(solution)/shard_map/ppermute | solution.py:68
  95.3 0.0 copy-done.1
  95.3 0.9 project.1
  96.2 0.1 collective-permute-start.17
  96.3 1.2 %collective-permute-done.17 = bf16[4,16,512]{2,1,0:T(8,128)(2,1)S(1)} collective-permute-done((bf16[4,16,512]{2,1,0:T(8,128)(2,1)S(1)}, bf16[4,16,512]{2,1,0:T(8,128)(2,1)S(1)}, u32[]{:S(2)}, u32[]{:S(2)}) %collective-permute-start.17) | collective-permute-done | bytes 65568 | tf_op jit(solution)/shard_map/ppermute | solution.py:392
  97.5 0.6 add_convert_fusion
  (4 shorter events, 0.1 us)
Async XLA Ops:
  0.0 5.6 %collective-permute-start = (bf16[4,2,32,128]{3,2,1,0:T(8,128)(2,1)}, bf16[4,2,32,128]{3,2,1,0:T(8,128)(2,1)S(1)}, u32[]{:S(2)}, u32[]{:S(2)}) collective-permute-start(bf16[4,2,32,128]{3,2,1,0:T(8,128)(2,1)} %param.7), channel_id=1, source_target_pairs={{0,8},{1,9},{2,10},{3,11},{4,12},{5,13},{6,14},{7,15},{8,0},{9,1},... | collective-permute-start | bytes 196616 | tf_op jit(solution)/shard_map/ppermute | solution.py:68
  3.0 7.1 %collective-permute-start.2 = (bf16[4,2,32,128]{3,2,1,0:T(8,128)(2,1)}, bf16[4,2,32,128]{3,2,1,0:T(8,128)(2,1)S(1)}, u32[]{:S(2)}, u32[]{:S(2)}) collective-permute-start(bf16[4,2,32,128]{3,2,1,0:T(8,128)(2,1)} %param.7), channel_id=1, source_target_pairs={{0,24},{1,25},{2,26},{3,27},{4,28},{5,29},{6,30},{7,31},{8,16},{9,... | collective-permute-start | bytes 196616 | tf_op jit(solution)/shard_map/ppermute | solution.py:68
  5.5 6.7 %collective-permute-start.1 = (bf16[4,2,32,128]{3,2,1,0:T(8,128)(2,1)}, bf16[4,2,32,128]{3,2,1,0:T(8,128)(2,1)S(1)}, u32[]{:S(2)}, u32[]{:S(2)}) collective-permute-start(bf16[4,2,32,128]{3,2,1,0:T(8,128)(2,1)} %param.7), channel_id=1, source_target_pairs={{0,16},{1,17},{2,18},{3,19},{4,20},{5,21},{6,22},{7,23},{8,24},{9,... | collective-permute-start | bytes 196616 | tf_op jit(solution)/shard_map/ppermute | solution.py:68
  13.1 11.9 %collective-permute-start.3 = (bf16[4,4,2,32,128]{4,3,2,1,0:T(8,128)(2,1)S(1)}, bf16[4,4,2,32,128]{4,3,2,1,0:T(8,128)(2,1)S(1)}, u32[]{:S(2)}, u32[]{:S(2)}) collective-permute-start(bf16[4,4,2,32,128]{4,3,2,1,0:T(8,128)(2,1)S(1)} %pad_maximum_fusion.q0), channel_id=1, source_target_pairs={{0,2},{1,5},{2,0},{3,7},{4,6},{5,1},{6,4},{7,3},{8,10},{9,13},{10,... | collective-permute-start | bytes 786440 | tf_op jit(solution)/shard_map/ppermute | solution.py:68
  23.4 6.4 %collective-permute-start.4 = (bf16[4,4,2,32,128]{4,3,2,1,0:T(8,128)(2,1)S(1)}, bf16[4,4,2,32,128]{4,3,2,1,0:T(8,128)(2,1)S(1)}, u32[]{:S(2)}, u32[]{:S(2)}) collective-permute-start(bf16[4,4,2,32,128]{4,3,2,1,0:T(8,128)(2,1)S(1)} %pad_maximum_fusion.q0), channel_id=1, source_target_pairs={{0,4},{1,3},{2,6},{3,1},{4,0},{5,7},{6,2},{7,5},{8,12},{9,11},{10,... | collective-permute-start | bytes 786440 | tf_op jit(solution)/shard_map/ppermute | solution.py:68
  24.9 7.7 %collective-permute-start.5 = (bf16[4,4,2,32,128]{4,3,2,1,0:T(8,128)(2,1)S(1)}, bf16[4,4,2,32,128]{4,3,2,1,0:T(8,128)(2,1)S(1)}, u32[]{:S(2)}, u32[]{:S(2)}) collective-permute-start(bf16[4,4,2,32,128]{4,3,2,1,0:T(8,128)(2,1)S(1)} %collective-permute-done.3.q1), channel_id=1, source_target_pairs={{0,4},{1,3},{2,6},{3,1},{4,0},{5,7},{6,2},{7,5},{8,12},{9,11},{10,... | collective-permute-start | bytes 786440 | tf_op jit(solution)/shard_map/ppermute | solution.py:68
  32.6 1.6 %copy-start = (bf16[16,128,4,128]{1,3,0,2:T(8,128)(2,1)S(1)}, bf16[16,128,4,128]{1,3,0,2:T(8,128)(2,1)}, u32[]{:S(2)}) copy-start(bf16[16,128,4,128]{1,3,0,2:T(8,128)(2,1)} %copy.13) | copy-start | bytes 6291460
  45.5 11.4 %collective-permute-start.6 = (bf16[1056,256]{1,0:T(8,128)(2,1)S(1)}, bf16[1056,256]{1,0:T(8,128)(2,1)S(1)}, u32[]{:S(2)}, u32[]{:S(2)}) collective-permute-start(bf16[1056,256]{1,0:T(8,128)(2,1)S(1)} %attention.3), channel_id=1, source_target_pairs={{0,2},{1,5},{2,0},{3,7},{4,6},{5,1},{6,4},{7,3},{8,10},{9,13},{10,... | collective-permute-start | bytes 1622024 | tf_op jit(solution)/shard_map/ppermute | solution.py:68
  45.6 49.7 %copy-start.1 = (bf16[4096,512]{1,0:T(8,128)(2,1)S(1)}, bf16[4096,512]{1,0:T(8,128)(2,1)}, u32[]{:S(2)}) copy-start(bf16[4096,512]{1,0:T(8,128)(2,1)} %weight.1) | copy-start | bytes 12582916
  57.1 6.5 %collective-permute-start.7 = (bf16[528,256]{1,0:T(8,128)(2,1)S(1)}, bf16[528,256]{1,0:T(8,128)(2,1)S(1)}, u32[]{:S(2)}, u32[]{:S(2)}) collective-permute-start(bf16[528,256]{1,0:T(8,128)(2,1)S(1)} %merge.3), channel_id=1, source_target_pairs={{0,4},{1,3},{2,6},{3,1},{4,0},{5,7},{6,2},{7,5},{8,12},{9,11},{10,... | collective-permute-start | bytes 811016 | tf_op jit(solution)/shard_map/ppermute | solution.py:68
  63.8 4.5 %collective-permute-start.8 = (bf16[144,256]{1,0:T(8,128)(2,1)S(1)}, bf16[144,256]{1,0:T(8,128)(2,1)S(1)}, u32[]{:S(2)}, u32[]{:S(2)}) collective-permute-start(bf16[144,256]{1,0:T(8,128)(2,1)S(1)} %get-tuple-element.12), channel_id=1, source_target_pairs={{0,8},{1,9},{2,10},{3,11},{4,12},{5,13},{6,14},{7,15},{8,0},{9,1},... | collective-permute-start | bytes 221192 | tf_op jit(solution)/shard_map/ppermute | solution.py:68
  63.9 5.9 %collective-permute-start.9 = (bf16[144,256]{1,0:T(8,128)(2,1)S(1)}, bf16[144,256]{1,0:T(8,128)(2,1)S(1)}, u32[]{:S(2)}, u32[]{:S(2)}) collective-permute-start(bf16[144,256]{1,0:T(8,128)(2,1)S(1)} %get-tuple-element.13), channel_id=1, source_target_pairs={{0,16},{1,17},{2,18},{3,19},{4,20},{5,21},{6,22},{7,23},{8,24},{9,... | collective-permute-start | bytes 221192 | tf_op jit(solution)/shard_map/ppermute | solution.py:68
  65.6 6.2 %collective-permute-start.10 = (bf16[144,256]{1,0:T(8,128)(2,1)S(1)}, bf16[144,256]{1,0:T(8,128)(2,1)S(1)}, u32[]{:S(2)}, u32[]{:S(2)}) collective-permute-start(bf16[144,256]{1,0:T(8,128)(2,1)S(1)} %get-tuple-element.14), channel_id=1, source_target_pairs={{0,24},{1,25},{2,26},{3,27},{4,28},{5,29},{6,30},{7,31},{8,16},{9,... | collective-permute-start | bytes 221192 | tf_op jit(solution)/shard_map/ppermute | solution.py:68
  72.0 6.1 %collective-permute-start.13 = (bf16[256,128]{1,0:T(8,128)(2,1)S(1)}, bf16[256,128]{1,0:T(8,128)(2,1)S(1)}, u32[]{:S(2)}, u32[]{:S(2)}) collective-permute-start(bf16[256,128]{1,0:T(8,128)(2,1)S(1)} %finish.1), channel_id=1, source_target_pairs={{0,24},{1,25},{2,26},{3,27},{4,28},{5,29},{6,30},{7,31},{8,16},{9,... | collective-permute-start | bytes 196616 | tf_op jit(solution)/shard_map/ppermute | solution.py:68
  74.7 5.2 %collective-permute-start.12 = (bf16[256,128]{1,0:T(8,128)(2,1)S(1)}, bf16[256,128]{1,0:T(8,128)(2,1)S(1)}, u32[]{:S(2)}, u32[]{:S(2)}) collective-permute-start(bf16[256,128]{1,0:T(8,128)(2,1)S(1)} %finish.1), channel_id=1, source_target_pairs={{0,16},{1,17},{2,18},{3,19},{4,20},{5,21},{6,22},{7,23},{8,24},{9,... | collective-permute-start | bytes 196616 | tf_op jit(solution)/shard_map/ppermute | solution.py:68
  74.9 5.0 %collective-permute-start.11 = (bf16[256,128]{1,0:T(8,128)(2,1)S(1)}, bf16[256,128]{1,0:T(8,128)(2,1)S(1)}, u32[]{:S(2)}, u32[]{:S(2)}) collective-permute-start(bf16[256,128]{1,0:T(8,128)(2,1)S(1)} %finish.1), channel_id=1, source_target_pairs={{0,8},{1,9},{2,10},{3,11},{4,12},{5,13},{6,14},{7,15},{8,0},{9,1},... | collective-permute-start | bytes 196616 | tf_op jit(solution)/shard_map/ppermute | solution.py:68
  79.9 9.0 %collective-permute-start.14 = (bf16[4,256,128]{2,1,0:T(8,128)(2,1)S(1)}, bf16[4,256,128]{2,1,0:T(8,128)(2,1)S(1)}, u32[]{:S(2)}, u32[]{:S(2)}) collective-permute-start(bf16[4,256,128]{2,1,0:T(8,128)(2,1)S(1)} %pad_maximum_fusion.1.a0), channel_id=1, source_target_pairs={{0,2},{1,5},{2,0},{3,7},{4,6},{5,1},{6,4},{7,3},{8,10},{9,13},{10,... | collective-permute-start | bytes 786440 | tf_op jit(solution)/shard_map/ppermute | solution.py:68
  81.3 7.8 %collective-permute-start.15 = (bf16[4,256,128]{2,1,0:T(8,128)(2,1)S(1)}, bf16[4,256,128]{2,1,0:T(8,128)(2,1)S(1)}, u32[]{:S(2)}, u32[]{:S(2)}) collective-permute-start(bf16[4,256,128]{2,1,0:T(8,128)(2,1)S(1)} %pad_maximum_fusion.1.a0), channel_id=1, source_target_pairs={{0,4},{1,3},{2,6},{3,1},{4,0},{5,7},{6,2},{7,5},{8,12},{9,11},{10,... | collective-permute-start | bytes 786440 | tf_op jit(solution)/shard_map/ppermute | solution.py:68
  88.9 6.4 %collective-permute-start.16 = (bf16[4,256,128]{2,1,0:T(8,128)(2,1)S(1)}, bf16[4,256,128]{2,1,0:T(8,128)(2,1)S(1)}, u32[]{:S(2)}, u32[]{:S(2)}) collective-permute-start(bf16[4,256,128]{2,1,0:T(8,128)(2,1)S(1)} %collective-permute-done.14.a1), channel_id=1, source_target_pairs={{0,4},{1,3},{2,6},{3,1},{4,0},{5,7},{6,2},{7,5},{8,12},{9,11},{10,... | collective-permute-start | bytes 786440 | tf_op jit(solution)/shard_map/ppermute | solution.py:68
  96.2 1.3 %collective-permute-start.17 = (bf16[4,16,512]{2,1,0:T(8,128)(2,1)S(1)}, bf16[4,16,512]{2,1,0:T(8,128)(2,1)S(1)}, u32[]{:S(2)}, u32[]{:S(2)}) collective-permute-start(bf16[4,16,512]{2,1,0:T(8,128)(2,1)S(1)} %get-tuple-element.16), channel_id=1, source_target_pairs={{0,1},{1,0},{2,3},{3,2},{4,5},{5,4},{6,7},{7,6},{8,9},{9,8},{10,11... | collective-permute-start | bytes 196616 | tf_op jit(solution)/shard_map/ppermute | solution.py:392

commit v2 on v1

v2 whole, which is shorter than its diff:
```python
import functools
import math

import jax
import jax.numpy as jnp
from jax import lax
from jax.experimental import pallas as pl
from jax.experimental.pallas import tpu as pltpu
from jax.sharding import PartitionSpec as P

NEGATIVE = -1e30
POSITIVE = 1e30
STATS = 3
OWN_ROWS = 16
GROUP = 8
LIMIT = 48 * 1024 * 1024

NT = (((1,), (1,)), ((), ()))
TN = (((0,), (0,)), ((), ()))


def whole(space=pltpu.VMEM):
    return pl.BlockSpec(memory_space=space)


def in_bf16(value):
    return value.astype(jnp.bfloat16).astype(jnp.float32)


def stat_rows(units):
    return -(-units * STATS // 16) * 16


class Sizes:
    def __init__(self, ranges, queries, cached, kv):
        self.n = ranges
        self.cand, self.toks, self.heads, self.width = queries
        self.kv = kv
        self.group = self.heads // kv
        self.blocks, self.block_tokens = cached[0], cached[1]
        self.lines = ranges // kv
        self.row_groups = self.lines // self.cand
        self.tokens = self.toks * ranges
        self.group_tokens = self.tokens // self.row_groups
        self.rows = self.group_tokens * self.group
        if kv != 4 or self.row_groups * self.cand * kv != ranges:
            raise ValueError("shape")


def place(size, line, first, second):
    me, core = lax.axis_index("ctx"), lax.axis_index("tp")
    other = (me // size.kv) ^ line
    return other * size.kv + ((me % size.kv) ^ (first * (1 + core)) ^ (second * (2 - core)))


def hop(size, value, stage):
    pairs = []
    cores = lax.axis_size("tp")
    for c in range(size.n):
        for core in range(cores):
            if stage == "first":
                other = c ^ (1 + core)
            elif stage == "second":
                other = c ^ (2 - core)
            else:
                other = c ^ (stage * size.kv)
            pairs.append((c * cores + core, other * cores + core))
    return lax.ppermute(value, ("ctx", "tp"), pairs)


def gather_lines(size, value):
    return jnp.stack([value] + [hop(size, value, k) for k in range(1, size.lines)])


def attention_kernel(size, second, firsts, lists, counts, qa, qb, keys, values, own_keys, own_values, *rest):
    outs, (rows, acc, tops, sums, stats) = rest[: len(firsts)], rest[len(firsts) :]
    units = 2 * size.lines
    half = size.rows // 2
    chip_rows = size.toks * size.group
    scale = size.width ** (-0.5) * math.log2(math.e)
    me, core = lax.axis_index("ctx"), lax.axis_index("tp")
    here, spot = me // size.kv, me % size.kv
    a_here = (spot >> core) & 1
    b_side = ((spot >> (1 - core)) & 1) ^ second
    for first, ref in enumerate((qa, qb)):
        for line in range(size.lines):
            other = here ^ line
            chip = (other % size.cand) * 2 + (a_here ^ first)
            for j in range(size.cand):
                parts = [ref[line, j, t].astype(jnp.float32) for t in range(size.toks)]
                for kv in range(size.kv):
                    cut = [p[kv * size.group : (kv + 1) * size.group] for p in parts]
                    rows[other // size.cand, j, kv, chip] = jnp.concatenate(cut).astype(jnp.bfloat16)
    heads = [place(size, 0, f, s) % size.kv for f in firsts for s in range(2)]

    def weighed(scores, live, before):
        high = before
        for s, alive in zip(scores, live):
            top = jnp.max(s, axis=0, keepdims=True) * scale
            top = in_bf16(top if alive is None else jnp.where(alive, top, NEGATIVE))
            high = top if high is None else jnp.maximum(high, top)
        weights, total = [], None
        for s, alive in zip(scores, live):
            shift = high if alive is None else jnp.where(alive, high, POSITIVE)
            p = jnp.exp2(s * scale - shift)
            part = jnp.sum(p, axis=0, keepdims=True)
            total = part if total is None else total + part
            weights.append(p.astype(jnp.bfloat16))
        return high, weights, total

    def blocks_of(j, head, q, g):
        slots = [g * GROUP + b for b in range(GROUP)]
        live = [slot < counts[j] for slot in slots]
        blocks = [lists[j, slot] for slot in slots]
        scores = [
            lax.dot_general(keys[head, block], q, NT, preferred_element_type=jnp.float32)
            for block in blocks
        ]
        return scores, live, [values[head, block] for block in blocks]

    def part(group, carry):
        lane = lax.broadcasted_iota(jnp.int32, (OWN_ROWS, half), 1)
        chip = lane // chip_rows
        line = group * size.cand + chip // 2
        chip = line * size.kv + ((chip % 2) << core) + (b_side << (1 - core))
        token = chip * size.toks + (lane % chip_rows) // size.group
        own = lax.broadcasted_iota(jnp.int32, (OWN_ROWS, half), 0)
        seen = (own < size.toks) & (own + me * size.toks <= token)
        for j in range(size.cand):
            for h, head in enumerate(heads):
                q = rows[group, j, head].reshape(half, size.width)
                s = lax.dot_general(
                    own_keys[j, head], q, NT, preferred_element_type=jnp.float32
                )
                scores, live, cut = blocks_of(j, head, q, 0)
                s = jnp.where(seen, s, NEGATIVE)
                scores, live, cut = [s] + scores, [None] + live, [own_values[j, head]] + cut
                high, weights, total = weighed(scores, live, None)
                none = high <= 0.5 * NEGATIVE * scale
                weights[0] = jnp.where(none, 0.0, weights[0].astype(jnp.float32)).astype(jnp.bfloat16)
                total = jnp.where(none, 0.0, total)
                acc[j, h] = lax.dot_general(
                    jnp.concatenate(cut), jnp.concatenate(weights), TN, preferred_element_type=jnp.float32
                )
                tops[j, h] = jnp.broadcast_to(high, (8, half))
                sums[j, h] = jnp.broadcast_to(total, (8, half))

        def more(j, carry):
            def over(g, carry):
                for h, head in enumerate(heads):
                    q = rows[group, j, head].reshape(half, size.width)
                    scores, live, cut = blocks_of(j, head, q, g)
                    before = tops[j, h, 0:1]
                    high, weights, total = weighed(scores, live, before)
                    fade = jnp.exp2(before - high)
                    acc[j, h] = acc[j, h] * fade + lax.dot_general(
                        jnp.concatenate(cut),
                        jnp.concatenate(weights),
                        TN,
                        preferred_element_type=jnp.float32,
                    )
                    sums[j, h] = jnp.broadcast_to(sums[j, h, 0:1] * fade + total, (8, half))
                    tops[j, h] = jnp.broadcast_to(high, (8, half))
                return carry

            return lax.fori_loop(1, (counts[j] + GROUP - 1) // GROUP, over, carry)

        lax.fori_loop(0, size.cand, more, 0)
        for j in range(size.cand):
            for h in range(len(heads)):
                out, unit = outs[h // 2], (h % 2) * size.lines + group * size.cand + j
                at = pl.multiple_of(unit * size.width, size.width)
                out[pl.ds(at, size.width), :] = acc[j, h].astype(jnp.bfloat16)
                l = sums[j, h, 0:1]
                rounded = in_bf16(l)
                stats[h // 2, pl.ds(unit, 1), :] = tops[j, h, 0:1]
                stats[h // 2, pl.ds(units + unit, 1), :] = rounded
                stats[h // 2, pl.ds(2 * units + unit, 1), :] = l - rounded
        return carry

    stats[...] = jnp.zeros_like(stats)
    lax.fori_loop(0, size.row_groups, part, 0)
    for f, out in enumerate(outs):
        out[pl.ds(units * size.width, stat_rows(units)), :] = stats[f].astype(jnp.bfloat16)


def attention_part(size, second, firsts, lists, counts, qa, qb, keys, values, own_keys, own_values):
    units, half = 2 * size.lines, size.rows // 2
    length = units * size.width + stat_rows(units)
    count = 2 * len(firsts)
    chips = size.n // size.row_groups // 2
    return pl.pallas_call(
        functools.partial(attention_kernel, size, second, firsts),
        out_shape=[jax.ShapeDtypeStruct((length, half), jnp.bfloat16)] * len(firsts),
        in_specs=[whole(pltpu.SMEM)] * 2 + [whole()] * 6,
        out_specs=[whole()] * len(firsts),
        scratch_shapes=[
            pltpu.VMEM(
                (size.row_groups, size.cand, size.kv, chips, size.toks * size.group, size.width),
                jnp.bfloat16,
            ),
            pltpu.VMEM((size.cand, count, size.width, half), jnp.float32),
            pltpu.VMEM((size.cand, count, 8, half), jnp.float32),
            pltpu.VMEM((size.cand, count, 8, half), jnp.float32),
            pltpu.VMEM((len(firsts), stat_rows(units), half), jnp.float32),
        ],
        compiler_params=pltpu.CompilerParams(vmem_limit_bytes=LIMIT),
        name="attention",
    )(lists, counts, qa, qb, keys, values, own_keys, own_values)


def merge_units(size, parts, firsts, stats_at, unit_lists, units_of):
    stats = []
    for ref, at, units, unit in zip(parts, stats_at, units_of, unit_lists):
        block = ref[pl.ds(at, stat_rows(units)), :].astype(jnp.float32)
        m = block[unit : unit + 1]
        l = block[units + unit : units + unit + 1] + block[2 * units + unit : 2 * units + unit + 1]
        stats.append((m, l))
    high = functools.reduce(jnp.maximum, [m for m, _ in stats])
    fades = [jnp.exp2(m - high) for m, _ in stats]
    total = functools.reduce(jnp.add, [l * f for (_, l), f in zip(stats, fades)])
    sums = None
    for ref, unit, fade in zip(parts, unit_lists, fades):
        value = ref[pl.ds(unit * size.width, size.width), :].astype(jnp.float32) * fade
        sums = value if sums is None else sums + value
    return sums, high, total


def merge_pair(size, mine, theirs, unit, units):
    at = units * size.width
    return merge_units(size, (mine, theirs), (0, 0), (at, at), (unit, unit), (units, units))


def merge_kernel(size, start, units, units_in, mine, theirs, out):
    highs, totals = [], []
    for unit in range(units):
        sums, high, total = merge_pair(size, mine, theirs, start + unit, units_in)
        out[pl.ds(unit * size.width, size.width), :] = sums.astype(jnp.bfloat16)
        highs.append(high)
        totals.append(total)
    lengths = [in_bf16(t) for t in totals]
    rows = highs + lengths + [t - l for t, l in zip(totals, lengths)]
    left = stat_rows(units) - len(rows)
    if left:
        rows.append(jnp.zeros((left, mine.shape[1]), jnp.float32))
    out[pl.ds(units * size.width, stat_rows(units)), :] = jnp.concatenate(rows).astype(jnp.bfloat16)


def merge(size, start, units, units_in, mine, theirs):
    length = units * size.width + stat_rows(units)
    return pl.pallas_call(
        functools.partial(merge_kernel, size, start, units, units_in),
        out_shape=jax.ShapeDtypeStruct((length, mine.shape[1]), jnp.bfloat16),
        in_specs=[whole()] * 2,
        out_specs=whole(),
        compiler_params=pltpu.CompilerParams(vmem_limit_bytes=LIMIT),
        name="merge",
    )(mine, theirs)


def split_kernel(size, near_mine, near_theirs, far_mine, far_theirs, *outs):
    here = lax.axis_index("ctx") // size.kv
    lines, width = size.lines, size.width
    for unit in range(lines):
        merged = [
            merge_pair(size, near_mine, near_theirs, unit, lines),
            merge_pair(size, far_mine, far_theirs, unit, lines),
        ]
        lengths = [in_bf16(total) for _, _, total in merged]
        tail = [high for _, high, _ in merged] + lengths
        tail += [total - length for (_, _, total), length in zip(merged, lengths)]
        tail.append(jnp.zeros((stat_rows(2) - len(tail), near_mine.shape[1]), jnp.float32))
        tail = jnp.concatenate(tail).astype(jnp.bfloat16)
        bodies = [sums.astype(jnp.bfloat16) for sums, _, _ in merged]
        for line, out in enumerate(outs):

            @pl.when((here ^ line) == unit)
            def _():
                out[:width, :] = bodies[0]
                out[width : 2 * width, :] = bodies[1]
                out[2 * width :, :] = tail


def split_merge(size, near_mine, near_theirs, far_mine, far_theirs):
    shape = jax.ShapeDtypeStruct((2 * size.width + stat_rows(2), size.rows // 2), jnp.bfloat16)
    return pl.pallas_call(
        functools.partial(split_kernel, size),
        out_shape=[shape] * size.lines,
        in_specs=[whole()] * 4,
        out_specs=[whole()] * size.lines,
        compiler_params=pltpu.CompilerParams(vmem_limit_bytes=LIMIT),
        name="split",
    )(near_mine, near_theirs, far_mine, far_theirs)


def finish_kernel(size, *refs):
    parts, out, turned = refs[:-2], refs[-2], refs[-1]
    count = len(parts)
    chip_rows = size.toks * size.group
    spot, core = lax.axis_index("ctx") % size.kv, lax.axis_index("tp")
    b_here = (spot >> (1 - core)) & 1
    for side in range(2):
        at = 2 * size.width
        sums, _, total = merge_units(
            size, parts, (0,) * count, (at,) * count, (side,) * count, (2,) * count
        )
        half = (sums / total).T
        for chip in range(size.n // size.row_groups // 2):
            absolute = chip // 2 * size.kv + ((chip % 2) << core) + ((b_here ^ side) << (1 - core))
            to = pl.multiple_of(absolute * chip_rows, chip_rows)
            turned[pl.ds(to, chip_rows), :] = half[chip * chip_rows : (chip + 1) * chip_rows]
    for g in range(size.group):
        piece = turned[pl.ds(g, size.group_tokens, stride=size.group), :]
        out[pl.ds(g * size.group_tokens, size.group_tokens), :] = piece.astype(jnp.bfloat16)


def finish(size, parts):
    return pl.pallas_call(
        functools.partial(finish_kernel, size),
        out_shape=jax.ShapeDtypeStruct((size.rows, size.width), jnp.bfloat16),
        in_specs=[whole()] * len(parts),
        out_specs=whole(),
        scratch_shapes=[pltpu.VMEM((size.rows, size.width), jnp.float32)],
        compiler_params=pltpu.CompilerParams(vmem_limit_bytes=LIMIT),
        name="finish",
    )(*parts)


def project_kernel(size, a0, a1, a2, a3, weight, kept, sent, whole_rows, product):
    core = lax.axis_index("tp")
    for index, ref in enumerate((a0, a1, a2, a3)):
        for line in range(size.lines):
            chip = place(size, line, index % 2, index // 2)
            kv, other = chip % size.kv, chip // size.kv
            j, part = other % size.cand, other // size.cand
            at = pl.multiple_of(j * size.tokens + part * size.group_tokens, size.group_tokens)
            for g in range(size.group):
                piece = ref[line, pl.ds(g * size.group_tokens, size.group_tokens), :]
                whole_rows[kv * size.group + g, pl.ds(at, size.group_tokens), :] = piece
    total = None
    for h in range(0, size.heads, 2):
        pair = jnp.concatenate([whole_rows[h], whole_rows[h + 1]], axis=1)
        term = jnp.dot(
            pair,
            weight[pl.ds(h * size.width, 2 * size.width), :],
            preferred_element_type=jnp.float32,
        )
        total = term if total is None else total + term
    product[...] = total
    half = size.tokens // 2
    for j in range(size.cand):
        near = pl.multiple_of(j * size.tokens + core * half, half)
        far = pl.multiple_of(j * size.tokens + (1 - core) * half, half)
        kept[j] = product[pl.ds(near, half), :]
        sent[j] = product[pl.ds(far, half), :].astype(jnp.bfloat16)


def project(size, gathered, weight):
    columns = weight.shape[1]
    shape = (size.cand, size.tokens // 2, columns)
    return pl.pallas_call(
        functools.partial(project_kernel, size),
        out_shape=[
            jax.ShapeDtypeStruct(shape, jnp.float32),
            jax.ShapeDtypeStruct(shape, jnp.bfloat16),
        ],
        in_specs=[whole()] * 5,
        out_specs=[whole()] * 2,
        scratch_shapes=[
            pltpu.VMEM((size.heads, size.cand * size.tokens, size.width), jnp.bfloat16),
            pltpu.VMEM((size.cand * size.tokens, columns), jnp.float32),
        ],
        compiler_params=pltpu.CompilerParams(vmem_limit_bytes=LIMIT),
        name="project",
    )(*gathered, weight)


def gather_all(size, value):
    a0 = gather_lines(size, value)
    a1 = hop(size, a0, "first")
    a2 = hop(size, a0, "second")
    a3 = hop(size, a1, "second")
    return a0, a1, a2, a3


def listed_here(size, block_lists):
    lowest = lax.axis_index("ctx") * size.blocks
    local = block_lists - lowest
    below = jnp.sum((local < 0).astype(jnp.int32), axis=1)
    inside = jnp.sum((local < size.blocks).astype(jnp.int32), axis=1) - below
    slots = jnp.arange(-(-size.blocks // GROUP) * GROUP)
    entry = jnp.arange(block_lists.shape[1])
    hit = entry[None, None, :] == (below[:, None] + slots[None, :])[:, :, None]
    hit = hit & (slots[None, :] < inside[:, None])[:, :, None]
    return jnp.sum(jnp.where(hit, local[:, None, :], 0), axis=2), inside


def on_device(
    queries,
    cand_keys,
    candidate_values,
    cached_prompt_keys,
    cached_prompt_values,
    block_lists,
    out_weight,
):
    size = Sizes(
        lax.axis_size("ctx"), queries.shape, cached_prompt_keys.shape, cand_keys.shape[2]
    )
    lists, counts = listed_here(size, block_lists)
    keys = jnp.transpose(cached_prompt_keys, (2, 0, 1, 3))
    values = jnp.transpose(cached_prompt_values, (2, 0, 1, 3))
    room = ((0, 0), (0, 0), (0, OWN_ROWS - size.toks), (0, 0))
    own_keys = jnp.pad(jnp.transpose(cand_keys, (0, 2, 1, 3)), room)
    own_values = jnp.pad(jnp.transpose(candidate_values, (0, 2, 1, 3)), room)
    moved = [queries] + [hop(size, queries, k) for k in range(1, size.lines)]
    ready = (lists, counts, keys, values, own_keys, own_values)
    moved, ready = lax.optimization_barrier((moved, ready))
    lists, counts, keys, values, own_keys, own_values = ready
    q0 = jnp.stack(moved)
    q1, q2 = hop(size, q0, "first"), hop(size, q0, "second")
    q3 = hop(size, q1, "second")
    lines, units = size.lines, 2 * size.lines
    near_away, near = attention_part(size, 0, (1, 0), lists, counts, q0, q1, *ready[2:])
    near_away = hop(size, near_away, "first")
    (far_away,) = attention_part(size, 1, (1,), lists, counts, q2, q3, *ready[2:])
    far_away = hop(size, far_away, "first")
    (far,) = attention_part(size, 1, (0,), lists, counts, q2, q3, *ready[2:])
    near_leaves = hop(size, merge(size, lines, lines, units, near, near_away), "second")
    near_stays = merge(size, 0, lines, units, near, near_away)
    far_leaves = hop(size, merge(size, lines, lines, units, far, far_away), "second")
    far_stays = merge(size, 0, lines, units, far, far_away)
    parts = split_merge(size, near_stays, far_leaves, far_stays, near_leaves)
    parts = [parts[0]] + [hop(size, parts[k], k) for k in range(1, lines)]
    attention = finish(size, parts)
    kept, sent = project(size, gather_all(size, attention), out_weight)
    cores = lax.axis_size("tp")
    sent = lax.ppermute(sent, "tp", [(i, cores - 1 - i) for i in range(cores)])
    return (kept + sent.astype(jnp.float32)).astype(jnp.bfloat16)


def solution(mesh):
    placed = (
        P("groups", "ctx", "tp", None),
        P("groups", "ctx", "tp", None),
        P("groups", "ctx", "tp", None),
        P(("groups", "ctx"), None, "tp", None),
        P(("groups", "ctx"), None, "tp", None),
        P("groups", None),
        P("tp", "ctx"),
    )
    return jax.shard_map(
        on_device, mesh=mesh, in_specs=placed, out_specs=P("groups", "tp", "ctx"), check_vma=False
    )
```

time: 98 us -> 87.2 us (0.89)
  waiting for transfers between devices: 41.7 us -> 32.7 us
  local copies, waits for them, and re-layouts: 9.46 us -> 4.73 us
  starting transfers between devices: 20 us -> 23.7 us
    ppermute x17 -> x19, waiting for transfers between devices: 40.4 us -> 31.5 us  [hop(): return lax.ppermute(value, ('ctx', 'tp'), pairs)]
    unnamed x8 -> x6, local copies, waits for them, and re-layouts: 9.44 us -> 1.43 us
    ppermute x17 -> x19, starting transfers between devices: 19.9 us -> 23.6 us  [hop(): return lax.ppermute(value, ('ctx', 'tp'), pairs)]
    transpose x0 -> x1, local copies, waits for them, and re-layouts: none -> 3.28 us  [on_device(): values = jnp.transpose(cached_prompt_values, (2, 0, 1, 3))]
    pallas_call x2 -> x3, Pallas kernels: 22.6 us -> 22.7 us  [attention_part(): pl.pallas_call(functools.partial(attention_kernel, size, second, firsts),...]
  transfers between devices with their start and end apart: 18 -> 20, of which waited for: 12 -> 11; matrix products, arithmetic and copies ran while one was open for 9% -> 7% of each run, Pallas kernels for 12% -> 26%
where the time goes in v2:
time: 87.2 us; the launch traced here: 87.4 us
  waiting for transfers between devices  32.7 us (38%)
  Pallas kernels  24.3 us (28%)
  starting transfers between devices  23.7 us (27%)
  local copies, waits for them, and re-layouts  4.73 us (5%)
  other arithmetic  1.92 us (2%)
    ppermute x19, waiting for transfers between devices, hop(): return lax.ppermute(value, ('ctx', 'tp'), pairs)  31.5 us
    ppermute x19, starting transfers between devices, hop(): return lax.ppermute(value, ('ctx', 'tp'), pairs)  23.6 us
    pallas_call x3, Pallas kernels, attention_part(): pl.pallas_call(functools.partial(attention_kernel, size, second, firsts),...  22.7 us
    transpose x1, local copies, waits for them, and re-layouts, on_device(): values = jnp.transpose(cached_prompt_values, (2, 0, 1, 3))  3.28 us
  transfers between devices with their start and end apart: 20, of which 11 were waited for; matrix products, arithmetic and copies ran while one was open for 7% of the time, Pallas kernels for 26%

profile of v2, /device:TPU:0, one launch (start us, length us, event | category | flops | bytes accessed | tf_op | source)
XLA Modules:
  0.0 87.4 jit_solution(2804494914933802877)
XLA Ops:
  0.0 4.0 %collective-permute-start.1 = (bf16[4,2,32,128]{3,2,1,0:T(8,128)(2,1)}, bf16[4,2,32,128]{3,2,1,0:T(8,128)(2,1)S(1)}, u32[]{:S(2)}, u32[]{:S(2)}) collective-permute-start(bf16[4,2,32,128]{3,2,1,0:T(8,128)(2,1)} %param.7), channel_id=1, source_target_pairs={{0,16},{1,17},{2,18},{3,19},{4,20},{5,21},{6,22},{7,23},{8,24},{9,... | collective-permute-start | bytes 196616 | tf_op jit(solution)/shard_map/ppermute | solution.py:68
  4.0 1.6 %collective-permute-start = (bf16[4,2,32,128]{3,2,1,0:T(8,128)(2,1)}, bf16[4,2,32,128]{3,2,1,0:T(8,128)(2,1)S(1)}, u32[]{:S(2)}, u32[]{:S(2)}) collective-permute-start(bf16[4,2,32,128]{3,2,1,0:T(8,128)(2,1)} %param.7), channel_id=1, source_target_pairs={{0,8},{1,9},{2,10},{3,11},{4,12},{5,13},{6,14},{7,15},{8,0},{9,1},... | collective-permute-start | bytes 196616 | tf_op jit(solution)/shard_map/ppermute | solution.py:68
  5.6 0.0 collective-permute-start.2
  5.6 0.8 convert_reduce_fusion
  6.4 0.1 iota_add_fusion
  6.5 0.1 iota_compare_fusion.1
  6.6 0.7 copy.21
  7.3 0.7 copy.20
  8.0 0.0 copy-start.1
  8.1 3.3 %copy_bitcast_fusion = (bf16[4,16,128,128]{3,2,1,0:T(8,128)(2,1)S(1)}, bf16[4,16,128,128]{3,2,1,0:T(8,128)(2,1)S(1)}) fusion(bf16[16,128,4,128]{3,2,1,0:T(4,128)(2,1)} %param.11, bf16[16,128,4,128]{3,2,1,0:T(4,128)(2,1)} %param.10), kind=kLoop, calls=%fused_computation | loop fusion | bytes 8388608 | tf_op jit(solution)/shard_map/transpose | solution.py:412
  11.4 0.2 select_reduce_fusion.lists
  11.6 0.0 collective-permute-done.1
  11.6 0.0 collective-permute-done
  11.6 0.3 collective-permute-done.2
  11.9 0.0 copy-done.1
  11.9 1.6 %collective-permute-start.3 = (bf16[4,4,2,32,128]{4,3,2,1,0:T(8,128)(2,1)S(1)}, bf16[4,4,2,32,128]{4,3,2,1,0:T(8,128)(2,1)S(1)}, u32[]{:S(2)}, u32[]{:S(2)}) collective-permute-start(bf16[4,4,2,32,128]{4,3,2,1,0:T(8,128)(2,1)S(1)} %pad_maximum_fusion.qa), channel_id=1, source_target_pairs={{0,2},{1,5},{2,0},{3,7},{4,6},{5,1},{6,4},{7,3},{8,10},{9,13},{10,... | collective-permute-start | bytes 786440 | tf_op jit(solution)/shard_map/ppermute | solution.py:68
  13.5 1.5 %collective-permute-start.5 = (bf16[4,4,2,32,128]{4,3,2,1,0:T(8,128)(2,1)S(1)}, bf16[4,4,2,32,128]{4,3,2,1,0:T(8,128)(2,1)S(1)}, u32[]{:S(2)}, u32[]{:S(2)}) collective-permute-start(bf16[4,4,2,32,128]{4,3,2,1,0:T(8,128)(2,1)S(1)} %pad_maximum_fusion.qa), channel_id=1, source_target_pairs={{0,4},{1,3},{2,6},{3,1},{4,0},{5,7},{6,2},{7,5},{8,12},{9,11},{10,... | collective-permute-start | bytes 786440 | tf_op jit(solution)/shard_map/ppermute | solution.py:68
  15.0 6.1 %collective-permute-done.3.qb = bf16[4,4,2,32,128]{4,3,2,1,0:T(8,128)(2,1)S(1)} collective-permute-done((bf16[4,4,2,32,128]{4,3,2,1,0:T(8,128)(2,1)S(1)}, bf16[4,4,2,32,128]{4,3,2,1,0:T(8,128)(2,1)S(1)}, u32[]{:S(2)}, u32[]{:S(2)}) %collective-permute-start.3) | collective-permute-done | bytes 262176 | tf_op jit(solution)/shard_map/ppermute | solution.py:68
  21.1 0.1 collective-permute-start.6
  21.2 10.9 %attention.3 = (bf16[1056,128]{1,0:T(8,128)(2,1)S(1)}, bf16[1056,128]{1,0:T(8,128)(2,1)S(1)}) custom-call(s32[4,16]{1,0:T(4,128)S(1)} %select_reduce_fusion.lists, s32[4]{0:T(128)S(1)} %sub.15.counts, bf16[4,4,2,32,128]{4,3,2,1,0:T(8,128)(2,1)S(1)} %pad_maximum_fusion.qa, bf16[4,4,2,32,128]{4,3,2,1,0:T(8,128)(2,1)S(1)} %collective-permute-done.3.qb, ...), custom_call_target="tpu_custom_call" | custom-call | tf_op jit(solution)/shard_map/attention/pallas_call | solution.py:192
  32.1 0.1 collective-permute-start.4
  32.2 0.0 collective-permute-done.5.qa
  32.2 0.0 collective-permute-done.6.qb
  32.2 5.9 %attention.5 = bf16[1056,128]{1,0:T(8,128)(2,1)S(1)} custom-call(s32[4,16]{1,0:T(4,128)S(1)} %select_reduce_fusion.lists, s32[4]{0:T(128)S(1)} %sub.15.counts, bf16[4,4,2,32,128]{4,3,2,1,0:T(8,128)(2,1)S(1)} %collective-permute-done.5.qa, bf16[4,4,2,32,128]{4,3,2,1,0:T(8,128)(2,1)S(1)} %collective-permute-done.6.qb, ...), custom_call_target="tpu_custom_call" | custom-call | tf_op jit(solution)/shard_map/attention/pallas_call | solution.py:192
  38.1 1.1 %collective-permute-start.7 = (bf16[1056,128]{1,0:T(8,128)(2,1)S(1)}, bf16[1056,128]{1,0:T(8,128)(2,1)S(1)}, u32[]{:S(2)}, u32[]{:S(2)}) collective-permute-start(bf16[1056,128]{1,0:T(8,128)(2,1)S(1)} %attention.5), channel_id=1, source_target_pairs={{0,2},{1,5},{2,0},{3,7},{4,6},{5,1},{6,4},{7,3},{8,10},{9,13},{10,... | collective-permute-start | bytes 811016 | tf_op jit(solution)/shard_map/ppermute | solution.py:68
  39.2 0.0 copy-start
  39.2 5.9 %attention.4.mine = bf16[1056,128]{1,0:T(8,128)(2,1)S(1)} custom-call(s32[4,16]{1,0:T(4,128)S(1)} %select_reduce_fusion.lists, s32[4]{0:T(128)S(1)} %sub.15.counts, bf16[4,4,2,32,128]{4,3,2,1,0:T(8,128)(2,1)S(1)} %collective-permute-done.5.qa, bf16[4,4,2,32,128]{4,3,2,1,0:T(8,128)(2,1)S(1)} %collective-permute-done.6.qb, ...), custom_call_target="tpu_custom_call" | custom-call | tf_op jit(solution)/shard_map/attention/pallas_call | solution.py:192
  45.1 0.0 collective-permute-done.4.theirs
  45.1 0.1 merge.7
  45.2 0.1 collective-permute-start.9
  45.2 0.0 collective-permute-done.7.theirs
  45.2 0.1 merge.5
  45.3 2.1 %collective-permute-start.8 = (bf16[528,128]{1,0:T(8,128)(2,1)S(1)}, bf16[528,128]{1,0:T(8,128)(2,1)S(1)}, u32[]{:S(2)}, u32[]{:S(2)}) collective-permute-start(bf16[528,128]{1,0:T(8,128)(2,1)S(1)} %merge.5), channel_id=1, source_target_pairs={{0,4},{1,3},{2,6},{3,1},{4,0},{5,7},{6,2},{7,5},{8,12},{9,11},{10,... | collective-permute-start | bytes 405512 | tf_op jit(solution)/shard_map/ppermute | solution.py:68
  47.4 0.1 merge.4.near_mine
  47.5 0.1 merge.6.far_mine
  47.5 2.7 %collective-permute-done.9.far_theirs = bf16[528,128]{1,0:T(8,128)(2,1)S(1)} collective-permute-done((bf16[528,128]{1,0:T(8,128)(2,1)S(1)}, bf16[528,128]{1,0:T(8,128)(2,1)S(1)}, u32[]{:S(2)}, u32[]{:S(2)}) %collective-permute-start.9) | collective-permute-done | bytes 135200 | tf_op jit(solution)/shard_map/ppermute | solution.py:68
  50.2 1.4 %collective-permute-done.8.near_theirs = bf16[528,128]{1,0:T(8,128)(2,1)S(1)} collective-permute-done((bf16[528,128]{1,0:T(8,128)(2,1)S(1)}, bf16[528,128]{1,0:T(8,128)(2,1)S(1)}, u32[]{:S(2)}, u32[]{:S(2)}) %collective-permute-start.8) | collective-permute-done | bytes 135200 | tf_op jit(solution)/shard_map/ppermute | solution.py:68
  51.7 0.2 split.1
  51.9 2.0 %collective-permute-start.10 = (bf16[272,128]{1,0:T(8,128)(2,1)S(1)}, bf16[272,128]{1,0:T(8,128)(2,1)S(1)}, u32[]{:S(2)}, u32[]{:S(2)}) collective-permute-start(bf16[272,128]{1,0:T(8,128)(2,1)S(1)} %get-tuple-element.36), channel_id=1, source_target_pairs={{0,8},{1,9},{2,10},{3,11},{4,12},{5,13},{6,14},{7,15},{8,0},{9,1},... | collective-permute-start | bytes 208904 | tf_op jit(solution)/shard_map/ppermute | solution.py:68
  53.9 3.2 %collective-permute-start.11 = (bf16[272,128]{1,0:T(8,128)(2,1)S(1)}, bf16[272,128]{1,0:T(8,128)(2,1)S(1)}, u32[]{:S(2)}, u32[]{:S(2)}) collective-permute-start(bf16[272,128]{1,0:T(8,128)(2,1)S(1)} %get-tuple-element.37), channel_id=1, source_target_pairs={{0,16},{1,17},{2,18},{3,19},{4,20},{5,21},{6,22},{7,23},{8,24},{9,... | collective-permute-start | bytes 208904 | tf_op jit(solution)/shard_map/ppermute | solution.py:68
  57.1 0.0 collective-permute-start.12
  57.1 0.0 collective-permute-done.10.refs_1_
  57.1 3.2 %collective-permute-done.11.refs_2_ = bf16[272,128]{1,0:T(8,128)(2,1)S(1)} collective-permute-done((bf16[272,128]{1,0:T(8,128)(2,1)S(1)}, bf16[272,128]{1,0:T(8,128)(2,1)S(1)}, u32[]{:S(2)}, u32[]{:S(2)}) %collective-permute-start.11) | collective-permute-done | bytes 69664 | tf_op jit(solution)/shard_map/ppermute | solution.py:68
  60.3 3.7 %collective-permute-done.12.refs_3_ = bf16[272,128]{1,0:T(8,128)(2,1)S(1)} collective-permute-done((bf16[272,128]{1,0:T(8,128)(2,1)S(1)}, bf16[272,128]{1,0:T(8,128)(2,1)S(1)}, u32[]{:S(2)}, u32[]{:S(2)}) %collective-permute-start.12) | collective-permute-done | bytes 69664 | tf_op jit(solution)/shard_map/ppermute | solution.py:68
  64.0 0.2 finish.1
  64.1 1.4 %collective-permute-start.15 = (bf16[256,128]{1,0:T(8,128)(2,1)S(1)}, bf16[256,128]{1,0:T(8,128)(2,1)S(1)}, u32[]{:S(2)}, u32[]{:S(2)}) collective-permute-start(bf16[256,128]{1,0:T(8,128)(2,1)S(1)} %finish.1), channel_id=1, source_target_pairs={{0,24},{1,25},{2,26},{3,27},{4,28},{5,29},{6,30},{7,31},{8,16},{9,... | collective-permute-start | bytes 196616 | tf_op jit(solution)/shard_map/ppermute | solution.py:68
  65.5 0.2 collective-permute-start.14
  65.8 2.8 %collective-permute-start.13 = (bf16[256,128]{1,0:T(8,128)(2,1)S(1)}, bf16[256,128]{1,0:T(8,128)(2,1)S(1)}, u32[]{:S(2)}, u32[]{:S(2)}) collective-permute-start(bf16[256,128]{1,0:T(8,128)(2,1)S(1)} %finish.1), channel_id=1, source_target_pairs={{0,8},{1,9},{2,10},{3,11},{4,12},{5,13},{6,14},{7,15},{8,0},{9,1},... | collective-permute-start | bytes 196616 | tf_op jit(solution)/shard_map/ppermute | solution.py:68
  68.6 1.7 %collective-permute-done.15 = bf16[256,128]{1,0:T(8,128)(2,1)S(1)} collective-permute-done((bf16[256,128]{1,0:T(8,128)(2,1)S(1)}, bf16[256,128]{1,0:T(8,128)(2,1)S(1)}, u32[]{:S(2)}, u32[]{:S(2)}) %collective-permute-start.15) | collective-permute-done | bytes 65568 | tf_op jit(solution)/shard_map/ppermute | solution.py:68
  70.3 1.4 %collective-permute-done.14 = bf16[256,128]{1,0:T(8,128)(2,1)S(1)} collective-permute-done((bf16[256,128]{1,0:T(8,128)(2,1)S(1)}, bf16[256,128]{1,0:T(8,128)(2,1)S(1)}, u32[]{:S(2)}, u32[]{:S(2)}) %collective-permute-start.14) | collective-permute-done | bytes 65568 | tf_op jit(solution)/shard_map/ppermute | solution.py:68
  71.7 0.0 collective-permute-done.13
  71.7 0.5 collective-permute-start.16
  72.2 1.1 %collective-permute-start.17 = (bf16[4,256,128]{2,1,0:T(8,128)(2,1)S(1)}, bf16[4,256,128]{2,1,0:T(8,128)(2,1)S(1)}, u32[]{:S(2)}, u32[]{:S(2)}) collective-permute-start(bf16[4,256,128]{2,1,0:T(8,128)(2,1)S(1)} %pad_maximum_fusion.1.a0), channel_id=1, source_target_pairs={{0,4},{1,3},{2,6},{3,1},{4,0},{5,7},{6,2},{7,5},{8,12},{9,11},{10,... | collective-permute-start | bytes 786440 | tf_op jit(solution)/shard_map/ppermute | solution.py:68
  73.2 4.9 %collective-permute-done.16.a1 = bf16[4,256,128]{2,1,0:T(8,128)(2,1)S(1)} collective-permute-done((bf16[4,256,128]{2,1,0:T(8,128)(2,1)S(1)}, bf16[4,256,128]{2,1,0:T(8,128)(2,1)S(1)}, u32[]{:S(2)}, u32[]{:S(2)}) %collective-permute-start.16) | collective-permute-done | bytes 262176 | tf_op jit(solution)/shard_map/ppermute | solution.py:68
  78.2 0.4 collective-permute-start.18
  78.5 0.0 collective-permute-done.17.a2
  78.5 6.0 %collective-permute-done.18.a3 = bf16[4,256,128]{2,1,0:T(8,128)(2,1)S(1)} collective-permute-done((bf16[4,256,128]{2,1,0:T(8,128)(2,1)S(1)}, bf16[4,256,128]{2,1,0:T(8,128)(2,1)S(1)}, u32[]{:S(2)}, u32[]{:S(2)}) %collective-permute-start.18) | collective-permute-done | bytes 262176 | tf_op jit(solution)/shard_map/ppermute | solution.py:68
  84.5 0.0 copy-done
  84.5 0.9 %project.1 = (f32[4,16,512]{2,1,0:T(8,128)S(1)}, bf16[4,16,512]{2,1,0:T(8,128)(2,1)S(1)}) custom-call(bf16[4,256,128]{2,1,0:T(8,128)(2,1)S(1)} %pad_maximum_fusion.1.a0, bf16[4,256,128]{2,1,0:T(8,128)(2,1)S(1)} %collective-permute-done.16.a1, bf16[4,256,128]{2,1,0:T(8,128)(2,1)S(1)} %collective-permute-done.17.a2, ...), custom_call_target="tpu_custom_call" | custom-call | tf_op jit(solution)/shard_map/project/pallas_call | solution.py:361
  85.5 0.1 collective-permute-start.19
  85.6 1.2 %collective-permute-done.19 = bf16[4,16,512]{2,1,0:T(8,128)(2,1)S(1)} collective-permute-done((bf16[4,16,512]{2,1,0:T(8,128)(2,1)S(1)}, bf16[4,16,512]{2,1,0:T(8,128)(2,1)S(1)}, u32[]{:S(2)}, u32[]{:S(2)}) %collective-permute-start.19) | collective-permute-done | bytes 65568 | tf_op jit(solution)/shard_map/ppermute | solution.py:438
  86.8 0.6 add_convert_fusion
  (5 shorter events, 0.1 us)
Async XLA Ops:
  0.0 11.6 %collective-permute-start.1 = (bf16[4,2,32,128]{3,2,1,0:T(8,128)(2,1)}, bf16[4,2,32,128]{3,2,1,0:T(8,128)(2,1)S(1)}, u32[]{:S(2)}, u32[]{:S(2)}) collective-permute-start(bf16[4,2,32,128]{3,2,1,0:T(8,128)(2,1)} %param.7), channel_id=1, source_target_pairs={{0,16},{1,17},{2,18},{3,19},{4,20},{5,21},{6,22},{7,23},{8,24},{9,... | collective-permute-start | bytes 196616 | tf_op jit(solution)/shard_map/ppermute | solution.py:68
  4.0 7.6 %collective-permute-start = (bf16[4,2,32,128]{3,2,1,0:T(8,128)(2,1)}, bf16[4,2,32,128]{3,2,1,0:T(8,128)(2,1)S(1)}, u32[]{:S(2)}, u32[]{:S(2)}) collective-permute-start(bf16[4,2,32,128]{3,2,1,0:T(8,128)(2,1)} %param.7), channel_id=1, source_target_pairs={{0,8},{1,9},{2,10},{3,11},{4,12},{5,13},{6,14},{7,15},{8,0},{9,1},... | collective-permute-start | bytes 196616 | tf_op jit(solution)/shard_map/ppermute | solution.py:68
  5.6 6.3 %collective-permute-start.2 = (bf16[4,2,32,128]{3,2,1,0:T(8,128)(2,1)}, bf16[4,2,32,128]{3,2,1,0:T(8,128)(2,1)S(1)}, u32[]{:S(2)}, u32[]{:S(2)}) collective-permute-start(bf16[4,2,32,128]{3,2,1,0:T(8,128)(2,1)} %param.7), channel_id=1, source_target_pairs={{0,24},{1,25},{2,26},{3,27},{4,28},{5,29},{6,30},{7,31},{8,16},{9,... | collective-permute-start | bytes 196616 | tf_op jit(solution)/shard_map/ppermute | solution.py:68
  8.0 3.8 %copy-start.1 = (bf16[4,2,32,128]{3,2,1,0:T(8,128)(2,1)S(1)}, bf16[4,2,32,128]{3,2,1,0:T(8,128)(2,1)}, u32[]{:S(2)}) copy-start(bf16[4,2,32,128]{3,2,1,0:T(8,128)(2,1)} %param.7) | copy-start | bytes 196612
  11.9 9.2 %collective-permute-start.3 = (bf16[4,4,2,32,128]{4,3,2,1,0:T(8,128)(2,1)S(1)}, bf16[4,4,2,32,128]{4,3,2,1,0:T(8,128)(2,1)S(1)}, u32[]{:S(2)}, u32[]{:S(2)}) collective-permute-start(bf16[4,4,2,32,128]{4,3,2,1,0:T(8,128)(2,1)S(1)} %pad_maximum_fusion.qa), channel_id=1, source_target_pairs={{0,2},{1,5},{2,0},{3,7},{4,6},{5,1},{6,4},{7,3},{8,10},{9,13},{10,... | collective-permute-start | bytes 786440 | tf_op jit(solution)/shard_map/ppermute | solution.py:68
  13.5 18.7 %collective-permute-start.5 = (bf16[4,4,2,32,128]{4,3,2,1,0:T(8,128)(2,1)S(1)}, bf16[4,4,2,32,128]{4,3,2,1,0:T(8,128)(2,1)S(1)}, u32[]{:S(2)}, u32[]{:S(2)}) collective-permute-start(bf16[4,4,2,32,128]{4,3,2,1,0:T(8,128)(2,1)S(1)} %pad_maximum_fusion.qa), channel_id=1, source_target_pairs={{0,4},{1,3},{2,6},{3,1},{4,0},{5,7},{6,2},{7,5},{8,12},{9,11},{10,... | collective-permute-start | bytes 786440 | tf_op jit(solution)/shard_map/ppermute | solution.py:68
  21.1 11.1 %collective-permute-start.6 = (bf16[4,4,2,32,128]{4,3,2,1,0:T(8,128)(2,1)S(1)}, bf16[4,4,2,32,128]{4,3,2,1,0:T(8,128)(2,1)S(1)}, u32[]{:S(2)}, u32[]{:S(2)}) collective-permute-start(bf16[4,4,2,32,128]{4,3,2,1,0:T(8,128)(2,1)S(1)} %collective-permute-done.3.qb), channel_id=1, source_target_pairs={{0,4},{1,3},{2,6},{3,1},{4,0},{5,7},{6,2},{7,5},{8,12},{9,11},{10,... | collective-permute-start | bytes 786440 | tf_op jit(solution)/shard_map/ppermute | solution.py:68
  32.1 13.0 %collective-permute-start.4 = (bf16[1056,128]{1,0:T(8,128)(2,1)S(1)}, bf16[1056,128]{1,0:T(8,128)(2,1)S(1)}, u32[]{:S(2)}, u32[]{:S(2)}) collective-permute-start(bf16[1056,128]{1,0:T(8,128)(2,1)S(1)} %get-tuple-element.34), channel_id=1, source_target_pairs={{0,2},{1,5},{2,0},{3,7},{4,6},{5,1},{6,4},{7,3},{8,10},{9,13},{10,... | collective-permute-start | bytes 811016 | tf_op jit(solution)/shard_map/ppermute | solution.py:68
  38.1 7.1 %collective-permute-start.7 = (bf16[1056,128]{1,0:T(8,128)(2,1)S(1)}, bf16[1056,128]{1,0:T(8,128)(2,1)S(1)}, u32[]{:S(2)}, u32[]{:S(2)}) collective-permute-start(bf16[1056,128]{1,0:T(8,128)(2,1)S(1)} %attention.5), channel_id=1, source_target_pairs={{0,2},{1,5},{2,0},{3,7},{4,6},{5,1},{6,4},{7,3},{8,10},{9,13},{10,... | collective-permute-start | bytes 811016 | tf_op jit(solution)/shard_map/ppermute | solution.py:68
  39.2 45.4 %copy-start = (bf16[4096,512]{1,0:T(8,128)(2,1)S(1)}, bf16[4096,512]{1,0:T(8,128)(2,1)}, u32[]{:S(2)}) copy-start(bf16[4096,512]{1,0:T(8,128)(2,1)} %weight.1) | copy-start | bytes 12582916
  45.2 5.1 %collective-permute-start.9 = (bf16[528,128]{1,0:T(8,128)(2,1)S(1)}, bf16[528,128]{1,0:T(8,128)(2,1)S(1)}, u32[]{:S(2)}, u32[]{:S(2)}) collective-permute-start(bf16[528,128]{1,0:T(8,128)(2,1)S(1)} %merge.7), channel_id=1, source_target_pairs={{0,4},{1,3},{2,6},{3,1},{4,0},{5,7},{6,2},{7,5},{8,12},{9,11},{10,... | collective-permute-start | bytes 405512 | tf_op jit(solution)/shard_map/ppermute | solution.py:68
  45.3 6.4 %collective-permute-start.8 = (bf16[528,128]{1,0:T(8,128)(2,1)S(1)}, bf16[528,128]{1,0:T(8,128)(2,1)S(1)}, u32[]{:S(2)}, u32[]{:S(2)}) collective-permute-start(bf16[528,128]{1,0:T(8,128)(2,1)S(1)} %merge.5), channel_id=1, source_target_pairs={{0,4},{1,3},{2,6},{3,1},{4,0},{5,7},{6,2},{7,5},{8,12},{9,11},{10,... | collective-permute-start | bytes 405512 | tf_op jit(solution)/shard_map/ppermute | solution.py:68
  51.9 5.2 %collective-permute-start.10 = (bf16[272,128]{1,0:T(8,128)(2,1)S(1)}, bf16[272,128]{1,0:T(8,128)(2,1)S(1)}, u32[]{:S(2)}, u32[]{:S(2)}) collective-permute-start(bf16[272,128]{1,0:T(8,128)(2,1)S(1)} %get-tuple-element.36), channel_id=1, source_target_pairs={{0,8},{1,9},{2,10},{3,11},{4,12},{5,13},{6,14},{7,15},{8,0},{9,1},... | collective-permute-start | bytes 208904 | tf_op jit(solution)/shard_map/ppermute | solution.py:68
  53.9 6.4 %collective-permute-start.11 = (bf16[272,128]{1,0:T(8,128)(2,1)S(1)}, bf16[272,128]{1,0:T(8,128)(2,1)S(1)}, u32[]{:S(2)}, u32[]{:S(2)}) collective-permute-start(bf16[272,128]{1,0:T(8,128)(2,1)S(1)} %get-tuple-element.37), channel_id=1, source_target_pairs={{0,16},{1,17},{2,18},{3,19},{4,20},{5,21},{6,22},{7,23},{8,24},{9,... | collective-permute-start | bytes 208904 | tf_op jit(solution)/shard_map/ppermute | solution.py:68
  57.1 6.9 %collective-permute-start.12 = (bf16[272,128]{1,0:T(8,128)(2,1)S(1)}, bf16[272,128]{1,0:T(8,128)(2,1)S(1)}, u32[]{:S(2)}, u32[]{:S(2)}) collective-permute-start(bf16[272,128]{1,0:T(8,128)(2,1)S(1)} %get-tuple-element.38), channel_id=1, source_target_pairs={{0,24},{1,25},{2,26},{3,27},{4,28},{5,29},{6,30},{7,31},{8,16},{9,... | collective-permute-start | bytes 208904 | tf_op jit(solution)/shard_map/ppermute | solution.py:68
  64.1 6.2 %collective-permute-start.15 = (bf16[256,128]{1,0:T(8,128)(2,1)S(1)}, bf16[256,128]{1,0:T(8,128)(2,1)S(1)}, u32[]{:S(2)}, u32[]{:S(2)}) collective-permute-start(bf16[256,128]{1,0:T(8,128)(2,1)S(1)} %finish.1), channel_id=1, source_target_pairs={{0,24},{1,25},{2,26},{3,27},{4,28},{5,29},{6,30},{7,31},{8,16},{9,... | collective-permute-start | bytes 196616 | tf_op jit(solution)/shard_map/ppermute | solution.py:68
  65.5 6.2 %collective-permute-start.14 = (bf16[256,128]{1,0:T(8,128)(2,1)S(1)}, bf16[256,128]{1,0:T(8,128)(2,1)S(1)}, u32[]{:S(2)}, u32[]{:S(2)}) collective-permute-start(bf16[256,128]{1,0:T(8,128)(2,1)S(1)} %finish.1), channel_id=1, source_target_pairs={{0,16},{1,17},{2,18},{3,19},{4,20},{5,21},{6,22},{7,23},{8,24},{9,... | collective-permute-start | bytes 196616 | tf_op jit(solution)/shard_map/ppermute | solution.py:68
  65.8 5.9 %collective-permute-start.13 = (bf16[256,128]{1,0:T(8,128)(2,1)S(1)}, bf16[256,128]{1,0:T(8,128)(2,1)S(1)}, u32[]{:S(2)}, u32[]{:S(2)}) collective-permute-start(bf16[256,128]{1,0:T(8,128)(2,1)S(1)} %finish.1), channel_id=1, source_target_pairs={{0,8},{1,9},{2,10},{3,11},{4,12},{5,13},{6,14},{7,15},{8,0},{9,1},... | collective-permute-start | bytes 196616 | tf_op jit(solution)/shard_map/ppermute | solution.py:68
  71.7 6.4 %collective-permute-start.16 = (bf16[4,256,128]{2,1,0:T(8,128)(2,1)S(1)}, bf16[4,256,128]{2,1,0:T(8,128)(2,1)S(1)}, u32[]{:S(2)}, u32[]{:S(2)}) collective-permute-start(bf16[4,256,128]{2,1,0:T(8,128)(2,1)S(1)} %pad_maximum_fusion.1.a0), channel_id=1, source_target_pairs={{0,2},{1,5},{2,0},{3,7},{4,6},{5,1},{6,4},{7,3},{8,10},{9,13},{10,... | collective-permute-start | bytes 786440 | tf_op jit(solution)/shard_map/ppermute | solution.py:68
  72.2 6.4 %collective-permute-start.17 = (bf16[4,256,128]{2,1,0:T(8,128)(2,1)S(1)}, bf16[4,256,128]{2,1,0:T(8,128)(2,1)S(1)}, u32[]{:S(2)}, u32[]{:S(2)}) collective-permute-start(bf16[4,256,128]{2,1,0:T(8,128)(2,1)S(1)} %pad_maximum_fusion.1.a0), channel_id=1, source_target_pairs={{0,4},{1,3},{2,6},{3,1},{4,0},{5,7},{6,2},{7,5},{8,12},{9,11},{10,... | collective-permute-start | bytes 786440 | tf_op jit(solution)/shard_map/ppermute | solution.py:68
  78.2 6.4 %collective-permute-start.18 = (bf16[4,256,128]{2,1,0:T(8,128)(2,1)S(1)}, bf16[4,256,128]{2,1,0:T(8,128)(2,1)S(1)}, u32[]{:S(2)}, u32[]{:S(2)}) collective-permute-start(bf16[4,256,128]{2,1,0:T(8,128)(2,1)S(1)} %collective-permute-done.16.a1), channel_id=1, source_target_pairs={{0,4},{1,3},{2,6},{3,1},{4,0},{5,7},{6,2},{7,5},{8,12},{9,11},{10,... | collective-permute-start | bytes 786440 | tf_op jit(solution)/shard_map/ppermute | solution.py:68
  85.5 1.3 %collective-permute-start.19 = (bf16[4,16,512]{2,1,0:T(8,128)(2,1)S(1)}, bf16[4,16,512]{2,1,0:T(8,128)(2,1)S(1)}, u32[]{:S(2)}, u32[]{:S(2)}) collective-permute-start(bf16[4,16,512]{2,1,0:T(8,128)(2,1)S(1)} %get-tuple-element.40), channel_id=1, source_target_pairs={{0,1},{1,0},{2,3},{3,2},{4,5},{5,4},{6,7},{7,6},{8,9},{9,8},{10,11... | collective-permute-start | bytes 196616 | tf_op jit(solution)/shard_map/ppermute | solution.py:438

commit v3 on v2

--- a/solution.py
+++ b/solution.py
@@ -73,7 +73,7 @@
 
 
 def attention_kernel(size, second, firsts, lists, counts, qa, qb, keys, values, own_keys, own_values, *rest):
-    outs, (rows, acc, tops, sums, stats) = rest[: len(firsts)], rest[len(firsts) :]
+    outs, (rows, acc, first_scores, tops, sums, stats) = rest[: len(firsts)], rest[len(firsts) :]
     units = 2 * size.lines
     half = size.rows // 2
     chip_rows = size.toks * size.group
@@ -93,30 +93,43 @@
                     rows[other // size.cand, j, kv, chip] = jnp.concatenate(cut).astype(jnp.bfloat16)
     heads = [place(size, 0, f, s) % size.kv for f in firsts for s in range(2)]
 
-    def weighed(scores, live, before):
-        high = before
-        for s, alive in zip(scores, live):
-            top = jnp.max(s, axis=0, keepdims=True) * scale
-            top = in_bf16(top if alive is None else jnp.where(alive, top, NEGATIVE))
-            high = top if high is None else jnp.maximum(high, top)
+    def weighed(scores, live, before, own_top):
+        highs = [
+            jnp.where(alive, jnp.max(s.reshape(-1, 8, half), axis=0) * scale, NEGATIVE)
+            for s, alive in zip(scores, live)
+        ]
+        if own_top is not None:
+            highs.append(own_top)
+        high = in_bf16(jnp.max(functools.reduce(jnp.maximum, highs), axis=0, keepdims=True))
+        fade = None
+        if before is not None:
+            high = jnp.maximum(before, high)
+            fade = jnp.exp2(before - high)
         weights, total = [], None
         for s, alive in zip(scores, live):
-            shift = high if alive is None else jnp.where(alive, high, POSITIVE)
-            p = jnp.exp2(s * scale - shift)
-            part = jnp.sum(p, axis=0, keepdims=True)
+            p = jnp.exp2(s * scale - jnp.where(alive, high, POSITIVE))
+            part = jnp.sum(p.reshape(-1, 8, half), axis=0)
             total = part if total is None else total + part
             weights.append(p.astype(jnp.bfloat16))
-        return high, weights, total
+        return high, weights, total, fade
 
     def blocks_of(j, head, q, g):
         slots = [g * GROUP + b for b in range(GROUP)]
         live = [slot < counts[j] for slot in slots]
         blocks = [lists[j, slot] for slot in slots]
-        scores = [
-            lax.dot_general(keys[head, block], q, NT, preferred_element_type=jnp.float32)
-            for block in blocks
-        ]
+        scores = lax.dot_general(
+            jnp.concatenate([keys[head, block] for block in blocks]),
+            q,
+            NT,
+            preferred_element_type=jnp.float32,
+        )
+        scores = [scores[b * size.block_tokens : (b + 1) * size.block_tokens] for b in range(GROUP)]
         return scores, live, [values[head, block] for block in blocks]
+
+    def gathered_values(cut, weights):
+        return lax.dot_general(
+            jnp.concatenate(cut), jnp.concatenate(weights), TN, preferred_element_type=jnp.float32
+        )
 
     def part(group, carry):
         lane = lax.broadcasted_iota(jnp.int32, (OWN_ROWS, half), 1)
@@ -129,37 +142,37 @@
         for j in range(size.cand):
             for h, head in enumerate(heads):
                 q = rows[group, j, head].reshape(half, size.width)
-                s = lax.dot_general(
-                    own_keys[j, head], q, NT, preferred_element_type=jnp.float32
-                )
-                scores, live, cut = blocks_of(j, head, q, 0)
-                s = jnp.where(seen, s, NEGATIVE)
-                scores, live, cut = [s] + scores, [None] + live, [own_values[j, head]] + cut
-                high, weights, total = weighed(scores, live, None)
-                none = high <= 0.5 * NEGATIVE * scale
-                weights[0] = jnp.where(none, 0.0, weights[0].astype(jnp.float32)).astype(jnp.bfloat16)
-                total = jnp.where(none, 0.0, total)
-                acc[j, h] = lax.dot_general(
-                    jnp.concatenate(cut), jnp.concatenate(weights), TN, preferred_element_type=jnp.float32
-                )
-                tops[j, h] = jnp.broadcast_to(high, (8, half))
-                sums[j, h] = jnp.broadcast_to(total, (8, half))
+                s = lax.dot_general(own_keys[j, head], q, NT, preferred_element_type=jnp.float32)
+                first_scores[j, h] = jnp.where(seen, s * scale, NEGATIVE)
+
+        work = [(j, h) for j in range(size.cand) for h in range(len(heads))]
+        found = []
+        for j, h in work:
+            q = rows[group, j, heads[h]].reshape(half, size.width)
+            found.append(blocks_of(j, heads[h], q, 0))
+        for (j, h), (scores, live, cut) in zip(work, found):
+            own_scores = first_scores[j, h]
+            own_top = jnp.max(own_scores.reshape(-1, 8, half), axis=0)
+            high, weights, total, _ = weighed(scores, live, None, own_top)
+            p = jnp.where(seen, jnp.exp2(own_scores - high), 0.0)
+            total = total + jnp.sum(p.reshape(-1, 8, half), axis=0)
+            acc[j, h] = gathered_values(
+                cut + [own_values[j, heads[h]]], weights + [p.astype(jnp.bfloat16)]
+            )
+            tops[j, h] = jnp.broadcast_to(high, (8, half))
+            sums[j, h] = total
 
         def more(j, carry):
             def over(g, carry):
-                for h, head in enumerate(heads):
+                found = []
+                for head in heads:
                     q = rows[group, j, head].reshape(half, size.width)
-                    scores, live, cut = blocks_of(j, head, q, g)
+                    found.append(blocks_of(j, head, q, g))
+                for h, (scores, live, cut) in enumerate(found):
                     before = tops[j, h, 0:1]
-                    high, weights, total = weighed(scores, live, before)
-                    fade = jnp.exp2(before - high)
-                    acc[j, h] = acc[j, h] * fade + lax.dot_general(
-                        jnp.concatenate(cut),
-                        jnp.concatenate(weights),
-                        TN,
-                        preferred_element_type=jnp.float32,
-                    )
-                    sums[j, h] = jnp.broadcast_to(sums[j, h, 0:1] * fade + total, (8, half))
+                    high, weights, total, fade = weighed(scores, live, before, None)
+                    acc[j, h] = acc[j, h] * fade + gathered_values(cut, weights)
+                    sums[j, h] = sums[j, h] * fade + total
                     tops[j, h] = jnp.broadcast_to(high, (8, half))
                 return carry
 
@@ -171,7 +184,7 @@
                 out, unit = outs[h // 2], (h % 2) * size.lines + group * size.cand + j
                 at = pl.multiple_of(unit * size.width, size.width)
                 out[pl.ds(at, size.width), :] = acc[j, h].astype(jnp.bfloat16)
-                l = sums[j, h, 0:1]
+                l = jnp.sum(sums[j, h], axis=0, keepdims=True)
                 rounded = in_bf16(l)
                 stats[h // 2, pl.ds(unit, 1), :] = tops[j, h, 0:1]
                 stats[h // 2, pl.ds(units + unit, 1), :] = rounded
@@ -200,6 +213,7 @@
                 jnp.bfloat16,
             ),
             pltpu.VMEM((size.cand, count, size.width, half), jnp.float32),
+            pltpu.VMEM((size.cand, count, OWN_ROWS, half), jnp.float32),
             pltpu.VMEM((size.cand, count, 8, half), jnp.float32),
             pltpu.VMEM((size.cand, count, 8, half), jnp.float32),
             pltpu.VMEM((len(firsts), stat_rows(units), half), jnp.float32),

time: 87.2 us -> 79.7 us (0.914)
  Pallas kernels: 24.3 us -> 10.8 us
  waiting for transfers between devices: 32.7 us -> 38.2 us
    pallas_call x3, Pallas kernels: 22.7 us -> 9.28 us  [attention_part(): pl.pallas_call(functools.partial(attention_kernel, size, second, firsts),...]
    ppermute x19, waiting for transfers between devices: 31.5 us -> 37 us  [hop(): return lax.ppermute(value, ('ctx', 'tp'), pairs)]
  transfers between devices with their start and end apart: 20 -> 20, of which waited for: 11 -> 14; matrix products, arithmetic and copies ran while one was open for 7% -> 7% of each run, Pallas kernels for 26% -> 12%
where the time goes in v3:
time: 79.7 us; the launch traced here: 79.4 us
  waiting for transfers between devices  38.2 us (48%)
  starting transfers between devices  23.5 us (29%)
  Pallas kernels  10.8 us (14%)
  local copies, waits for them, and re-layouts  4.73 us (6%)
  other arithmetic  1.92 us (2%)
    ppermute x19, waiting for transfers between devices, hop(): return lax.ppermute(value, ('ctx', 'tp'), pairs)  37 us
    ppermute x19, starting transfers between devices, hop(): return lax.ppermute(value, ('ctx', 'tp'), pairs)  23.5 us
    pallas_call x3, Pallas kernels, attention_part(): pl.pallas_call(functools.partial(attention_kernel, size, second, firsts),...  9.28 us
    transpose x1, local copies, waits for them, and re-layouts, on_device(): values = jnp.transpose(cached_prompt_values, (2, 0, 1, 3))  3.28 us
  transfers between devices with their start and end apart: 20, of which 14 were waited for; matrix products, arithmetic and copies ran while one was open for 7% of the time, Pallas kernels for 12%

profile of v3, /device:TPU:0, one launch (start us, length us, event | category | flops | bytes accessed | tf_op | source)
XLA Modules:
  0.0 79.4 jit_solution(4650933521466611212)
XLA Ops:
  0.0 4.0 %collective-permute-start.1 = (bf16[4,2,32,128]{3,2,1,0:T(8,128)(2,1)}, bf16[4,2,32,128]{3,2,1,0:T(8,128)(2,1)S(1)}, u32[]{:S(2)}, u32[]{:S(2)}) collective-permute-start(bf16[4,2,32,128]{3,2,1,0:T(8,128)(2,1)} %param.7), channel_id=1, source_target_pairs={{0,16},{1,17},{2,18},{3,19},{4,20},{5,21},{6,22},{7,23},{8,24},{9,... | collective-permute-start | bytes 196616 | tf_op jit(solution)/shard_map/ppermute | solution.py:68
  4.0 1.6 %collective-permute-start = (bf16[4,2,32,128]{3,2,1,0:T(8,128)(2,1)}, bf16[4,2,32,128]{3,2,1,0:T(8,128)(2,1)S(1)}, u32[]{:S(2)}, u32[]{:S(2)}) collective-permute-start(bf16[4,2,32,128]{3,2,1,0:T(8,128)(2,1)} %param.7), channel_id=1, source_target_pairs={{0,8},{1,9},{2,10},{3,11},{4,12},{5,13},{6,14},{7,15},{8,0},{9,1},... | collective-permute-start | bytes 196616 | tf_op jit(solution)/shard_map/ppermute | solution.py:68
  5.6 0.0 collective-permute-start.2
  5.6 0.8 %convert_reduce_fusion = (s32[4]{0:T(128)S(1)}, s32[4]{0:T(128)S(1)}, s32[4,128]{1,0:T(4,128)S(1)}) fusion(s32[4,128]{1,0:T(4,128)} %param.12, s32[]{:T(128)S(6)} %mul.3), kind=kLoop, calls=%fused_computation.10 | loop fusion | flops 3576 | bytes 4132 | tf_op jit(solution)/shard_map/reduce_sum | solution.py:404
  6.4 0.1 iota_add_fusion
  6.5 0.1 iota_compare_fusion.1
  6.6 0.7 copy.21
  7.3 0.7 copy.20
  8.0 0.0 copy-start.1
  8.1 3.3 %copy_bitcast_fusion = (bf16[4,16,128,128]{3,2,1,0:T(8,128)(2,1)S(1)}, bf16[4,16,128,128]{3,2,1,0:T(8,128)(2,1)S(1)}) fusion(bf16[16,128,4,128]{3,2,1,0:T(4,128)(2,1)} %param.11, bf16[16,128,4,128]{3,2,1,0:T(4,128)(2,1)} %param.10), kind=kLoop, calls=%fused_computation | loop fusion | bytes 8388608 | tf_op jit(solution)/shard_map/transpose | solution.py:426
  11.4 0.2 select_reduce_fusion.lists
  11.6 0.0 collective-permute-done.1
  11.6 0.0 collective-permute-done
  11.6 0.3 collective-permute-done.2
  11.9 0.0 copy-done.1
  11.9 1.6 %collective-permute-start.3 = (bf16[4,4,2,32,128]{4,3,2,1,0:T(8,128)(2,1)S(1)}, bf16[4,4,2,32,128]{4,3,2,1,0:T(8,128)(2,1)S(1)}, u32[]{:S(2)}, u32[]{:S(2)}) collective-permute-start(bf16[4,4,2,32,128]{4,3,2,1,0:T(8,128)(2,1)S(1)} %pad_maximum_fusion.qa), channel_id=1, source_target_pairs={{0,2},{1,5},{2,0},{3,7},{4,6},{5,1},{6,4},{7,3},{8,10},{9,13},{10,... | collective-permute-start | bytes 786440 | tf_op jit(solution)/shard_map/ppermute | solution.py:68
  13.5 1.5 %collective-permute-start.5 = (bf16[4,4,2,32,128]{4,3,2,1,0:T(8,128)(2,1)S(1)}, bf16[4,4,2,32,128]{4,3,2,1,0:T(8,128)(2,1)S(1)}, u32[]{:S(2)}, u32[]{:S(2)}) collective-permute-start(bf16[4,4,2,32,128]{4,3,2,1,0:T(8,128)(2,1)S(1)} %pad_maximum_fusion.qa), channel_id=1, source_target_pairs={{0,4},{1,3},{2,6},{3,1},{4,0},{5,7},{6,2},{7,5},{8,12},{9,11},{10,... | collective-permute-start | bytes 786440 | tf_op jit(solution)/shard_map/ppermute | solution.py:68
  15.0 6.1 %collective-permute-done.3.qb = bf16[4,4,2,32,128]{4,3,2,1,0:T(8,128)(2,1)S(1)} collective-permute-done((bf16[4,4,2,32,128]{4,3,2,1,0:T(8,128)(2,1)S(1)}, bf16[4,4,2,32,128]{4,3,2,1,0:T(8,128)(2,1)S(1)}, u32[]{:S(2)}, u32[]{:S(2)}) %collective-permute-start.3) | collective-permute-done | bytes 262176 | tf_op jit(solution)/shard_map/ppermute | solution.py:68
  21.1 0.1 collective-permute-start.6
  21.2 4.1 %attention.3 = (bf16[1056,128]{1,0:T(8,128)(2,1)S(1)}, bf16[1056,128]{1,0:T(8,128)(2,1)S(1)}) custom-call(s32[4,16]{1,0:T(4,128)S(1)} %select_reduce_fusion.lists, s32[4]{0:T(128)S(1)} %sub.15.counts, bf16[4,4,2,32,128]{4,3,2,1,0:T(8,128)(2,1)S(1)} %pad_maximum_fusion.qa, bf16[4,4,2,32,128]{4,3,2,1,0:T(8,128)(2,1)S(1)} %collective-permute-done.3.qb, ...), custom_call_target="tpu_custom_call" | custom-call | tf_op jit(solution)/shard_map/attention/pallas_call | solution.py:205
  25.4 1.5 %collective-permute-start.4 = (bf16[1056,128]{1,0:T(8,128)(2,1)S(1)}, bf16[1056,128]{1,0:T(8,128)(2,1)S(1)}, u32[]{:S(2)}, u32[]{:S(2)}) collective-permute-start(bf16[1056,128]{1,0:T(8,128)(2,1)S(1)} %get-tuple-element.34), channel_id=1, source_target_pairs={{0,2},{1,5},{2,0},{3,7},{4,6},{5,1},{6,4},{7,3},{8,10},{9,13},{10,... | collective-permute-start | bytes 811016 | tf_op jit(solution)/shard_map/ppermute | solution.py:68
  26.8 0.0 collective-permute-done.5.qa
  26.8 3.4 %collective-permute-done.6.qb = bf16[4,4,2,32,128]{4,3,2,1,0:T(8,128)(2,1)S(1)} collective-permute-done((bf16[4,4,2,32,128]{4,3,2,1,0:T(8,128)(2,1)S(1)}, bf16[4,4,2,32,128]{4,3,2,1,0:T(8,128)(2,1)S(1)}, u32[]{:S(2)}, u32[]{:S(2)}) %collective-permute-start.6) | collective-permute-done | bytes 262176 | tf_op jit(solution)/shard_map/ppermute | solution.py:68
  30.2 2.6 %attention.5 = bf16[1056,128]{1,0:T(8,128)(2,1)S(1)} custom-call(s32[4,16]{1,0:T(4,128)S(1)} %select_reduce_fusion.lists, s32[4]{0:T(128)S(1)} %sub.15.counts, bf16[4,4,2,32,128]{4,3,2,1,0:T(8,128)(2,1)S(1)} %collective-permute-done.5.qa, bf16[4,4,2,32,128]{4,3,2,1,0:T(8,128)(2,1)S(1)} %collective-permute-done.6.qb, ...), custom_call_target="tpu_custom_call" | custom-call | tf_op jit(solution)/shard_map/attention/pallas_call | solution.py:205
  32.8 1.5 %collective-permute-start.7 = (bf16[1056,128]{1,0:T(8,128)(2,1)S(1)}, bf16[1056,128]{1,0:T(8,128)(2,1)S(1)}, u32[]{:S(2)}, u32[]{:S(2)}) collective-permute-start(bf16[1056,128]{1,0:T(8,128)(2,1)S(1)} %attention.5), channel_id=1, source_target_pairs={{0,2},{1,5},{2,0},{3,7},{4,6},{5,1},{6,4},{7,3},{8,10},{9,13},{10,... | collective-permute-start | bytes 811016 | tf_op jit(solution)/shard_map/ppermute | solution.py:68
  34.4 0.0 copy-start
  34.4 2.6 %attention.4.mine = bf16[1056,128]{1,0:T(8,128)(2,1)S(1)} custom-call(s32[4,16]{1,0:T(4,128)S(1)} %select_reduce_fusion.lists, s32[4]{0:T(128)S(1)} %sub.15.counts, bf16[4,4,2,32,128]{4,3,2,1,0:T(8,128)(2,1)S(1)} %collective-permute-done.5.qa, bf16[4,4,2,32,128]{4,3,2,1,0:T(8,128)(2,1)S(1)} %collective-permute-done.6.qb, ...), custom_call_target="tpu_custom_call" | custom-call | tf_op jit(solution)/shard_map/attention/pallas_call | solution.py:205
  36.9 0.0 collective-permute-done.4.theirs
  36.9 0.1 merge.7
  37.0 0.3 collective-permute-start.9
  37.3 2.9 %collective-permute-done.7.theirs = bf16[1056,128]{1,0:T(8,128)(2,1)S(1)} collective-permute-done((bf16[1056,128]{1,0:T(8,128)(2,1)S(1)}, bf16[1056,128]{1,0:T(8,128)(2,1)S(1)}, u32[]{:S(2)}, u32[]{:S(2)}) %collective-permute-start.7) | collective-permute-done | bytes 270368 | tf_op jit(solution)/shard_map/ppermute | solution.py:68
  40.2 0.1 merge.5
  40.3 0.3 collective-permute-start.8
  40.6 0.1 merge.4.near_mine
  40.7 0.1 merge.6.far_mine
  40.7 1.4 %collective-permute-done.9.far_theirs = bf16[528,128]{1,0:T(8,128)(2,1)S(1)} collective-permute-done((bf16[528,128]{1,0:T(8,128)(2,1)S(1)}, bf16[528,128]{1,0:T(8,128)(2,1)S(1)}, u32[]{:S(2)}, u32[]{:S(2)}) %collective-permute-start.9) | collective-permute-done | bytes 135200 | tf_op jit(solution)/shard_map/ppermute | solution.py:68
  42.1 3.3 %collective-permute-done.8.near_theirs = bf16[528,128]{1,0:T(8,128)(2,1)S(1)} collective-permute-done((bf16[528,128]{1,0:T(8,128)(2,1)S(1)}, bf16[528,128]{1,0:T(8,128)(2,1)S(1)}, u32[]{:S(2)}, u32[]{:S(2)}) %collective-permute-start.8) | collective-permute-done | bytes 135200 | tf_op jit(solution)/shard_map/ppermute | solution.py:68
  45.3 0.2 split.1
  45.6 0.7 collective-permute-start.10
  46.3 3.5 %collective-permute-start.11 = (bf16[272,128]{1,0:T(8,128)(2,1)S(1)}, bf16[272,128]{1,0:T(8,128)(2,1)S(1)}, u32[]{:S(2)}, u32[]{:S(2)}) collective-permute-start(bf16[272,128]{1,0:T(8,128)(2,1)S(1)} %get-tuple-element.37), channel_id=1, source_target_pairs={{0,16},{1,17},{2,18},{3,19},{4,20},{5,21},{6,22},{7,23},{8,24},{9,... | collective-permute-start | bytes 208904 | tf_op jit(solution)/shard_map/ppermute | solution.py:68
  49.7 0.3 collective-permute-start.12
  50.0 0.0 collective-permute-done.10.refs_1_
  50.0 4.7 %collective-permute-done.11.refs_2_ = bf16[272,128]{1,0:T(8,128)(2,1)S(1)} collective-permute-done((bf16[272,128]{1,0:T(8,128)(2,1)S(1)}, bf16[272,128]{1,0:T(8,128)(2,1)S(1)}, u32[]{:S(2)}, u32[]{:S(2)}) %collective-permute-start.11) | collective-permute-done | bytes 69664 | tf_op jit(solution)/shard_map/ppermute | solution.py:68
  54.7 1.2 %collective-permute-done.12.refs_3_ = bf16[272,128]{1,0:T(8,128)(2,1)S(1)} collective-permute-done((bf16[272,128]{1,0:T(8,128)(2,1)S(1)}, bf16[272,128]{1,0:T(8,128)(2,1)S(1)}, u32[]{:S(2)}, u32[]{:S(2)}) %collective-permute-start.12) | collective-permute-done | bytes 69664 | tf_op jit(solution)/shard_map/ppermute | solution.py:68
  56.0 0.2 finish.1
  56.1 1.5 %collective-permute-start.15 = (bf16[256,128]{1,0:T(8,128)(2,1)S(1)}, bf16[256,128]{1,0:T(8,128)(2,1)S(1)}, u32[]{:S(2)}, u32[]{:S(2)}) collective-permute-start(bf16[256,128]{1,0:T(8,128)(2,1)S(1)} %finish.1), channel_id=1, source_target_pairs={{0,24},{1,25},{2,26},{3,27},{4,28},{5,29},{6,30},{7,31},{8,16},{9,... | collective-permute-start | bytes 196616 | tf_op jit(solution)/shard_map/ppermute | solution.py:68
  57.6 1.0 %collective-permute-start.14 = (bf16[256,128]{1,0:T(8,128)(2,1)S(1)}, bf16[256,128]{1,0:T(8,128)(2,1)S(1)}, u32[]{:S(2)}, u32[]{:S(2)}) collective-permute-start(bf16[256,128]{1,0:T(8,128)(2,1)S(1)} %finish.1), channel_id=1, source_target_pairs={{0,16},{1,17},{2,18},{3,19},{4,20},{5,21},{6,22},{7,23},{8,24},{9,... | collective-permute-start | bytes 196616 | tf_op jit(solution)/shard_map/ppermute | solution.py:68
  58.6 1.9 %collective-permute-start.13 = (bf16[256,128]{1,0:T(8,128)(2,1)S(1)}, bf16[256,128]{1,0:T(8,128)(2,1)S(1)}, u32[]{:S(2)}, u32[]{:S(2)}) collective-permute-start(bf16[256,128]{1,0:T(8,128)(2,1)S(1)} %finish.1), channel_id=1, source_target_pairs={{0,8},{1,9},{2,10},{3,11},{4,12},{5,13},{6,14},{7,15},{8,0},{9,1},... | collective-permute-start | bytes 196616 | tf_op jit(solution)/shard_map/ppermute | solution.py:68
  60.6 1.7 %collective-permute-done.15 = bf16[256,128]{1,0:T(8,128)(2,1)S(1)} collective-permute-done((bf16[256,128]{1,0:T(8,128)(2,1)S(1)}, bf16[256,128]{1,0:T(8,128)(2,1)S(1)}, u32[]{:S(2)}, u32[]{:S(2)}) %collective-permute-start.15) | collective-permute-done | bytes 65568 | tf_op jit(solution)/shard_map/ppermute | solution.py:68
  62.3 1.4 %collective-permute-done.14 = bf16[256,128]{1,0:T(8,128)(2,1)S(1)} collective-permute-done((bf16[256,128]{1,0:T(8,128)(2,1)S(1)}, bf16[256,128]{1,0:T(8,128)(2,1)S(1)}, u32[]{:S(2)}, u32[]{:S(2)}) %collective-permute-start.14) | collective-permute-done | bytes 65568 | tf_op jit(solution)/shard_map/ppermute | solution.py:68
  63.7 0.0 collective-permute-done.13
  63.7 1.3 %collective-permute-start.16 = (bf16[4,256,128]{2,1,0:T(8,128)(2,1)S(1)}, bf16[4,256,128]{2,1,0:T(8,128)(2,1)S(1)}, u32[]{:S(2)}, u32[]{:S(2)}) collective-permute-start(bf16[4,256,128]{2,1,0:T(8,128)(2,1)S(1)} %pad_maximum_fusion.1.a0), channel_id=1, source_target_pairs={{0,2},{1,5},{2,0},{3,7},{4,6},{5,1},{6,4},{7,3},{8,10},{9,13},{10,... | collective-permute-start | bytes 786440 | tf_op jit(solution)/shard_map/ppermute | solution.py:68
  65.0 0.6 collective-permute-start.17
  65.5 4.6 %collective-permute-done.16.a1 = bf16[4,256,128]{2,1,0:T(8,128)(2,1)S(1)} collective-permute-done((bf16[4,256,128]{2,1,0:T(8,128)(2,1)S(1)}, bf16[4,256,128]{2,1,0:T(8,128)(2,1)S(1)}, u32[]{:S(2)}, u32[]{:S(2)}) %collective-permute-start.16) | collective-permute-done | bytes 262176 | tf_op jit(solution)/shard_map/ppermute | solution.py:68
  70.1 0.3 collective-permute-start.18
  70.5 0.9 %collective-permute-done.17.a2 = bf16[4,256,128]{2,1,0:T(8,128)(2,1)S(1)} collective-permute-done((bf16[4,256,128]{2,1,0:T(8,128)(2,1)S(1)}, bf16[4,256,128]{2,1,0:T(8,128)(2,1)S(1)}, u32[]{:S(2)}, u32[]{:S(2)}) %collective-permute-start.17) | collective-permute-done | bytes 262176 | tf_op jit(solution)/shard_map/ppermute | solution.py:68
  71.4 5.2 %collective-permute-done.18.a3 = bf16[4,256,128]{2,1,0:T(8,128)(2,1)S(1)} collective-permute-done((bf16[4,256,128]{2,1,0:T(8,128)(2,1)S(1)}, bf16[4,256,128]{2,1,0:T(8,128)(2,1)S(1)}, u32[]{:S(2)}, u32[]{:S(2)}) %collective-permute-start.18) | collective-permute-done | bytes 262176 | tf_op jit(solution)/shard_map/ppermute | solution.py:68
  76.5 0.0 copy-done
  76.5 0.9 %project.1 = (f32[4,16,512]{2,1,0:T(8,128)S(1)}, bf16[4,16,512]{2,1,0:T(8,128)(2,1)S(1)}) custom-call(bf16[4,256,128]{2,1,0:T(8,128)(2,1)S(1)} %pad_maximum_fusion.1.a0, bf16[4,256,128]{2,1,0:T(8,128)(2,1)S(1)} %collective-permute-done.16.a1, bf16[4,256,128]{2,1,0:T(8,128)(2,1)S(1)} %collective-permute-done.17.a2, ...), custom_call_target="tpu_custom_call" | custom-call | tf_op jit(solution)/shard_map/project/pallas_call | solution.py:375
  77.4 0.1 collective-permute-start.19
  77.5 1.2 %collective-permute-done.19 = bf16[4,16,512]{2,1,0:T(8,128)(2,1)S(1)} collective-permute-done((bf16[4,16,512]{2,1,0:T(8,128)(2,1)S(1)}, bf16[4,16,512]{2,1,0:T(8,128)(2,1)S(1)}, u32[]{:S(2)}, u32[]{:S(2)}) %collective-permute-start.19) | collective-permute-done | bytes 65568 | tf_op jit(solution)/shard_map/ppermute | solution.py:452
  78.8 0.6 add_convert_fusion
  (5 shorter events, 0.1 us)
Async XLA Ops:
  0.0 11.6 %collective-permute-start.1 = (bf16[4,2,32,128]{3,2,1,0:T(8,128)(2,1)}, bf16[4,2,32,128]{3,2,1,0:T(8,128)(2,1)S(1)}, u32[]{:S(2)}, u32[]{:S(2)}) collective-permute-start(bf16[4,2,32,128]{3,2,1,0:T(8,128)(2,1)} %param.7), channel_id=1, source_target_pairs={{0,16},{1,17},{2,18},{3,19},{4,20},{5,21},{6,22},{7,23},{8,24},{9,... | collective-permute-start | bytes 196616 | tf_op jit(solution)/shard_map/ppermute | solution.py:68
  4.0 7.6 %collective-permute-start = (bf16[4,2,32,128]{3,2,1,0:T(8,128)(2,1)}, bf16[4,2,32,128]{3,2,1,0:T(8,128)(2,1)S(1)}, u32[]{:S(2)}, u32[]{:S(2)}) collective-permute-start(bf16[4,2,32,128]{3,2,1,0:T(8,128)(2,1)} %param.7), channel_id=1, source_target_pairs={{0,8},{1,9},{2,10},{3,11},{4,12},{5,13},{6,14},{7,15},{8,0},{9,1},... | collective-permute-start | bytes 196616 | tf_op jit(solution)/shard_map/ppermute | solution.py:68
  5.6 6.3 %collective-permute-start.2 = (bf16[4,2,32,128]{3,2,1,0:T(8,128)(2,1)}, bf16[4,2,32,128]{3,2,1,0:T(8,128)(2,1)S(1)}, u32[]{:S(2)}, u32[]{:S(2)}) collective-permute-start(bf16[4,2,32,128]{3,2,1,0:T(8,128)(2,1)} %param.7), channel_id=1, source_target_pairs={{0,24},{1,25},{2,26},{3,27},{4,28},{5,29},{6,30},{7,31},{8,16},{9,... | collective-permute-start | bytes 196616 | tf_op jit(solution)/shard_map/ppermute | solution.py:68
  8.0 3.8 %copy-start.1 = (bf16[4,2,32,128]{3,2,1,0:T(8,128)(2,1)S(1)}, bf16[4,2,32,128]{3,2,1,0:T(8,128)(2,1)}, u32[]{:S(2)}) copy-start(bf16[4,2,32,128]{3,2,1,0:T(8,128)(2,1)} %param.7) | copy-start | bytes 196612
  11.9 9.2 %collective-permute-start.3 = (bf16[4,4,2,32,128]{4,3,2,1,0:T(8,128)(2,1)S(1)}, bf16[4,4,2,32,128]{4,3,2,1,0:T(8,128)(2,1)S(1)}, u32[]{:S(2)}, u32[]{:S(2)}) collective-permute-start(bf16[4,4,2,32,128]{4,3,2,1,0:T(8,128)(2,1)S(1)} %pad_maximum_fusion.qa), channel_id=1, source_target_pairs={{0,2},{1,5},{2,0},{3,7},{4,6},{5,1},{6,4},{7,3},{8,10},{9,13},{10,... | collective-permute-start | bytes 786440 | tf_op jit(solution)/shard_map/ppermute | solution.py:68
  13.5 13.4 %collective-permute-start.5 = (bf16[4,4,2,32,128]{4,3,2,1,0:T(8,128)(2,1)S(1)}, bf16[4,4,2,32,128]{4,3,2,1,0:T(8,128)(2,1)S(1)}, u32[]{:S(2)}, u32[]{:S(2)}) collective-permute-start(bf16[4,4,2,32,128]{4,3,2,1,0:T(8,128)(2,1)S(1)} %pad_maximum_fusion.qa), channel_id=1, source_target_pairs={{0,4},{1,3},{2,6},{3,1},{4,0},{5,7},{6,2},{7,5},{8,12},{9,11},{10,... | collective-permute-start | bytes 786440 | tf_op jit(solution)/shard_map/ppermute | solution.py:68
  21.1 9.1 %collective-permute-start.6 = (bf16[4,4,2,32,128]{4,3,2,1,0:T(8,128)(2,1)S(1)}, bf16[4,4,2,32,128]{4,3,2,1,0:T(8,128)(2,1)S(1)}, u32[]{:S(2)}, u32[]{:S(2)}) collective-permute-start(bf16[4,4,2,32,128]{4,3,2,1,0:T(8,128)(2,1)S(1)} %collective-permute-done.3.qb), channel_id=1, source_target_pairs={{0,4},{1,3},{2,6},{3,1},{4,0},{5,7},{6,2},{7,5},{8,12},{9,11},{10,... | collective-permute-start | bytes 786440 | tf_op jit(solution)/shard_map/ppermute | solution.py:68
  25.4 11.6 %collective-permute-start.4 = (bf16[1056,128]{1,0:T(8,128)(2,1)S(1)}, bf16[1056,128]{1,0:T(8,128)(2,1)S(1)}, u32[]{:S(2)}, u32[]{:S(2)}) collective-permute-start(bf16[1056,128]{1,0:T(8,128)(2,1)S(1)} %get-tuple-element.34), channel_id=1, source_target_pairs={{0,2},{1,5},{2,0},{3,7},{4,6},{5,1},{6,4},{7,3},{8,10},{9,13},{10,... | collective-permute-start | bytes 811016 | tf_op jit(solution)/shard_map/ppermute | solution.py:68
  32.8 7.4 %collective-permute-start.7 = (bf16[1056,128]{1,0:T(8,128)(2,1)S(1)}, bf16[1056,128]{1,0:T(8,128)(2,1)S(1)}, u32[]{:S(2)}, u32[]{:S(2)}) collective-permute-start(bf16[1056,128]{1,0:T(8,128)(2,1)S(1)} %attention.5), channel_id=1, source_target_pairs={{0,2},{1,5},{2,0},{3,7},{4,6},{5,1},{6,4},{7,3},{8,10},{9,13},{10,... | collective-permute-start | bytes 811016 | tf_op jit(solution)/shard_map/ppermute | solution.py:68
  34.4 42.2 %copy-start = (bf16[4096,512]{1,0:T(8,128)(2,1)S(1)}, bf16[4096,512]{1,0:T(8,128)(2,1)}, u32[]{:S(2)}) copy-start(bf16[4096,512]{1,0:T(8,128)(2,1)} %weight.1) | copy-start | bytes 12582916
  37.0 5.1 %collective-permute-start.9 = (bf16[528,128]{1,0:T(8,128)(2,1)S(1)}, bf16[528,128]{1,0:T(8,128)(2,1)S(1)}, u32[]{:S(2)}, u32[]{:S(2)}) collective-permute-start(bf16[528,128]{1,0:T(8,128)(2,1)S(1)} %merge.7), channel_id=1, source_target_pairs={{0,4},{1,3},{2,6},{3,1},{4,0},{5,7},{6,2},{7,5},{8,12},{9,11},{10,... | collective-permute-start | bytes 405512 | tf_op jit(solution)/shard_map/ppermute | solution.py:68
  40.3 5.1 %collective-permute-start.8 = (bf16[528,128]{1,0:T(8,128)(2,1)S(1)}, bf16[528,128]{1,0:T(8,128)(2,1)S(1)}, u32[]{:S(2)}, u32[]{:S(2)}) collective-permute-start(bf16[528,128]{1,0:T(8,128)(2,1)S(1)} %merge.5), channel_id=1, source_target_pairs={{0,4},{1,3},{2,6},{3,1},{4,0},{5,7},{6,2},{7,5},{8,12},{9,11},{10,... | collective-permute-start | bytes 405512 | tf_op jit(solution)/shard_map/ppermute | solution.py:68
  45.6 4.5 %collective-permute-start.10 = (bf16[272,128]{1,0:T(8,128)(2,1)S(1)}, bf16[272,128]{1,0:T(8,128)(2,1)S(1)}, u32[]{:S(2)}, u32[]{:S(2)}) collective-permute-start(bf16[272,128]{1,0:T(8,128)(2,1)S(1)} %get-tuple-element.36), channel_id=1, source_target_pairs={{0,8},{1,9},{2,10},{3,11},{4,12},{5,13},{6,14},{7,15},{8,0},{9,1},... | collective-permute-start | bytes 208904 | tf_op jit(solution)/shard_map/ppermute | solution.py:68
  46.3 8.5 %collective-permute-start.11 = (bf16[272,128]{1,0:T(8,128)(2,1)S(1)}, bf16[272,128]{1,0:T(8,128)(2,1)S(1)}, u32[]{:S(2)}, u32[]{:S(2)}) collective-permute-start(bf16[272,128]{1,0:T(8,128)(2,1)S(1)} %get-tuple-element.37), channel_id=1, source_target_pairs={{0,16},{1,17},{2,18},{3,19},{4,20},{5,21},{6,22},{7,23},{8,24},{9,... | collective-permute-start | bytes 208904 | tf_op jit(solution)/shard_map/ppermute | solution.py:68
  49.7 6.2 %collective-permute-start.12 = (bf16[272,128]{1,0:T(8,128)(2,1)S(1)}, bf16[272,128]{1,0:T(8,128)(2,1)S(1)}, u32[]{:S(2)}, u32[]{:S(2)}) collective-permute-start(bf16[272,128]{1,0:T(8,128)(2,1)S(1)} %get-tuple-element.38), channel_id=1, source_target_pairs={{0,24},{1,25},{2,26},{3,27},{4,28},{5,29},{6,30},{7,31},{8,16},{9,... | collective-permute-start | bytes 208904 | tf_op jit(solution)/shard_map/ppermute | solution.py:68
  56.1 6.2 %collective-permute-start.15 = (bf16[256,128]{1,0:T(8,128)(2,1)S(1)}, bf16[256,128]{1,0:T(8,128)(2,1)S(1)}, u32[]{:S(2)}, u32[]{:S(2)}) collective-permute-start(bf16[256,128]{1,0:T(8,128)(2,1)S(1)} %finish.1), channel_id=1, source_target_pairs={{0,24},{1,25},{2,26},{3,27},{4,28},{5,29},{6,30},{7,31},{8,16},{9,... | collective-permute-start | bytes 196616 | tf_op jit(solution)/shard_map/ppermute | solution.py:68
  57.6 6.1 %collective-permute-start.14 = (bf16[256,128]{1,0:T(8,128)(2,1)S(1)}, bf16[256,128]{1,0:T(8,128)(2,1)S(1)}, u32[]{:S(2)}, u32[]{:S(2)}) collective-permute-start(bf16[256,128]{1,0:T(8,128)(2,1)S(1)} %finish.1), channel_id=1, source_target_pairs={{0,16},{1,17},{2,18},{3,19},{4,20},{5,21},{6,22},{7,23},{8,24},{9,... | collective-permute-start | bytes 196616 | tf_op jit(solution)/shard_map/ppermute | solution.py:68
  58.6 5.0 %collective-permute-start.13 = (bf16[256,128]{1,0:T(8,128)(2,1)S(1)}, bf16[256,128]{1,0:T(8,128)(2,1)S(1)}, u32[]{:S(2)}, u32[]{:S(2)}) collective-permute-start(bf16[256,128]{1,0:T(8,128)(2,1)S(1)} %finish.1), channel_id=1, source_target_pairs={{0,8},{1,9},{2,10},{3,11},{4,12},{5,13},{6,14},{7,15},{8,0},{9,1},... | collective-permute-start | bytes 196616 | tf_op jit(solution)/shard_map/ppermute | solution.py:68
  63.7 6.4 %collective-permute-start.16 = (bf16[4,256,128]{2,1,0:T(8,128)(2,1)S(1)}, bf16[4,256,128]{2,1,0:T(8,128)(2,1)S(1)}, u32[]{:S(2)}, u32[]{:S(2)}) collective-permute-start(bf16[4,256,128]{2,1,0:T(8,128)(2,1)S(1)} %pad_maximum_fusion.1.a0), channel_id=1, source_target_pairs={{0,2},{1,5},{2,0},{3,7},{4,6},{5,1},{6,4},{7,3},{8,10},{9,13},{10,... | collective-permute-start | bytes 786440 | tf_op jit(solution)/shard_map/ppermute | solution.py:68
  65.0 6.4 %collective-permute-start.17 = (bf16[4,256,128]{2,1,0:T(8,128)(2,1)S(1)}, bf16[4,256,128]{2,1,0:T(8,128)(2,1)S(1)}, u32[]{:S(2)}, u32[]{:S(2)}) collective-permute-start(bf16[4,256,128]{2,1,0:T(8,128)(2,1)S(1)} %pad_maximum_fusion.1.a0), channel_id=1, source_target_pairs={{0,4},{1,3},{2,6},{3,1},{4,0},{5,7},{6,2},{7,5},{8,12},{9,11},{10,... | collective-permute-start | bytes 786440 | tf_op jit(solution)/shard_map/ppermute | solution.py:68
  70.1 6.4 %collective-permute-start.18 = (bf16[4,256,128]{2,1,0:T(8,128)(2,1)S(1)}, bf16[4,256,128]{2,1,0:T(8,128)(2,1)S(1)}, u32[]{:S(2)}, u32[]{:S(2)}) collective-permute-start(bf16[4,256,128]{2,1,0:T(8,128)(2,1)S(1)} %collective-permute-done.16.a1), channel_id=1, source_target_pairs={{0,4},{1,3},{2,6},{3,1},{4,0},{5,7},{6,2},{7,5},{8,12},{9,11},{10,... | collective-permute-start | bytes 786440 | tf_op jit(solution)/shard_map/ppermute | solution.py:68
  77.4 1.3 %collective-permute-start.19 = (bf16[4,16,512]{2,1,0:T(8,128)(2,1)S(1)}, bf16[4,16,512]{2,1,0:T(8,128)(2,1)S(1)}, u32[]{:S(2)}, u32[]{:S(2)}) collective-permute-start(bf16[4,16,512]{2,1,0:T(8,128)(2,1)S(1)} %get-tuple-element.40), channel_id=1, source_target_pairs={{0,1},{1,0},{2,3},{3,2},{4,5},{5,4},{6,7},{7,6},{8,9},{9,8},{10,11... | collective-permute-start | bytes 196616 | tf_op jit(solution)/shard_map/ppermute | solution.py:452

commit v4 on v3

--- a/solution.py
+++ b/solution.py
@@ -62,6 +62,8 @@
                 other = c ^ (1 + core)
             elif stage == "second":
                 other = c ^ (2 - core)
+            elif stage == "both":
+                other = c ^ 3
             else:
                 other = c ^ (stage * size.kv)
             pairs.append((c * cores + core, other * cores + core))
@@ -72,16 +74,16 @@
     return jnp.stack([value] + [hop(size, value, k) for k in range(1, size.lines)])
 
 
-def attention_kernel(size, second, firsts, lists, counts, qa, qb, keys, values, own_keys, own_values, *rest):
-    outs, (rows, acc, first_scores, tops, sums, stats) = rest[: len(firsts)], rest[len(firsts) :]
-    units = 2 * size.lines
+def attention_kernel(size, far, places, lists, counts, qa, qb, keys, values, own_keys, own_values, *rest):
+    outs, (rows, acc, first_scores, tops, sums, stats) = rest[: len(places)], rest[len(places) :]
+    units = size.lines
     half = size.rows // 2
     chip_rows = size.toks * size.group
     scale = size.width ** (-0.5) * math.log2(math.e)
     me, core = lax.axis_index("ctx"), lax.axis_index("tp")
     here, spot = me // size.kv, me % size.kv
     a_here = (spot >> core) & 1
-    b_side = ((spot >> (1 - core)) & 1) ^ second
+    b_side = ((spot >> (1 - core)) & 1) ^ far
     for first, ref in enumerate((qa, qb)):
         for line in range(size.lines):
             other = here ^ line
@@ -91,7 +93,7 @@
                 for kv in range(size.kv):
                     cut = [p[kv * size.group : (kv + 1) * size.group] for p in parts]
                     rows[other // size.cand, j, kv, chip] = jnp.concatenate(cut).astype(jnp.bfloat16)
-    heads = [place(size, 0, f, s) % size.kv for f in firsts for s in range(2)]
+    heads = [place(size, 0, *at) % size.kv for at in places]
 
     def weighed(scores, live, before, own_top):
         highs = [
@@ -181,14 +183,14 @@
         lax.fori_loop(0, size.cand, more, 0)
         for j in range(size.cand):
             for h in range(len(heads)):
-                out, unit = outs[h // 2], (h % 2) * size.lines + group * size.cand + j
+                out, unit = outs[h], group * size.cand + j
                 at = pl.multiple_of(unit * size.width, size.width)
                 out[pl.ds(at, size.width), :] = acc[j, h].astype(jnp.bfloat16)
                 l = jnp.sum(sums[j, h], axis=0, keepdims=True)
                 rounded = in_bf16(l)
-                stats[h // 2, pl.ds(unit, 1), :] = tops[j, h, 0:1]
-                stats[h // 2, pl.ds(units + unit, 1), :] = rounded
-                stats[h // 2, pl.ds(2 * units + unit, 1), :] = l - rounded
+                stats[h, pl.ds(unit, 1), :] = tops[j, h, 0:1]
+                stats[h, pl.ds(units + unit, 1), :] = rounded
+                stats[h, pl.ds(2 * units + unit, 1), :] = l - rounded
         return carry
 
     stats[...] = jnp.zeros_like(stats)
@@ -197,16 +199,16 @@
         out[pl.ds(units * size.width, stat_rows(units)), :] = stats[f].astype(jnp.bfloat16)
 
 
-def attention_part(size, second, firsts, lists, counts, qa, qb, keys, values, own_keys, own_values):
-    units, half = 2 * size.lines, size.rows // 2
+def attention_part(size, far, places, lists, counts, qa, qb, keys, values, own_keys, own_values):
+    units, half = size.lines, size.rows // 2
     length = units * size.width + stat_rows(units)
-    count = 2 * len(firsts)
+    count = len(places)
     chips = size.n // size.row_groups // 2
     return pl.pallas_call(
-        functools.partial(attention_kernel, size, second, firsts),
-        out_shape=[jax.ShapeDtypeStruct((length, half), jnp.bfloat16)] * len(firsts),
+        functools.partial(attention_kernel, size, far, places),
+        out_shape=[jax.ShapeDtypeStruct((length, half), jnp.bfloat16)] * count,
         in_specs=[whole(pltpu.SMEM)] * 2 + [whole()] * 6,
-        out_specs=[whole()] * len(firsts),
+        out_specs=[whole()] * count,
         scratch_shapes=[
             pltpu.VMEM(
                 (size.row_groups, size.cand, size.kv, chips, size.toks * size.group, size.width),
@@ -216,16 +218,16 @@
             pltpu.VMEM((size.cand, count, OWN_ROWS, half), jnp.float32),
             pltpu.VMEM((size.cand, count, 8, half), jnp.float32),
             pltpu.VMEM((size.cand, count, 8, half), jnp.float32),
-            pltpu.VMEM((len(firsts), stat_rows(units), half), jnp.float32),
+            pltpu.VMEM((count, stat_rows(units), half), jnp.float32),
         ],
         compiler_params=pltpu.CompilerParams(vmem_limit_bytes=LIMIT),
         name="attention",
     )(lists, counts, qa, qb, keys, values, own_keys, own_values)
 
 
-def merge_units(size, parts, firsts, stats_at, unit_lists, units_of):
+def merge_units(size, parts, at, units, unit):
     stats = []
-    for ref, at, units, unit in zip(parts, stats_at, units_of, unit_lists):
+    for ref in parts:
         block = ref[pl.ds(at, stat_rows(units)), :].astype(jnp.float32)
         m = block[unit : unit + 1]
         l = block[units + unit : units + unit + 1] + block[2 * units + unit : 2 * units + unit + 1]
@@ -234,56 +236,22 @@
     fades = [jnp.exp2(m - high) for m, _ in stats]
     total = functools.reduce(jnp.add, [l * f for (_, l), f in zip(stats, fades)])
     sums = None
-    for ref, unit, fade in zip(parts, unit_lists, fades):
+    for ref, fade in zip(parts, fades):
         value = ref[pl.ds(unit * size.width, size.width), :].astype(jnp.float32) * fade
         sums = value if sums is None else sums + value
     return sums, high, total
 
 
-def merge_pair(size, mine, theirs, unit, units):
-    at = units * size.width
-    return merge_units(size, (mine, theirs), (0, 0), (at, at), (unit, unit), (units, units))
-
-
-def merge_kernel(size, start, units, units_in, mine, theirs, out):
-    highs, totals = [], []
-    for unit in range(units):
-        sums, high, total = merge_pair(size, mine, theirs, start + unit, units_in)
-        out[pl.ds(unit * size.width, size.width), :] = sums.astype(jnp.bfloat16)
-        highs.append(high)
-        totals.append(total)
-    lengths = [in_bf16(t) for t in totals]
-    rows = highs + lengths + [t - l for t, l in zip(totals, lengths)]
-    left = stat_rows(units) - len(rows)
-    if left:
-        rows.append(jnp.zeros((left, mine.shape[1]), jnp.float32))
-    out[pl.ds(units * size.width, stat_rows(units)), :] = jnp.concatenate(rows).astype(jnp.bfloat16)
-
-
-def merge(size, start, units, units_in, mine, theirs):
-    length = units * size.width + stat_rows(units)
-    return pl.pallas_call(
-        functools.partial(merge_kernel, size, start, units, units_in),
-        out_shape=jax.ShapeDtypeStruct((length, mine.shape[1]), jnp.bfloat16),
-        in_specs=[whole()] * 2,
-        out_specs=whole(),
-        compiler_params=pltpu.CompilerParams(vmem_limit_bytes=LIMIT),
-        name="merge",
-    )(mine, theirs)
-
-
-def split_kernel(size, near_mine, near_theirs, far_mine, far_theirs, *outs):
+def split_kernel(size, count, *refs):
+    near, far, outs = refs[:count], refs[count : 2 * count], refs[2 * count :]
     here = lax.axis_index("ctx") // size.kv
     lines, width = size.lines, size.width
     for unit in range(lines):
-        merged = [
-            merge_pair(size, near_mine, near_theirs, unit, lines),
-            merge_pair(size, far_mine, far_theirs, unit, lines),
-        ]
+        merged = [merge_units(size, side, lines * width, lines, unit) for side in (near, far)]
         lengths = [in_bf16(total) for _, _, total in merged]
         tail = [high for _, high, _ in merged] + lengths
         tail += [total - length for (_, _, total), length in zip(merged, lengths)]
-        tail.append(jnp.zeros((stat_rows(2) - len(tail), near_mine.shape[1]), jnp.float32))
+        tail.append(jnp.zeros((stat_rows(2) - len(tail), near[0].shape[1]), jnp.float32))
         tail = jnp.concatenate(tail).astype(jnp.bfloat16)
         bodies = [sums.astype(jnp.bfloat16) for sums, _, _ in merged]
         for line, out in enumerate(outs):
@@ -295,29 +263,25 @@
                 out[2 * width :, :] = tail
 
 
-def split_merge(size, near_mine, near_theirs, far_mine, far_theirs):
+def split_merge(size, near, far):
     shape = jax.ShapeDtypeStruct((2 * size.width + stat_rows(2), size.rows // 2), jnp.bfloat16)
     return pl.pallas_call(
-        functools.partial(split_kernel, size),
+        functools.partial(split_kernel, size, len(near)),
         out_shape=[shape] * size.lines,
-        in_specs=[whole()] * 4,
+        in_specs=[whole()] * (2 * len(near)),
         out_specs=[whole()] * size.lines,
         compiler_params=pltpu.CompilerParams(vmem_limit_bytes=LIMIT),
         name="split",
-    )(near_mine, near_theirs, far_mine, far_theirs)
+    )(*near, *far)
 
 
 def finish_kernel(size, *refs):
     parts, out, turned = refs[:-2], refs[-2], refs[-1]
-    count = len(parts)
     chip_rows = size.toks * size.group
     spot, core = lax.axis_index("ctx") % size.kv, lax.axis_index("tp")
     b_here = (spot >> (1 - core)) & 1
     for side in range(2):
-        at = 2 * size.width
-        sums, _, total = merge_units(
-            size, parts, (0,) * count, (at,) * count, (side,) * count, (2,) * count
-        )
+        sums, _, total = merge_units(size, parts, 2 * size.width, 2, side)
         half = (sums / total).T
         for chip in range(size.n // size.row_groups // 2):
             absolute = chip // 2 * size.kv + ((chip % 2) << core) + ((b_here ^ side) << (1 - core))
@@ -393,7 +357,7 @@
     a0 = gather_lines(size, value)
     a1 = hop(size, a0, "first")
     a2 = hop(size, a0, "second")
-    a3 = hop(size, a1, "second")
+    a3 = hop(size, a0, "both")
     return a0, a1, a2, a3
 
 
@@ -429,22 +393,21 @@
     own_values = jnp.pad(jnp.transpose(candidate_values, (0, 2, 1, 3)), room)
     moved = [queries] + [hop(size, queries, k) for k in range(1, size.lines)]
     ready = (lists, counts, keys, values, own_keys, own_values)
-    moved, ready = lax.optimization_barrier((moved, ready))
-    lists, counts, keys, values, own_keys, own_values = ready
+    moved, (lists, counts, keys, values, own_keys, own_values) = lax.optimization_barrier((moved, ready))
     q0 = jnp.stack(moved)
     q1, q2 = hop(size, q0, "first"), hop(size, q0, "second")
     q3 = hop(size, q1, "second")
-    lines, units = size.lines, 2 * size.lines
-    near_away, near = attention_part(size, 0, (1, 0), lists, counts, q0, q1, *ready[2:])
-    near_away = hop(size, near_away, "first")
-    (far_away,) = attention_part(size, 1, (1,), lists, counts, q2, q3, *ready[2:])
-    far_away = hop(size, far_away, "first")
-    (far,) = attention_part(size, 1, (0,), lists, counts, q2, q3, *ready[2:])
-    near_leaves = hop(size, merge(size, lines, lines, units, near, near_away), "second")
-    near_stays = merge(size, 0, lines, units, near, near_away)
-    far_leaves = hop(size, merge(size, lines, lines, units, far, far_away), "second")
-    far_stays = merge(size, 0, lines, units, far, far_away)
-    parts = split_merge(size, near_stays, far_leaves, far_stays, near_leaves)
+    shared = (keys, values, own_keys, own_values)
+    lines = size.lines
+    near_a, near_ab, near_b, near = attention_part(
+        size, 0, ((1, 0), (1, 1), (0, 1), (0, 0)), lists, counts, q0, q1, *shared
+    )
+    near_a, near_ab, near_b = hop(size, near_a, "first"), hop(size, near_ab, "both"), hop(size, near_b, "second")
+    far_a, far_ab = attention_part(size, 1, ((1, 0), (1, 1)), lists, counts, q2, q3, *shared)
+    far_a, far_ab = hop(size, far_a, "first"), hop(size, far_ab, "both")
+    far_b, far = attention_part(size, 1, ((0, 1), (0, 0)), lists, counts, q2, q3, *shared)
+    far_b = hop(size, far_b, "second")
+    parts = split_merge(size, (near, near_a, far_b, far_ab), (far, far_a, near_b, near_ab))
     parts = [parts[0]] + [hop(size, parts[k], k) for k in range(1, lines)]
     attention = finish(size, parts)
     kept, sent = project(size, gather_all(size, attention), out_weight)

time: 79.7 us -> 76.2 us (0.956)
  waiting for transfers between devices: 38.2 us -> 27.9 us
  starting transfers between devices: 23.5 us -> 29.7 us
    ppermute x19 -> x21, waiting for transfers between devices: 37 us -> 26.7 us  [hop(): return lax.ppermute(value, ('ctx', 'tp'), pairs)]
    ppermute x19 -> x21, starting transfers between devices: 23.5 us -> 29.6 us  [hop(): return lax.ppermute(value, ('ctx', 'tp'), pairs)]
    pallas_call x8 -> x4, Pallas kernels: 9.75 us -> 9.63 us  [the longest x3 9.25 us: attention_part(): pl.pallas_call(functools.partial(attention_kernel, size, far, places), ou...]
  transfers between devices with their start and end apart: 20 -> 22, of which waited for: 14 -> 12; matrix products, arithmetic and copies ran while one was open for 7% -> 8% of each run, Pallas kernels for 12% -> 12%
where the time goes in v4:
time: 76.2 us; the launch traced here: 75.1 us
  starting transfers between devices  29.7 us (39%)
  waiting for transfers between devices  27.9 us (37%)
  Pallas kernels  10.7 us (14%)
  local copies, waits for them, and re-layouts  4.73 us (6%)
  other arithmetic  1.92 us (3%)
    ppermute x21, starting transfers between devices, hop(): return lax.ppermute(value, ('ctx', 'tp'), pairs)  29.6 us
    ppermute x21, waiting for transfers between devices, hop(): return lax.ppermute(value, ('ctx', 'tp'), pairs)  26.7 us
    pallas_call x3, Pallas kernels, attention_part(): pl.pallas_call(functools.partial(attention_kernel, size, far, places), ou...  9.25 us
    transpose x1, local copies, waits for them, and re-layouts, on_device(): values = jnp.transpose(cached_prompt_values, (2, 0, 1, 3))  3.28 us
  transfers between devices with their start and end apart: 22, of which 12 were waited for; matrix products, arithmetic and copies ran while one was open for 8% of the time, Pallas kernels for 12%

profile of v4, /device:TPU:0, one launch (start us, length us, event | category | flops | bytes accessed | tf_op | source)
XLA Modules:
  0.0 75.1 jit_solution(17041934508235591150)
XLA Ops:
  0.0 3.0 %collective-permute-start = (bf16[4,2,32,128]{3,2,1,0:T(8,128)(2,1)}, bf16[4,2,32,128]{3,2,1,0:T(8,128)(2,1)S(1)}, u32[]{:S(2)}, u32[]{:S(2)}) collective-permute-start(bf16[4,2,32,128]{3,2,1,0:T(8,128)(2,1)} %param.7), channel_id=1, source_target_pairs={{0,8},{1,9},{2,10},{3,11},{4,12},{5,13},{6,14},{7,15},{8,0},{9,1},... | collective-permute-start | bytes 196616 | tf_op jit(solution)/shard_map/ppermute | solution.py:70
  3.0 2.6 %collective-permute-start.1 = (bf16[4,2,32,128]{3,2,1,0:T(8,128)(2,1)}, bf16[4,2,32,128]{3,2,1,0:T(8,128)(2,1)S(1)}, u32[]{:S(2)}, u32[]{:S(2)}) collective-permute-start(bf16[4,2,32,128]{3,2,1,0:T(8,128)(2,1)} %param.7), channel_id=1, source_target_pairs={{0,16},{1,17},{2,18},{3,19},{4,20},{5,21},{6,22},{7,23},{8,24},{9,... | collective-permute-start | bytes 196616 | tf_op jit(solution)/shard_map/ppermute | solution.py:70
  5.6 0.0 collective-permute-start.2
  5.6 0.8 %convert_reduce_fusion = (s32[4]{0:T(128)S(1)}, s32[4]{0:T(128)S(1)}, s32[4,128]{1,0:T(4,128)S(1)}) fusion(s32[4,128]{1,0:T(4,128)} %param.12, s32[]{:T(128)S(6)} %mul.3), kind=kLoop, calls=%fused_computation.10 | loop fusion | flops 3576 | bytes 4132 | tf_op jit(solution)/shard_map/reduce_sum | solution.py:368
  6.4 0.1 iota_add_fusion
  6.5 0.1 iota_compare_fusion.1
  6.6 0.7 copy.21
  7.3 0.7 copy.20
  8.0 0.0 copy-start.1
  8.1 3.3 %copy_bitcast_fusion = (bf16[4,16,128,128]{3,2,1,0:T(8,128)(2,1)S(1)}, bf16[4,16,128,128]{3,2,1,0:T(8,128)(2,1)S(1)}) fusion(bf16[16,128,4,128]{3,2,1,0:T(4,128)(2,1)} %param.11, bf16[16,128,4,128]{3,2,1,0:T(4,128)(2,1)} %param.10), kind=kLoop, calls=%fused_computation | loop fusion | bytes 8388608 | tf_op jit(solution)/shard_map/transpose | solution.py:390
  11.4 0.2 select_reduce_fusion.lists
  11.6 0.0 collective-permute-done
  11.6 0.0 collective-permute-done.1
  11.6 0.3 collective-permute-done.2
  11.9 0.0 copy-done.1
  12.0 1.6 %collective-permute-start.3 = (bf16[4,4,2,32,128]{4,3,2,1,0:T(8,128)(2,1)S(1)}, bf16[4,4,2,32,128]{4,3,2,1,0:T(8,128)(2,1)S(1)}, u32[]{:S(2)}, u32[]{:S(2)}) collective-permute-start(bf16[4,4,2,32,128]{4,3,2,1,0:T(8,128)(2,1)S(1)} %pad_maximum_fusion.qa), channel_id=1, source_target_pairs={{0,2},{1,5},{2,0},{3,7},{4,6},{5,1},{6,4},{7,3},{8,10},{9,13},{10,... | collective-permute-start | bytes 786440 | tf_op jit(solution)/shard_map/ppermute | solution.py:70
  13.5 1.5 %collective-permute-start.5 = (bf16[4,4,2,32,128]{4,3,2,1,0:T(8,128)(2,1)S(1)}, bf16[4,4,2,32,128]{4,3,2,1,0:T(8,128)(2,1)S(1)}, u32[]{:S(2)}, u32[]{:S(2)}) collective-permute-start(bf16[4,4,2,32,128]{4,3,2,1,0:T(8,128)(2,1)S(1)} %pad_maximum_fusion.qa), channel_id=1, source_target_pairs={{0,4},{1,3},{2,6},{3,1},{4,0},{5,7},{6,2},{7,5},{8,12},{9,11},{10,... | collective-permute-start | bytes 786440 | tf_op jit(solution)/shard_map/ppermute | solution.py:70
  15.0 6.1 %collective-permute-done.3.qb = bf16[4,4,2,32,128]{4,3,2,1,0:T(8,128)(2,1)S(1)} collective-permute-done((bf16[4,4,2,32,128]{4,3,2,1,0:T(8,128)(2,1)S(1)}, bf16[4,4,2,32,128]{4,3,2,1,0:T(8,128)(2,1)S(1)}, u32[]{:S(2)}, u32[]{:S(2)}) %collective-permute-start.3) | collective-permute-done | bytes 262176 | tf_op jit(solution)/shard_map/ppermute | solution.py:70
  21.2 0.1 collective-permute-start.6
  21.2 4.1 %attention.3 = (bf16[528,128]{1,0:T(8,128)(2,1)S(1)}, bf16[528,128]{1,0:T(8,128)(2,1)S(1)}, bf16[528,128]{1,0:T(8,128)(2,1)S(1)}, bf16[528,128]{1,0:T(8,128)(2,1)S(1)}) custom-call(s32[4,16]{1,0:T(4,128)S(1)} %select_reduce_fusion.lists, s32[4]{0:T(128)S(1)} %sub.15.counts, bf16[4,4,2,32,128]{4,3,2,1,0:T(8,128)(2,1)S(1)} %pad_maximum_fusion.qa, ...), custom_call_target="tpu_custom_call" | custom-call | tf_op jit(solution)/shard_map/attention/pallas_call | solution.py:207
  25.3 2.0 %collective-permute-start.10 = (bf16[528,128]{1,0:T(8,128)(2,1)S(1)}, bf16[528,128]{1,0:T(8,128)(2,1)S(1)}, u32[]{:S(2)}, u32[]{:S(2)}) collective-permute-start(bf16[528,128]{1,0:T(8,128)(2,1)S(1)} %get-tuple-element.45), channel_id=1, source_target_pairs={{0,4},{1,3},{2,6},{3,1},{4,0},{5,7},{6,2},{7,5},{8,12},{9,11},{10,... | collective-permute-start | bytes 405512 | tf_op jit(solution)/shard_map/ppermute | solution.py:70
  27.4 1.9 %collective-permute-start.11 = (bf16[528,128]{1,0:T(8,128)(2,1)S(1)}, bf16[528,128]{1,0:T(8,128)(2,1)S(1)}, u32[]{:S(2)}, u32[]{:S(2)}) collective-permute-start(bf16[528,128]{1,0:T(8,128)(2,1)S(1)} %get-tuple-element.46), channel_id=1, source_target_pairs={{0,6},{1,7},{2,4},{3,5},{4,2},{5,3},{6,0},{7,1},{8,14},{9,15},{10,... | collective-permute-start | bytes 405512 | tf_op jit(solution)/shard_map/ppermute | solution.py:70
  29.3 0.0 collective-permute-start.4
  29.3 0.0 collective-permute-done.5.qa
  29.3 0.0 collective-permute-done.6.qb
  29.3 2.6 %attention.5 = (bf16[528,128]{1,0:T(8,128)(2,1)S(1)}, bf16[528,128]{1,0:T(8,128)(2,1)S(1)}) custom-call(s32[4,16]{1,0:T(4,128)S(1)} %select_reduce_fusion.lists, s32[4]{0:T(128)S(1)} %sub.15.counts, bf16[4,4,2,32,128]{4,3,2,1,0:T(8,128)(2,1)S(1)} %collective-permute-done.5.qa, bf16[4,4,2,32,128]{4,3,2,1,0:T(8,128)(2,1)S(1)} %collective-permute-done.6.qb, ...), custom_call_target="tpu_custom_call" | custom-call | tf_op jit(solution)/shard_map/attention/pallas_call | solution.py:207
  31.9 2.5 %collective-permute-start.8 = (bf16[528,128]{1,0:T(8,128)(2,1)S(1)}, bf16[528,128]{1,0:T(8,128)(2,1)S(1)}, u32[]{:S(2)}, u32[]{:S(2)}) collective-permute-start(bf16[528,128]{1,0:T(8,128)(2,1)S(1)} %get-tuple-element.42), channel_id=1, source_target_pairs={{0,6},{1,7},{2,4},{3,5},{4,2},{5,3},{6,0},{7,1},{8,14},{9,15},{10,... | collective-permute-start | bytes 405512 | tf_op jit(solution)/shard_map/ppermute | solution.py:70
  34.4 0.9 %collective-permute-start.9 = (bf16[528,128]{1,0:T(8,128)(2,1)S(1)}, bf16[528,128]{1,0:T(8,128)(2,1)S(1)}, u32[]{:S(2)}, u32[]{:S(2)}) collective-permute-start(bf16[528,128]{1,0:T(8,128)(2,1)S(1)} %get-tuple-element.44), channel_id=1, source_target_pairs={{0,2},{1,5},{2,0},{3,7},{4,6},{5,1},{6,4},{7,3},{8,10},{9,13},{10,... | collective-permute-start | bytes 405512 | tf_op jit(solution)/shard_map/ppermute | solution.py:70
  35.3 0.0 copy-start
  35.3 2.6 %attention.4 = (bf16[528,128]{1,0:T(8,128)(2,1)S(1)}, bf16[528,128]{1,0:T(8,128)(2,1)S(1)}) custom-call(s32[4,16]{1,0:T(4,128)S(1)} %select_reduce_fusion.lists, s32[4]{0:T(128)S(1)} %sub.15.counts, bf16[4,4,2,32,128]{4,3,2,1,0:T(8,128)(2,1)S(1)} %collective-permute-done.5.qa, bf16[4,4,2,32,128]{4,3,2,1,0:T(8,128)(2,1)S(1)} %collective-permute-done.6.qb, ...), custom_call_target="tpu_custom_call" | custom-call | tf_op jit(solution)/shard_map/attention/pallas_call | solution.py:207
  37.9 0.0 collective-permute-done.10.refs_6_
  37.9 1.5 %collective-permute-start.7 = (bf16[528,128]{1,0:T(8,128)(2,1)S(1)}, bf16[528,128]{1,0:T(8,128)(2,1)S(1)}, u32[]{:S(2)}, u32[]{:S(2)}) collective-permute-start(bf16[528,128]{1,0:T(8,128)(2,1)S(1)} %get-tuple-element.41), channel_id=1, source_target_pairs={{0,4},{1,3},{2,6},{3,1},{4,0},{5,7},{6,2},{7,5},{8,12},{9,11},{10,... | collective-permute-start | bytes 405512 | tf_op jit(solution)/shard_map/ppermute | solution.py:70
  39.4 0.0 collective-permute-done.11.refs_7_
  39.4 0.0 collective-permute-done.4.refs_1_
  39.4 0.0 collective-permute-done.8.refs_3_
  39.4 0.5 collective-permute-done.9.refs_5_
  39.9 3.1 %collective-permute-done.7.refs_2_ = bf16[528,128]{1,0:T(8,128)(2,1)S(1)} collective-permute-done((bf16[528,128]{1,0:T(8,128)(2,1)S(1)}, bf16[528,128]{1,0:T(8,128)(2,1)S(1)}, u32[]{:S(2)}, u32[]{:S(2)}) %collective-permute-start.7) | collective-permute-done | bytes 135200 | tf_op jit(solution)/shard_map/ppermute | solution.py:70
  43.0 0.4 split.1
  43.4 2.1 %collective-permute-start.12 = (bf16[272,128]{1,0:T(8,128)(2,1)S(1)}, bf16[272,128]{1,0:T(8,128)(2,1)S(1)}, u32[]{:S(2)}, u32[]{:S(2)}) collective-permute-start(bf16[272,128]{1,0:T(8,128)(2,1)S(1)} %get-tuple-element.48), channel_id=1, source_target_pairs={{0,8},{1,9},{2,10},{3,11},{4,12},{5,13},{6,14},{7,15},{8,0},{9,1},... | collective-permute-start | bytes 208904 | tf_op jit(solution)/shard_map/ppermute | solution.py:70
  45.5 2.9 %collective-permute-start.13 = (bf16[272,128]{1,0:T(8,128)(2,1)S(1)}, bf16[272,128]{1,0:T(8,128)(2,1)S(1)}, u32[]{:S(2)}, u32[]{:S(2)}) collective-permute-start(bf16[272,128]{1,0:T(8,128)(2,1)S(1)} %get-tuple-element.49), channel_id=1, source_target_pairs={{0,16},{1,17},{2,18},{3,19},{4,20},{5,21},{6,22},{7,23},{8,24},{9,... | collective-permute-start | bytes 208904 | tf_op jit(solution)/shard_map/ppermute | solution.py:70
  48.3 0.0 collective-permute-start.14
  48.3 0.0 collective-permute-done.12.refs_1_
  48.3 4.8 %collective-permute-done.13.refs_2_ = bf16[272,128]{1,0:T(8,128)(2,1)S(1)} collective-permute-done((bf16[272,128]{1,0:T(8,128)(2,1)S(1)}, bf16[272,128]{1,0:T(8,128)(2,1)S(1)}, u32[]{:S(2)}, u32[]{:S(2)}) %collective-permute-start.13) | collective-permute-done | bytes 69664 | tf_op jit(solution)/shard_map/ppermute | solution.py:70
  53.2 1.4 %collective-permute-done.14.refs_3_ = bf16[272,128]{1,0:T(8,128)(2,1)S(1)} collective-permute-done((bf16[272,128]{1,0:T(8,128)(2,1)S(1)}, bf16[272,128]{1,0:T(8,128)(2,1)S(1)}, u32[]{:S(2)}, u32[]{:S(2)}) %collective-permute-start.14) | collective-permute-done | bytes 69664 | tf_op jit(solution)/shard_map/ppermute | solution.py:70
  54.5 0.2 finish.1
  54.7 0.7 collective-permute-start.16
  55.4 2.5 %collective-permute-start.17 = (bf16[256,128]{1,0:T(8,128)(2,1)S(1)}, bf16[256,128]{1,0:T(8,128)(2,1)S(1)}, u32[]{:S(2)}, u32[]{:S(2)}) collective-permute-start(bf16[256,128]{1,0:T(8,128)(2,1)S(1)} %finish.1), channel_id=1, source_target_pairs={{0,24},{1,25},{2,26},{3,27},{4,28},{5,29},{6,30},{7,31},{8,16},{9,... | collective-permute-start | bytes 196616 | tf_op jit(solution)/shard_map/ppermute | solution.py:70
  57.8 0.4 collective-permute-start.15
  58.3 2.4 %collective-permute-done.16 = bf16[256,128]{1,0:T(8,128)(2,1)S(1)} collective-permute-done((bf16[256,128]{1,0:T(8,128)(2,1)S(1)}, bf16[256,128]{1,0:T(8,128)(2,1)S(1)}, u32[]{:S(2)}, u32[]{:S(2)}) %collective-permute-start.16) | collective-permute-done | bytes 65568 | tf_op jit(solution)/shard_map/ppermute | solution.py:70
  60.6 0.9 %collective-permute-done.17 = bf16[256,128]{1,0:T(8,128)(2,1)S(1)} collective-permute-done((bf16[256,128]{1,0:T(8,128)(2,1)S(1)}, bf16[256,128]{1,0:T(8,128)(2,1)S(1)}, u32[]{:S(2)}, u32[]{:S(2)}) %collective-permute-start.17) | collective-permute-done | bytes 65568 | tf_op jit(solution)/shard_map/ppermute | solution.py:70
  61.5 0.7 collective-permute-done.15
  62.3 0.8 %collective-permute-start.18 = (bf16[4,256,128]{2,1,0:T(8,128)(2,1)S(1)}, bf16[4,256,128]{2,1,0:T(8,128)(2,1)S(1)}, u32[]{:S(2)}, u32[]{:S(2)}) collective-permute-start(bf16[4,256,128]{2,1,0:T(8,128)(2,1)S(1)} %pad_maximum_fusion.1.a0), channel_id=1, source_target_pairs={{0,2},{1,5},{2,0},{3,7},{4,6},{5,1},{6,4},{7,3},{8,10},{9,13},{10,... | collective-permute-start | bytes 786440 | tf_op jit(solution)/shard_map/ppermute | solution.py:70
  63.1 1.7 %collective-permute-start.19 = (bf16[4,256,128]{2,1,0:T(8,128)(2,1)S(1)}, bf16[4,256,128]{2,1,0:T(8,128)(2,1)S(1)}, u32[]{:S(2)}, u32[]{:S(2)}) collective-permute-start(bf16[4,256,128]{2,1,0:T(8,128)(2,1)S(1)} %pad_maximum_fusion.1.a0), channel_id=1, source_target_pairs={{0,4},{1,3},{2,6},{3,1},{4,0},{5,7},{6,2},{7,5},{8,12},{9,11},{10,... | collective-permute-start | bytes 786440 | tf_op jit(solution)/shard_map/ppermute | solution.py:70
  64.8 1.1 %collective-permute-start.20 = (bf16[4,256,128]{2,1,0:T(8,128)(2,1)S(1)}, bf16[4,256,128]{2,1,0:T(8,128)(2,1)S(1)}, u32[]{:S(2)}, u32[]{:S(2)}) collective-permute-start(bf16[4,256,128]{2,1,0:T(8,128)(2,1)S(1)} %pad_maximum_fusion.1.a0), channel_id=1, source_target_pairs={{0,6},{1,7},{2,4},{3,5},{4,2},{5,3},{6,0},{7,1},{8,14},{9,15},{10,... | collective-permute-start | bytes 786440 | tf_op jit(solution)/shard_map/ppermute | solution.py:70
  65.8 2.9 %collective-permute-done.18.a1 = bf16[4,256,128]{2,1,0:T(8,128)(2,1)S(1)} collective-permute-done((bf16[4,256,128]{2,1,0:T(8,128)(2,1)S(1)}, bf16[4,256,128]{2,1,0:T(8,128)(2,1)S(1)}, u32[]{:S(2)}, u32[]{:S(2)}) %collective-permute-start.18) | collective-permute-done | bytes 262176 | tf_op jit(solution)/shard_map/ppermute | solution.py:70
  68.7 3.5 %collective-permute-done.19.a2 = bf16[4,256,128]{2,1,0:T(8,128)(2,1)S(1)} collective-permute-done((bf16[4,256,128]{2,1,0:T(8,128)(2,1)S(1)}, bf16[4,256,128]{2,1,0:T(8,128)(2,1)S(1)}, u32[]{:S(2)}, u32[]{:S(2)}) %collective-permute-start.19) | collective-permute-done | bytes 262176 | tf_op jit(solution)/shard_map/ppermute | solution.py:70
  72.2 0.0 collective-permute-done.20.a3
  72.2 0.0 copy-done
  72.2 0.9 %project.1 = (f32[4,16,512]{2,1,0:T(8,128)S(1)}, bf16[4,16,512]{2,1,0:T(8,128)(2,1)S(1)}) custom-call(bf16[4,256,128]{2,1,0:T(8,128)(2,1)S(1)} %pad_maximum_fusion.1.a0, bf16[4,256,128]{2,1,0:T(8,128)(2,1)S(1)} %collective-permute-done.18.a1, bf16[4,256,128]{2,1,0:T(8,128)(2,1)S(1)} %collective-permute-done.19.a2, ...), custom_call_target="tpu_custom_call" | custom-call | tf_op jit(solution)/shard_map/project/pallas_call | solution.py:339
  73.2 0.1 collective-permute-start.21
  73.3 1.2 %collective-permute-done.21 = bf16[4,16,512]{2,1,0:T(8,128)(2,1)S(1)} collective-permute-done((bf16[4,16,512]{2,1,0:T(8,128)(2,1)S(1)}, bf16[4,16,512]{2,1,0:T(8,128)(2,1)S(1)}, u32[]{:S(2)}, u32[]{:S(2)}) %collective-permute-start.21) | collective-permute-done | bytes 65568 | tf_op jit(solution)/shard_map/ppermute | solution.py:415
  74.5 0.6 add_convert_fusion
  (5 shorter events, 0.1 us)
Async XLA Ops:
  0.0 11.6 %collective-permute-start = (bf16[4,2,32,128]{3,2,1,0:T(8,128)(2,1)}, bf16[4,2,32,128]{3,2,1,0:T(8,128)(2,1)S(1)}, u32[]{:S(2)}, u32[]{:S(2)}) collective-permute-start(bf16[4,2,32,128]{3,2,1,0:T(8,128)(2,1)} %param.7), channel_id=1, source_target_pairs={{0,8},{1,9},{2,10},{3,11},{4,12},{5,13},{6,14},{7,15},{8,0},{9,1},... | collective-permute-start | bytes 196616 | tf_op jit(solution)/shard_map/ppermute | solution.py:70
  3.0 8.6 %collective-permute-start.1 = (bf16[4,2,32,128]{3,2,1,0:T(8,128)(2,1)}, bf16[4,2,32,128]{3,2,1,0:T(8,128)(2,1)S(1)}, u32[]{:S(2)}, u32[]{:S(2)}) collective-permute-start(bf16[4,2,32,128]{3,2,1,0:T(8,128)(2,1)} %param.7), channel_id=1, source_target_pairs={{0,16},{1,17},{2,18},{3,19},{4,20},{5,21},{6,22},{7,23},{8,24},{9,... | collective-permute-start | bytes 196616 | tf_op jit(solution)/shard_map/ppermute | solution.py:70
  5.6 6.3 %collective-permute-start.2 = (bf16[4,2,32,128]{3,2,1,0:T(8,128)(2,1)}, bf16[4,2,32,128]{3,2,1,0:T(8,128)(2,1)S(1)}, u32[]{:S(2)}, u32[]{:S(2)}) collective-permute-start(bf16[4,2,32,128]{3,2,1,0:T(8,128)(2,1)} %param.7), channel_id=1, source_target_pairs={{0,24},{1,25},{2,26},{3,27},{4,28},{5,29},{6,30},{7,31},{8,16},{9,... | collective-permute-start | bytes 196616 | tf_op jit(solution)/shard_map/ppermute | solution.py:70
  8.0 3.9 %copy-start.1 = (bf16[4,2,32,128]{3,2,1,0:T(8,128)(2,1)S(1)}, bf16[4,2,32,128]{3,2,1,0:T(8,128)(2,1)}, u32[]{:S(2)}) copy-start(bf16[4,2,32,128]{3,2,1,0:T(8,128)(2,1)} %param.7) | copy-start | bytes 196612
  12.0 9.2 %collective-permute-start.3 = (bf16[4,4,2,32,128]{4,3,2,1,0:T(8,128)(2,1)S(1)}, bf16[4,4,2,32,128]{4,3,2,1,0:T(8,128)(2,1)S(1)}, u32[]{:S(2)}, u32[]{:S(2)}) collective-permute-start(bf16[4,4,2,32,128]{4,3,2,1,0:T(8,128)(2,1)S(1)} %pad_maximum_fusion.qa), channel_id=1, source_target_pairs={{0,2},{1,5},{2,0},{3,7},{4,6},{5,1},{6,4},{7,3},{8,10},{9,13},{10,... | collective-permute-start | bytes 786440 | tf_op jit(solution)/shard_map/ppermute | solution.py:70
  13.5 15.8 %collective-permute-start.5 = (bf16[4,4,2,32,128]{4,3,2,1,0:T(8,128)(2,1)S(1)}, bf16[4,4,2,32,128]{4,3,2,1,0:T(8,128)(2,1)S(1)}, u32[]{:S(2)}, u32[]{:S(2)}) collective-permute-start(bf16[4,4,2,32,128]{4,3,2,1,0:T(8,128)(2,1)S(1)} %pad_maximum_fusion.qa), channel_id=1, source_target_pairs={{0,4},{1,3},{2,6},{3,1},{4,0},{5,7},{6,2},{7,5},{8,12},{9,11},{10,... | collective-permute-start | bytes 786440 | tf_op jit(solution)/shard_map/ppermute | solution.py:70
  21.2 8.2 %collective-permute-start.6 = (bf16[4,4,2,32,128]{4,3,2,1,0:T(8,128)(2,1)S(1)}, bf16[4,4,2,32,128]{4,3,2,1,0:T(8,128)(2,1)S(1)}, u32[]{:S(2)}, u32[]{:S(2)}) collective-permute-start(bf16[4,4,2,32,128]{4,3,2,1,0:T(8,128)(2,1)S(1)} %collective-permute-done.3.qb), channel_id=1, source_target_pairs={{0,4},{1,3},{2,6},{3,1},{4,0},{5,7},{6,2},{7,5},{8,12},{9,11},{10,... | collective-permute-start | bytes 786440 | tf_op jit(solution)/shard_map/ppermute | solution.py:70
  25.3 12.6 %collective-permute-start.10 = (bf16[528,128]{1,0:T(8,128)(2,1)S(1)}, bf16[528,128]{1,0:T(8,128)(2,1)S(1)}, u32[]{:S(2)}, u32[]{:S(2)}) collective-permute-start(bf16[528,128]{1,0:T(8,128)(2,1)S(1)} %get-tuple-element.45), channel_id=1, source_target_pairs={{0,4},{1,3},{2,6},{3,1},{4,0},{5,7},{6,2},{7,5},{8,12},{9,11},{10,... | collective-permute-start | bytes 405512 | tf_op jit(solution)/shard_map/ppermute | solution.py:70
  27.4 12.0 %collective-permute-start.11 = (bf16[528,128]{1,0:T(8,128)(2,1)S(1)}, bf16[528,128]{1,0:T(8,128)(2,1)S(1)}, u32[]{:S(2)}, u32[]{:S(2)}) collective-permute-start(bf16[528,128]{1,0:T(8,128)(2,1)S(1)} %get-tuple-element.46), channel_id=1, source_target_pairs={{0,6},{1,7},{2,4},{3,5},{4,2},{5,3},{6,0},{7,1},{8,14},{9,15},{10,... | collective-permute-start | bytes 405512 | tf_op jit(solution)/shard_map/ppermute | solution.py:70
  29.3 10.1 %collective-permute-start.4 = (bf16[528,128]{1,0:T(8,128)(2,1)S(1)}, bf16[528,128]{1,0:T(8,128)(2,1)S(1)}, u32[]{:S(2)}, u32[]{:S(2)}) collective-permute-start(bf16[528,128]{1,0:T(8,128)(2,1)S(1)} %get-tuple-element.40), channel_id=1, source_target_pairs={{0,2},{1,5},{2,0},{3,7},{4,6},{5,1},{6,4},{7,3},{8,10},{9,13},{10,... | collective-permute-start | bytes 405512 | tf_op jit(solution)/shard_map/ppermute | solution.py:70
  31.9 7.5 %collective-permute-start.8 = (bf16[528,128]{1,0:T(8,128)(2,1)S(1)}, bf16[528,128]{1,0:T(8,128)(2,1)S(1)}, u32[]{:S(2)}, u32[]{:S(2)}) collective-permute-start(bf16[528,128]{1,0:T(8,128)(2,1)S(1)} %get-tuple-element.42), channel_id=1, source_target_pairs={{0,6},{1,7},{2,4},{3,5},{4,2},{5,3},{6,0},{7,1},{8,14},{9,15},{10,... | collective-permute-start | bytes 405512 | tf_op jit(solution)/shard_map/ppermute | solution.py:70
  34.4 5.5 %collective-permute-start.9 = (bf16[528,128]{1,0:T(8,128)(2,1)S(1)}, bf16[528,128]{1,0:T(8,128)(2,1)S(1)}, u32[]{:S(2)}, u32[]{:S(2)}) collective-permute-start(bf16[528,128]{1,0:T(8,128)(2,1)S(1)} %get-tuple-element.44), channel_id=1, source_target_pairs={{0,2},{1,5},{2,0},{3,7},{4,6},{5,1},{6,4},{7,3},{8,10},{9,13},{10,... | collective-permute-start | bytes 405512 | tf_op jit(solution)/shard_map/ppermute | solution.py:70
  35.3 36.9 %copy-start = (bf16[4096,512]{1,0:T(8,128)(2,1)S(1)}, bf16[4096,512]{1,0:T(8,128)(2,1)}, u32[]{:S(2)}) copy-start(bf16[4096,512]{1,0:T(8,128)(2,1)} %weight.1) | copy-start | bytes 12582916
  37.9 5.1 %collective-permute-start.7 = (bf16[528,128]{1,0:T(8,128)(2,1)S(1)}, bf16[528,128]{1,0:T(8,128)(2,1)S(1)}, u32[]{:S(2)}, u32[]{:S(2)}) collective-permute-start(bf16[528,128]{1,0:T(8,128)(2,1)S(1)} %get-tuple-element.41), channel_id=1, source_target_pairs={{0,4},{1,3},{2,6},{3,1},{4,0},{5,7},{6,2},{7,5},{8,12},{9,11},{10,... | collective-permute-start | bytes 405512 | tf_op jit(solution)/shard_map/ppermute | solution.py:70
  43.4 5.0 %collective-permute-start.12 = (bf16[272,128]{1,0:T(8,128)(2,1)S(1)}, bf16[272,128]{1,0:T(8,128)(2,1)S(1)}, u32[]{:S(2)}, u32[]{:S(2)}) collective-permute-start(bf16[272,128]{1,0:T(8,128)(2,1)S(1)} %get-tuple-element.48), channel_id=1, source_target_pairs={{0,8},{1,9},{2,10},{3,11},{4,12},{5,13},{6,14},{7,15},{8,0},{9,1},... | collective-permute-start | bytes 208904 | tf_op jit(solution)/shard_map/ppermute | solution.py:70
  45.5 7.7 %collective-permute-start.13 = (bf16[272,128]{1,0:T(8,128)(2,1)S(1)}, bf16[272,128]{1,0:T(8,128)(2,1)S(1)}, u32[]{:S(2)}, u32[]{:S(2)}) collective-permute-start(bf16[272,128]{1,0:T(8,128)(2,1)S(1)} %get-tuple-element.49), channel_id=1, source_target_pairs={{0,16},{1,17},{2,18},{3,19},{4,20},{5,21},{6,22},{7,23},{8,24},{9,... | collective-permute-start | bytes 208904 | tf_op jit(solution)/shard_map/ppermute | solution.py:70
  48.3 6.2 %collective-permute-start.14 = (bf16[272,128]{1,0:T(8,128)(2,1)S(1)}, bf16[272,128]{1,0:T(8,128)(2,1)S(1)}, u32[]{:S(2)}, u32[]{:S(2)}) collective-permute-start(bf16[272,128]{1,0:T(8,128)(2,1)S(1)} %get-tuple-element.50), channel_id=1, source_target_pairs={{0,24},{1,25},{2,26},{3,27},{4,28},{5,29},{6,30},{7,31},{8,16},{9,... | collective-permute-start | bytes 208904 | tf_op jit(solution)/shard_map/ppermute | solution.py:70
  54.7 5.9 %collective-permute-start.16 = (bf16[256,128]{1,0:T(8,128)(2,1)S(1)}, bf16[256,128]{1,0:T(8,128)(2,1)S(1)}, u32[]{:S(2)}, u32[]{:S(2)}) collective-permute-start(bf16[256,128]{1,0:T(8,128)(2,1)S(1)} %finish.1), channel_id=1, source_target_pairs={{0,16},{1,17},{2,18},{3,19},{4,20},{5,21},{6,22},{7,23},{8,24},{9,... | collective-permute-start | bytes 196616 | tf_op jit(solution)/shard_map/ppermute | solution.py:70
  55.4 6.2 %collective-permute-start.17 = (bf16[256,128]{1,0:T(8,128)(2,1)S(1)}, bf16[256,128]{1,0:T(8,128)(2,1)S(1)}, u32[]{:S(2)}, u32[]{:S(2)}) collective-permute-start(bf16[256,128]{1,0:T(8,128)(2,1)S(1)} %finish.1), channel_id=1, source_target_pairs={{0,24},{1,25},{2,26},{3,27},{4,28},{5,29},{6,30},{7,31},{8,16},{9,... | collective-permute-start | bytes 196616 | tf_op jit(solution)/shard_map/ppermute | solution.py:70
  57.8 4.4 %collective-permute-start.15 = (bf16[256,128]{1,0:T(8,128)(2,1)S(1)}, bf16[256,128]{1,0:T(8,128)(2,1)S(1)}, u32[]{:S(2)}, u32[]{:S(2)}) collective-permute-start(bf16[256,128]{1,0:T(8,128)(2,1)S(1)} %finish.1), channel_id=1, source_target_pairs={{0,8},{1,9},{2,10},{3,11},{4,12},{5,13},{6,14},{7,15},{8,0},{9,1},... | collective-permute-start | bytes 196616 | tf_op jit(solution)/shard_map/ppermute | solution.py:70
  62.3 6.4 %collective-permute-start.18 = (bf16[4,256,128]{2,1,0:T(8,128)(2,1)S(1)}, bf16[4,256,128]{2,1,0:T(8,128)(2,1)S(1)}, u32[]{:S(2)}, u32[]{:S(2)}) collective-permute-start(bf16[4,256,128]{2,1,0:T(8,128)(2,1)S(1)} %pad_maximum_fusion.1.a0), channel_id=1, source_target_pairs={{0,2},{1,5},{2,0},{3,7},{4,6},{5,1},{6,4},{7,3},{8,10},{9,13},{10,... | collective-permute-start | bytes 786440 | tf_op jit(solution)/shard_map/ppermute | solution.py:70
  63.1 9.2 %collective-permute-start.19 = (bf16[4,256,128]{2,1,0:T(8,128)(2,1)S(1)}, bf16[4,256,128]{2,1,0:T(8,128)(2,1)S(1)}, u32[]{:S(2)}, u32[]{:S(2)}) collective-permute-start(bf16[4,256,128]{2,1,0:T(8,128)(2,1)S(1)} %pad_maximum_fusion.1.a0), channel_id=1, source_target_pairs={{0,4},{1,3},{2,6},{3,1},{4,0},{5,7},{6,2},{7,5},{8,12},{9,11},{10,... | collective-permute-start | bytes 786440 | tf_op jit(solution)/shard_map/ppermute | solution.py:70
  64.8 7.5 %collective-permute-start.20 = (bf16[4,256,128]{2,1,0:T(8,128)(2,1)S(1)}, bf16[4,256,128]{2,1,0:T(8,128)(2,1)S(1)}, u32[]{:S(2)}, u32[]{:S(2)}) collective-permute-start(bf16[4,256,128]{2,1,0:T(8,128)(2,1)S(1)} %pad_maximum_fusion.1.a0), channel_id=1, source_target_pairs={{0,6},{1,7},{2,4},{3,5},{4,2},{5,3},{6,0},{7,1},{8,14},{9,15},{10,... | collective-permute-start | bytes 786440 | tf_op jit(solution)/shard_map/ppermute | solution.py:70
  73.2 1.3 %collective-permute-start.21 = (bf16[4,16,512]{2,1,0:T(8,128)(2,1)S(1)}, bf16[4,16,512]{2,1,0:T(8,128)(2,1)S(1)}, u32[]{:S(2)}, u32[]{:S(2)}) collective-permute-start(bf16[4,16,512]{2,1,0:T(8,128)(2,1)S(1)} %get-tuple-element.52), channel_id=1, source_target_pairs={{0,1},{1,0},{2,3},{3,2},{4,5},{5,4},{6,7},{7,6},{8,9},{9,8},{10,11... | collective-permute-start | bytes 196616 | tf_op jit(solution)/shard_map/ppermute | solution.py:415

commit v5 on v4

--- a/solution.py
+++ b/solution.py
@@ -403,10 +403,10 @@
         size, 0, ((1, 0), (1, 1), (0, 1), (0, 0)), lists, counts, q0, q1, *shared
     )
     near_a, near_ab, near_b = hop(size, near_a, "first"), hop(size, near_ab, "both"), hop(size, near_b, "second")
-    far_a, far_ab = attention_part(size, 1, ((1, 0), (1, 1)), lists, counts, q2, q3, *shared)
-    far_a, far_ab = hop(size, far_a, "first"), hop(size, far_ab, "both")
-    far_b, far = attention_part(size, 1, ((0, 1), (0, 0)), lists, counts, q2, q3, *shared)
-    far_b = hop(size, far_b, "second")
+    far_a, far_ab, far_b, far = attention_part(
+        size, 1, ((1, 0), (1, 1), (0, 1), (0, 0)), lists, counts, q2, q3, *shared
+    )
+    far_a, far_ab, far_b = hop(size, far_a, "first"), hop(size, far_ab, "both"), hop(size, far_b, "second")
     parts = split_merge(size, (near, near_a, far_b, far_ab), (far, far_a, near_b, near_ab))
     parts = [parts[0]] + [hop(size, parts[k], k) for k in range(1, lines)]
     attention = finish(size, parts)

time: 76.2 us -> 76.3 us (level)
  starting transfers between devices: 29.7 us -> 27.7 us
  waiting for transfers between devices: 27.9 us -> 29.6 us
  Pallas kernels: 10.7 us -> 11.7 us
    ppermute x21, starting transfers between devices: 29.6 us -> 27.6 us  [hop(): return lax.ppermute(value, ('ctx', 'tp'), pairs)]
    ppermute x21, waiting for transfers between devices: 26.7 us -> 28.3 us  [hop(): return lax.ppermute(value, ('ctx', 'tp'), pairs)]
    pallas_call x3 -> x2, Pallas kernels: 9.25 us -> 10.2 us  [attention_part(): pl.pallas_call(functools.partial(attention_kernel, size, far, places), ou...]
  transfers between devices with their start and end apart: 22 -> 22, of which waited for: 12 -> 12; matrix products, arithmetic and copies ran while one was open for 8% -> 8% of each run, Pallas kernels for 12% -> 13%
where the time goes in v5:
time: 76.3 us; the launch traced here: 75.7 us
  waiting for transfers between devices  29.6 us (39%)
  starting transfers between devices  27.7 us (36%)
  Pallas kernels  11.7 us (15%)
  local copies, waits for them, and re-layouts  4.73 us (6%)
  other arithmetic  1.92 us (3%)
    ppermute x21, waiting for transfers between devices, hop(): return lax.ppermute(value, ('ctx', 'tp'), pairs)  28.3 us
    ppermute x21, starting transfers between devices, hop(): return lax.ppermute(value, ('ctx', 'tp'), pairs)  27.6 us
    pallas_call x2, Pallas kernels, attention_part(): pl.pallas_call(functools.partial(attention_kernel, size, far, places), ou...  10.2 us
    transpose x1, local copies, waits for them, and re-layouts, on_device(): values = jnp.transpose(cached_prompt_values, (2, 0, 1, 3))  3.28 us
  transfers between devices with their start and end apart: 22, of which 12 were waited for; matrix products, arithmetic and copies ran while one was open for 8% of the time, Pallas kernels for 13%

profile of v5, /device:TPU:0, one launch (start us, length us, event | category | flops | bytes accessed | tf_op | source)
XLA Modules:
  0.0 75.7 jit_solution(12179166650822776972)
XLA Ops:
  0.0 3.0 %collective-permute-start = (bf16[4,2,32,128]{3,2,1,0:T(8,128)(2,1)}, bf16[4,2,32,128]{3,2,1,0:T(8,128)(2,1)S(1)}, u32[]{:S(2)}, u32[]{:S(2)}) collective-permute-start(bf16[4,2,32,128]{3,2,1,0:T(8,128)(2,1)} %param.7), channel_id=1, source_target_pairs={{0,8},{1,9},{2,10},{3,11},{4,12},{5,13},{6,14},{7,15},{8,0},{9,1},... | collective-permute-start | bytes 196616 | tf_op jit(solution)/shard_map/ppermute | solution.py:70
  3.0 2.6 %collective-permute-start.1 = (bf16[4,2,32,128]{3,2,1,0:T(8,128)(2,1)}, bf16[4,2,32,128]{3,2,1,0:T(8,128)(2,1)S(1)}, u32[]{:S(2)}, u32[]{:S(2)}) collective-permute-start(bf16[4,2,32,128]{3,2,1,0:T(8,128)(2,1)} %param.7), channel_id=1, source_target_pairs={{0,16},{1,17},{2,18},{3,19},{4,20},{5,21},{6,22},{7,23},{8,24},{9,... | collective-permute-start | bytes 196616 | tf_op jit(solution)/shard_map/ppermute | solution.py:70
  5.6 0.0 collective-permute-start.2
  5.6 0.8 %convert_reduce_fusion = (s32[4]{0:T(128)S(1)}, s32[4]{0:T(128)S(1)}, s32[4,128]{1,0:T(4,128)S(1)}) fusion(s32[4,128]{1,0:T(4,128)} %param.12, s32[]{:T(128)S(6)} %mul.3), kind=kLoop, calls=%fused_computation.10 | loop fusion | flops 3576 | bytes 4132 | tf_op jit(solution)/shard_map/reduce_sum | solution.py:368
  6.4 0.1 iota_add_fusion
  6.5 0.1 iota_compare_fusion.1
  6.6 0.7 copy.21
  7.3 0.7 copy.20
  8.0 0.0 copy-start.1
  8.1 3.3 %copy_bitcast_fusion = (bf16[4,16,128,128]{3,2,1,0:T(8,128)(2,1)S(1)}, bf16[4,16,128,128]{3,2,1,0:T(8,128)(2,1)S(1)}) fusion(bf16[16,128,4,128]{3,2,1,0:T(4,128)(2,1)} %param.11, bf16[16,128,4,128]{3,2,1,0:T(4,128)(2,1)} %param.10), kind=kLoop, calls=%fused_computation | loop fusion | bytes 8388608 | tf_op jit(solution)/shard_map/transpose | solution.py:390
  11.4 0.2 select_reduce_fusion.lists
  11.6 0.0 collective-permute-done
  11.6 0.0 collective-permute-done.1
  11.6 0.3 collective-permute-done.2
  11.9 0.0 copy-done.1
  12.0 1.6 %collective-permute-start.3 = (bf16[4,4,2,32,128]{4,3,2,1,0:T(8,128)(2,1)S(1)}, bf16[4,4,2,32,128]{4,3,2,1,0:T(8,128)(2,1)S(1)}, u32[]{:S(2)}, u32[]{:S(2)}) collective-permute-start(bf16[4,4,2,32,128]{4,3,2,1,0:T(8,128)(2,1)S(1)} %pad_maximum_fusion.qa), channel_id=1, source_target_pairs={{0,2},{1,5},{2,0},{3,7},{4,6},{5,1},{6,4},{7,3},{8,10},{9,13},{10,... | collective-permute-start | bytes 786440 | tf_op jit(solution)/shard_map/ppermute | solution.py:70
  13.5 1.5 %collective-permute-start.5 = (bf16[4,4,2,32,128]{4,3,2,1,0:T(8,128)(2,1)S(1)}, bf16[4,4,2,32,128]{4,3,2,1,0:T(8,128)(2,1)S(1)}, u32[]{:S(2)}, u32[]{:S(2)}) collective-permute-start(bf16[4,4,2,32,128]{4,3,2,1,0:T(8,128)(2,1)S(1)} %pad_maximum_fusion.qa), channel_id=1, source_target_pairs={{0,4},{1,3},{2,6},{3,1},{4,0},{5,7},{6,2},{7,5},{8,12},{9,11},{10,... | collective-permute-start | bytes 786440 | tf_op jit(solution)/shard_map/ppermute | solution.py:70
  15.0 6.1 %collective-permute-done.3.qb = bf16[4,4,2,32,128]{4,3,2,1,0:T(8,128)(2,1)S(1)} collective-permute-done((bf16[4,4,2,32,128]{4,3,2,1,0:T(8,128)(2,1)S(1)}, bf16[4,4,2,32,128]{4,3,2,1,0:T(8,128)(2,1)S(1)}, u32[]{:S(2)}, u32[]{:S(2)}) %collective-permute-start.3) | collective-permute-done | bytes 262176 | tf_op jit(solution)/shard_map/ppermute | solution.py:70
  21.2 0.1 collective-permute-start.6
  21.2 5.1 %attention.2 = (bf16[528,128]{1,0:T(8,128)(2,1)S(1)}, bf16[528,128]{1,0:T(8,128)(2,1)S(1)}, bf16[528,128]{1,0:T(8,128)(2,1)S(1)}, bf16[528,128]{1,0:T(8,128)(2,1)S(1)}) custom-call(s32[4,16]{1,0:T(4,128)S(1)} %select_reduce_fusion.lists, s32[4]{0:T(128)S(1)} %sub.15.counts, bf16[4,4,2,32,128]{4,3,2,1,0:T(8,128)(2,1)S(1)} %pad_maximum_fusion.qa, ...), custom_call_target="tpu_custom_call" | custom-call | tf_op jit(solution)/shard_map/attention/pallas_call | solution.py:207
  26.3 2.0 %collective-permute-start.10 = (bf16[528,128]{1,0:T(8,128)(2,1)S(1)}, bf16[528,128]{1,0:T(8,128)(2,1)S(1)}, u32[]{:S(2)}, u32[]{:S(2)}) collective-permute-start(bf16[528,128]{1,0:T(8,128)(2,1)S(1)} %get-tuple-element.45), channel_id=1, source_target_pairs={{0,4},{1,3},{2,6},{3,1},{4,0},{5,7},{6,2},{7,5},{8,12},{9,11},{10,... | collective-permute-start | bytes 405512 | tf_op jit(solution)/shard_map/ppermute | solution.py:70
  28.4 0.0 collective-permute-start.11
  28.4 1.5 %collective-permute-start.4 = (bf16[528,128]{1,0:T(8,128)(2,1)S(1)}, bf16[528,128]{1,0:T(8,128)(2,1)S(1)}, u32[]{:S(2)}, u32[]{:S(2)}) collective-permute-start(bf16[528,128]{1,0:T(8,128)(2,1)S(1)} %get-tuple-element.40), channel_id=1, source_target_pairs={{0,2},{1,5},{2,0},{3,7},{4,6},{5,1},{6,4},{7,3},{8,10},{9,13},{10,... | collective-permute-start | bytes 405512 | tf_op jit(solution)/shard_map/ppermute | solution.py:70
  29.9 0.0 collective-permute-done.5.qa
  29.9 0.0 collective-permute-done.6.qb
  29.9 0.0 copy-start
  29.9 5.1 %attention.3 = (bf16[528,128]{1,0:T(8,128)(2,1)S(1)}, bf16[528,128]{1,0:T(8,128)(2,1)S(1)}, bf16[528,128]{1,0:T(8,128)(2,1)S(1)}, bf16[528,128]{1,0:T(8,128)(2,1)S(1)}) custom-call(s32[4,16]{1,0:T(4,128)S(1)} %select_reduce_fusion.lists, s32[4]{0:T(128)S(1)} %sub.15.counts, bf16[4,4,2,32,128]{4,3,2,1,0:T(8,128)(2,1)S(1)} %collective-permute-done.5.qa, ...), custom_call_target="tpu_custom_call" | custom-call | tf_op jit(solution)/shard_map/attention/pallas_call | solution.py:207
  35.0 2.0 %collective-permute-start.7 = (bf16[528,128]{1,0:T(8,128)(2,1)S(1)}, bf16[528,128]{1,0:T(8,128)(2,1)S(1)}, u32[]{:S(2)}, u32[]{:S(2)}) collective-permute-start(bf16[528,128]{1,0:T(8,128)(2,1)S(1)} %get-tuple-element.41), channel_id=1, source_target_pairs={{0,4},{1,3},{2,6},{3,1},{4,0},{5,7},{6,2},{7,5},{8,12},{9,11},{10,... | collective-permute-start | bytes 405512 | tf_op jit(solution)/shard_map/ppermute | solution.py:70
  37.0 0.0 collective-permute-start.8
  37.0 0.0 collective-permute-done.10.refs_6_
  37.0 1.5 %collective-permute-start.9 = (bf16[528,128]{1,0:T(8,128)(2,1)S(1)}, bf16[528,128]{1,0:T(8,128)(2,1)S(1)}, u32[]{:S(2)}, u32[]{:S(2)}) collective-permute-start(bf16[528,128]{1,0:T(8,128)(2,1)S(1)} %get-tuple-element.44), channel_id=1, source_target_pairs={{0,2},{1,5},{2,0},{3,7},{4,6},{5,1},{6,4},{7,3},{8,10},{9,13},{10,... | collective-permute-start | bytes 405512 | tf_op jit(solution)/shard_map/ppermute | solution.py:70
  38.6 0.0 collective-permute-done.11.refs_7_
  38.6 0.0 collective-permute-done.4.refs_1_
  38.6 2.5 %collective-permute-done.7.refs_2_ = bf16[528,128]{1,0:T(8,128)(2,1)S(1)} collective-permute-done((bf16[528,128]{1,0:T(8,128)(2,1)S(1)}, bf16[528,128]{1,0:T(8,128)(2,1)S(1)}, u32[]{:S(2)}, u32[]{:S(2)}) %collective-permute-start.7) | collective-permute-done | bytes 135200 | tf_op jit(solution)/shard_map/ppermute | solution.py:70
  41.0 1.9 %collective-permute-done.8.refs_3_ = bf16[528,128]{1,0:T(8,128)(2,1)S(1)} collective-permute-done((bf16[528,128]{1,0:T(8,128)(2,1)S(1)}, bf16[528,128]{1,0:T(8,128)(2,1)S(1)}, u32[]{:S(2)}, u32[]{:S(2)}) %collective-permute-start.8) | collective-permute-done | bytes 135200 | tf_op jit(solution)/shard_map/ppermute | solution.py:70
  42.9 0.1 collective-permute-done.9.refs_5_
  43.1 0.4 split.1
  43.4 0.7 collective-permute-start.12
  44.1 3.4 %collective-permute-start.13 = (bf16[272,128]{1,0:T(8,128)(2,1)S(1)}, bf16[272,128]{1,0:T(8,128)(2,1)S(1)}, u32[]{:S(2)}, u32[]{:S(2)}) collective-permute-start(bf16[272,128]{1,0:T(8,128)(2,1)S(1)} %get-tuple-element.49), channel_id=1, source_target_pairs={{0,16},{1,17},{2,18},{3,19},{4,20},{5,21},{6,22},{7,23},{8,24},{9,... | collective-permute-start | bytes 208904 | tf_op jit(solution)/shard_map/ppermute | solution.py:70
  47.5 0.4 collective-permute-start.14
  47.9 0.0 collective-permute-done.12.refs_1_
  47.9 4.5 %collective-permute-done.13.refs_2_ = bf16[272,128]{1,0:T(8,128)(2,1)S(1)} collective-permute-done((bf16[272,128]{1,0:T(8,128)(2,1)S(1)}, bf16[272,128]{1,0:T(8,128)(2,1)S(1)}, u32[]{:S(2)}, u32[]{:S(2)}) %collective-permute-start.13) | collective-permute-done | bytes 69664 | tf_op jit(solution)/shard_map/ppermute | solution.py:70
  52.4 1.4 %collective-permute-done.14.refs_3_ = bf16[272,128]{1,0:T(8,128)(2,1)S(1)} collective-permute-done((bf16[272,128]{1,0:T(8,128)(2,1)S(1)}, bf16[272,128]{1,0:T(8,128)(2,1)S(1)}, u32[]{:S(2)}, u32[]{:S(2)}) %collective-permute-start.14) | collective-permute-done | bytes 69664 | tf_op jit(solution)/shard_map/ppermute | solution.py:70
  53.8 0.2 finish.1
  54.0 2.5 %collective-permute-start.16 = (bf16[256,128]{1,0:T(8,128)(2,1)S(1)}, bf16[256,128]{1,0:T(8,128)(2,1)S(1)}, u32[]{:S(2)}, u32[]{:S(2)}) collective-permute-start(bf16[256,128]{1,0:T(8,128)(2,1)S(1)} %finish.1), channel_id=1, source_target_pairs={{0,16},{1,17},{2,18},{3,19},{4,20},{5,21},{6,22},{7,23},{8,24},{9,... | collective-permute-start | bytes 196616 | tf_op jit(solution)/shard_map/ppermute | solution.py:70
  56.5 1.2 %collective-permute-start.17 = (bf16[256,128]{1,0:T(8,128)(2,1)S(1)}, bf16[256,128]{1,0:T(8,128)(2,1)S(1)}, u32[]{:S(2)}, u32[]{:S(2)}) collective-permute-start(bf16[256,128]{1,0:T(8,128)(2,1)S(1)} %finish.1), channel_id=1, source_target_pairs={{0,24},{1,25},{2,26},{3,27},{4,28},{5,29},{6,30},{7,31},{8,16},{9,... | collective-permute-start | bytes 196616 | tf_op jit(solution)/shard_map/ppermute | solution.py:70
  57.7 0.0 collective-permute-start.15
  57.7 1.5 %collective-permute-done.16 = bf16[256,128]{1,0:T(8,128)(2,1)S(1)} collective-permute-done((bf16[256,128]{1,0:T(8,128)(2,1)S(1)}, bf16[256,128]{1,0:T(8,128)(2,1)S(1)}, u32[]{:S(2)}, u32[]{:S(2)}) %collective-permute-start.16) | collective-permute-done | bytes 65568 | tf_op jit(solution)/shard_map/ppermute | solution.py:70
  59.2 3.5 %collective-permute-done.17 = bf16[256,128]{1,0:T(8,128)(2,1)S(1)} collective-permute-done((bf16[256,128]{1,0:T(8,128)(2,1)S(1)}, bf16[256,128]{1,0:T(8,128)(2,1)S(1)}, u32[]{:S(2)}, u32[]{:S(2)}) %collective-permute-start.17) | collective-permute-done | bytes 65568 | tf_op jit(solution)/shard_map/ppermute | solution.py:70
  62.7 0.0 collective-permute-done.15
  62.7 0.9 %collective-permute-start.18 = (bf16[4,256,128]{2,1,0:T(8,128)(2,1)S(1)}, bf16[4,256,128]{2,1,0:T(8,128)(2,1)S(1)}, u32[]{:S(2)}, u32[]{:S(2)}) collective-permute-start(bf16[4,256,128]{2,1,0:T(8,128)(2,1)S(1)} %pad_maximum_fusion.1.a0), channel_id=1, source_target_pairs={{0,2},{1,5},{2,0},{3,7},{4,6},{5,1},{6,4},{7,3},{8,10},{9,13},{10,... | collective-permute-start | bytes 786440 | tf_op jit(solution)/shard_map/ppermute | solution.py:70
  63.6 0.8 %collective-permute-start.19 = (bf16[4,256,128]{2,1,0:T(8,128)(2,1)S(1)}, bf16[4,256,128]{2,1,0:T(8,128)(2,1)S(1)}, u32[]{:S(2)}, u32[]{:S(2)}) collective-permute-start(bf16[4,256,128]{2,1,0:T(8,128)(2,1)S(1)} %pad_maximum_fusion.1.a0), channel_id=1, source_target_pairs={{0,4},{1,3},{2,6},{3,1},{4,0},{5,7},{6,2},{7,5},{8,12},{9,11},{10,... | collective-permute-start | bytes 786440 | tf_op jit(solution)/shard_map/ppermute | solution.py:70
  64.4 1.8 %collective-permute-start.20 = (bf16[4,256,128]{2,1,0:T(8,128)(2,1)S(1)}, bf16[4,256,128]{2,1,0:T(8,128)(2,1)S(1)}, u32[]{:S(2)}, u32[]{:S(2)}) collective-permute-start(bf16[4,256,128]{2,1,0:T(8,128)(2,1)S(1)} %pad_maximum_fusion.1.a0), channel_id=1, source_target_pairs={{0,6},{1,7},{2,4},{3,5},{4,2},{5,3},{6,0},{7,1},{8,14},{9,15},{10,... | collective-permute-start | bytes 786440 | tf_op jit(solution)/shard_map/ppermute | solution.py:70
  66.3 2.9 %collective-permute-done.18.a1 = bf16[4,256,128]{2,1,0:T(8,128)(2,1)S(1)} collective-permute-done((bf16[4,256,128]{2,1,0:T(8,128)(2,1)S(1)}, bf16[4,256,128]{2,1,0:T(8,128)(2,1)S(1)}, u32[]{:S(2)}, u32[]{:S(2)}) %collective-permute-start.18) | collective-permute-done | bytes 262176 | tf_op jit(solution)/shard_map/ppermute | solution.py:70
  69.2 3.6 %collective-permute-done.19.a2 = bf16[4,256,128]{2,1,0:T(8,128)(2,1)S(1)} collective-permute-done((bf16[4,256,128]{2,1,0:T(8,128)(2,1)S(1)}, bf16[4,256,128]{2,1,0:T(8,128)(2,1)S(1)}, u32[]{:S(2)}, u32[]{:S(2)}) %collective-permute-start.19) | collective-permute-done | bytes 262176 | tf_op jit(solution)/shard_map/ppermute | solution.py:70
  72.8 0.0 collective-permute-done.20.a3
  72.8 0.0 copy-done
  72.8 0.9 %project.1 = (f32[4,16,512]{2,1,0:T(8,128)S(1)}, bf16[4,16,512]{2,1,0:T(8,128)(2,1)S(1)}) custom-call(bf16[4,256,128]{2,1,0:T(8,128)(2,1)S(1)} %pad_maximum_fusion.1.a0, bf16[4,256,128]{2,1,0:T(8,128)(2,1)S(1)} %collective-permute-done.18.a1, bf16[4,256,128]{2,1,0:T(8,128)(2,1)S(1)} %collective-permute-done.19.a2, ...), custom_call_target="tpu_custom_call" | custom-call | tf_op jit(solution)/shard_map/project/pallas_call | solution.py:339
  73.7 0.1 collective-permute-start.21
  73.8 1.2 %collective-permute-done.21 = bf16[4,16,512]{2,1,0:T(8,128)(2,1)S(1)} collective-permute-done((bf16[4,16,512]{2,1,0:T(8,128)(2,1)S(1)}, bf16[4,16,512]{2,1,0:T(8,128)(2,1)S(1)}, u32[]{:S(2)}, u32[]{:S(2)}) %collective-permute-start.21) | collective-permute-done | bytes 65568 | tf_op jit(solution)/shard_map/ppermute | solution.py:415
  75.1 0.6 add_convert_fusion
  (5 shorter events, 0.1 us)
Async XLA Ops:
  0.0 11.6 %collective-permute-start = (bf16[4,2,32,128]{3,2,1,0:T(8,128)(2,1)}, bf16[4,2,32,128]{3,2,1,0:T(8,128)(2,1)S(1)}, u32[]{:S(2)}, u32[]{:S(2)}) collective-permute-start(bf16[4,2,32,128]{3,2,1,0:T(8,128)(2,1)} %param.7), channel_id=1, source_target_pairs={{0,8},{1,9},{2,10},{3,11},{4,12},{5,13},{6,14},{7,15},{8,0},{9,1},... | collective-permute-start | bytes 196616 | tf_op jit(solution)/shard_map/ppermute | solution.py:70
  3.0 8.6 %collective-permute-start.1 = (bf16[4,2,32,128]{3,2,1,0:T(8,128)(2,1)}, bf16[4,2,32,128]{3,2,1,0:T(8,128)(2,1)S(1)}, u32[]{:S(2)}, u32[]{:S(2)}) collective-permute-start(bf16[4,2,32,128]{3,2,1,0:T(8,128)(2,1)} %param.7), channel_id=1, source_target_pairs={{0,16},{1,17},{2,18},{3,19},{4,20},{5,21},{6,22},{7,23},{8,24},{9,... | collective-permute-start | bytes 196616 | tf_op jit(solution)/shard_map/ppermute | solution.py:70
  5.6 6.3 %collective-permute-start.2 = (bf16[4,2,32,128]{3,2,1,0:T(8,128)(2,1)}, bf16[4,2,32,128]{3,2,1,0:T(8,128)(2,1)S(1)}, u32[]{:S(2)}, u32[]{:S(2)}) collective-permute-start(bf16[4,2,32,128]{3,2,1,0:T(8,128)(2,1)} %param.7), channel_id=1, source_target_pairs={{0,24},{1,25},{2,26},{3,27},{4,28},{5,29},{6,30},{7,31},{8,16},{9,... | collective-permute-start | bytes 196616 | tf_op jit(solution)/shard_map/ppermute | solution.py:70
  8.0 3.9 %copy-start.1 = (bf16[4,2,32,128]{3,2,1,0:T(8,128)(2,1)S(1)}, bf16[4,2,32,128]{3,2,1,0:T(8,128)(2,1)}, u32[]{:S(2)}) copy-start(bf16[4,2,32,128]{3,2,1,0:T(8,128)(2,1)} %param.7) | copy-start | bytes 196612
  12.0 9.2 %collective-permute-start.3 = (bf16[4,4,2,32,128]{4,3,2,1,0:T(8,128)(2,1)S(1)}, bf16[4,4,2,32,128]{4,3,2,1,0:T(8,128)(2,1)S(1)}, u32[]{:S(2)}, u32[]{:S(2)}) collective-permute-start(bf16[4,4,2,32,128]{4,3,2,1,0:T(8,128)(2,1)S(1)} %pad_maximum_fusion.qa), channel_id=1, source_target_pairs={{0,2},{1,5},{2,0},{3,7},{4,6},{5,1},{6,4},{7,3},{8,10},{9,13},{10,... | collective-permute-start | bytes 786440 | tf_op jit(solution)/shard_map/ppermute | solution.py:70
  13.5 16.4 %collective-permute-start.5 = (bf16[4,4,2,32,128]{4,3,2,1,0:T(8,128)(2,1)S(1)}, bf16[4,4,2,32,128]{4,3,2,1,0:T(8,128)(2,1)S(1)}, u32[]{:S(2)}, u32[]{:S(2)}) collective-permute-start(bf16[4,4,2,32,128]{4,3,2,1,0:T(8,128)(2,1)S(1)} %pad_maximum_fusion.qa), channel_id=1, source_target_pairs={{0,4},{1,3},{2,6},{3,1},{4,0},{5,7},{6,2},{7,5},{8,12},{9,11},{10,... | collective-permute-start | bytes 786440 | tf_op jit(solution)/shard_map/ppermute | solution.py:70
  21.2 8.7 %collective-permute-start.6 = (bf16[4,4,2,32,128]{4,3,2,1,0:T(8,128)(2,1)S(1)}, bf16[4,4,2,32,128]{4,3,2,1,0:T(8,128)(2,1)S(1)}, u32[]{:S(2)}, u32[]{:S(2)}) collective-permute-start(bf16[4,4,2,32,128]{4,3,2,1,0:T(8,128)(2,1)S(1)} %collective-permute-done.3.qb), channel_id=1, source_target_pairs={{0,4},{1,3},{2,6},{3,1},{4,0},{5,7},{6,2},{7,5},{8,12},{9,11},{10,... | collective-permute-start | bytes 786440 | tf_op jit(solution)/shard_map/ppermute | solution.py:70
  26.3 10.7 %collective-permute-start.10 = (bf16[528,128]{1,0:T(8,128)(2,1)S(1)}, bf16[528,128]{1,0:T(8,128)(2,1)S(1)}, u32[]{:S(2)}, u32[]{:S(2)}) collective-permute-start(bf16[528,128]{1,0:T(8,128)(2,1)S(1)} %get-tuple-element.45), channel_id=1, source_target_pairs={{0,4},{1,3},{2,6},{3,1},{4,0},{5,7},{6,2},{7,5},{8,12},{9,11},{10,... | collective-permute-start | bytes 405512 | tf_op jit(solution)/shard_map/ppermute | solution.py:70
  28.4 10.2 %collective-permute-start.11 = (bf16[528,128]{1,0:T(8,128)(2,1)S(1)}, bf16[528,128]{1,0:T(8,128)(2,1)S(1)}, u32[]{:S(2)}, u32[]{:S(2)}) collective-permute-start(bf16[528,128]{1,0:T(8,128)(2,1)S(1)} %get-tuple-element.46), channel_id=1, source_target_pairs={{0,6},{1,7},{2,4},{3,5},{4,2},{5,3},{6,0},{7,1},{8,14},{9,15},{10,... | collective-permute-start | bytes 405512 | tf_op jit(solution)/shard_map/ppermute | solution.py:70
  28.4 10.2 %collective-permute-start.4 = (bf16[528,128]{1,0:T(8,128)(2,1)S(1)}, bf16[528,128]{1,0:T(8,128)(2,1)S(1)}, u32[]{:S(2)}, u32[]{:S(2)}) collective-permute-start(bf16[528,128]{1,0:T(8,128)(2,1)S(1)} %get-tuple-element.40), channel_id=1, source_target_pairs={{0,2},{1,5},{2,0},{3,7},{4,6},{5,1},{6,4},{7,3},{8,10},{9,13},{10,... | collective-permute-start | bytes 405512 | tf_op jit(solution)/shard_map/ppermute | solution.py:70
  29.9 42.9 %copy-start = (bf16[4096,512]{1,0:T(8,128)(2,1)S(1)}, bf16[4096,512]{1,0:T(8,128)(2,1)}, u32[]{:S(2)}) copy-start(bf16[4096,512]{1,0:T(8,128)(2,1)} %weight.1) | copy-start | bytes 12582916
  35.0 6.0 %collective-permute-start.7 = (bf16[528,128]{1,0:T(8,128)(2,1)S(1)}, bf16[528,128]{1,0:T(8,128)(2,1)S(1)}, u32[]{:S(2)}, u32[]{:S(2)}) collective-permute-start(bf16[528,128]{1,0:T(8,128)(2,1)S(1)} %get-tuple-element.41), channel_id=1, source_target_pairs={{0,4},{1,3},{2,6},{3,1},{4,0},{5,7},{6,2},{7,5},{8,12},{9,11},{10,... | collective-permute-start | bytes 405512 | tf_op jit(solution)/shard_map/ppermute | solution.py:70
  37.0 5.9 %collective-permute-start.8 = (bf16[528,128]{1,0:T(8,128)(2,1)S(1)}, bf16[528,128]{1,0:T(8,128)(2,1)S(1)}, u32[]{:S(2)}, u32[]{:S(2)}) collective-permute-start(bf16[528,128]{1,0:T(8,128)(2,1)S(1)} %get-tuple-element.42), channel_id=1, source_target_pairs={{0,6},{1,7},{2,4},{3,5},{4,2},{5,3},{6,0},{7,1},{8,14},{9,15},{10,... | collective-permute-start | bytes 405512 | tf_op jit(solution)/shard_map/ppermute | solution.py:70
  37.0 6.0 %collective-permute-start.9 = (bf16[528,128]{1,0:T(8,128)(2,1)S(1)}, bf16[528,128]{1,0:T(8,128)(2,1)S(1)}, u32[]{:S(2)}, u32[]{:S(2)}) collective-permute-start(bf16[528,128]{1,0:T(8,128)(2,1)S(1)} %get-tuple-element.44), channel_id=1, source_target_pairs={{0,2},{1,5},{2,0},{3,7},{4,6},{5,1},{6,4},{7,3},{8,10},{9,13},{10,... | collective-permute-start | bytes 405512 | tf_op jit(solution)/shard_map/ppermute | solution.py:70
  43.4 4.5 %collective-permute-start.12 = (bf16[272,128]{1,0:T(8,128)(2,1)S(1)}, bf16[272,128]{1,0:T(8,128)(2,1)S(1)}, u32[]{:S(2)}, u32[]{:S(2)}) collective-permute-start(bf16[272,128]{1,0:T(8,128)(2,1)S(1)} %get-tuple-element.48), channel_id=1, source_target_pairs={{0,8},{1,9},{2,10},{3,11},{4,12},{5,13},{6,14},{7,15},{8,0},{9,1},... | collective-permute-start | bytes 208904 | tf_op jit(solution)/shard_map/ppermute | solution.py:70
  44.1 8.3 %collective-permute-start.13 = (bf16[272,128]{1,0:T(8,128)(2,1)S(1)}, bf16[272,128]{1,0:T(8,128)(2,1)S(1)}, u32[]{:S(2)}, u32[]{:S(2)}) collective-permute-start(bf16[272,128]{1,0:T(8,128)(2,1)S(1)} %get-tuple-element.49), channel_id=1, source_target_pairs={{0,16},{1,17},{2,18},{3,19},{4,20},{5,21},{6,22},{7,23},{8,24},{9,... | collective-permute-start | bytes 208904 | tf_op jit(solution)/shard_map/ppermute | solution.py:70
  47.5 6.3 %collective-permute-start.14 = (bf16[272,128]{1,0:T(8,128)(2,1)S(1)}, bf16[272,128]{1,0:T(8,128)(2,1)S(1)}, u32[]{:S(2)}, u32[]{:S(2)}) collective-permute-start(bf16[272,128]{1,0:T(8,128)(2,1)S(1)} %get-tuple-element.50), channel_id=1, source_target_pairs={{0,24},{1,25},{2,26},{3,27},{4,28},{5,29},{6,30},{7,31},{8,16},{9,... | collective-permute-start | bytes 208904 | tf_op jit(solution)/shard_map/ppermute | solution.py:70
  54.0 5.2 %collective-permute-start.16 = (bf16[256,128]{1,0:T(8,128)(2,1)S(1)}, bf16[256,128]{1,0:T(8,128)(2,1)S(1)}, u32[]{:S(2)}, u32[]{:S(2)}) collective-permute-start(bf16[256,128]{1,0:T(8,128)(2,1)S(1)} %finish.1), channel_id=1, source_target_pairs={{0,16},{1,17},{2,18},{3,19},{4,20},{5,21},{6,22},{7,23},{8,24},{9,... | collective-permute-start | bytes 196616 | tf_op jit(solution)/shard_map/ppermute | solution.py:70
  56.5 6.2 %collective-permute-start.17 = (bf16[256,128]{1,0:T(8,128)(2,1)S(1)}, bf16[256,128]{1,0:T(8,128)(2,1)S(1)}, u32[]{:S(2)}, u32[]{:S(2)}) collective-permute-start(bf16[256,128]{1,0:T(8,128)(2,1)S(1)} %finish.1), channel_id=1, source_target_pairs={{0,24},{1,25},{2,26},{3,27},{4,28},{5,29},{6,30},{7,31},{8,16},{9,... | collective-permute-start | bytes 196616 | tf_op jit(solution)/shard_map/ppermute | solution.py:70
  57.7 5.0 %collective-permute-start.15 = (bf16[256,128]{1,0:T(8,128)(2,1)S(1)}, bf16[256,128]{1,0:T(8,128)(2,1)S(1)}, u32[]{:S(2)}, u32[]{:S(2)}) collective-permute-start(bf16[256,128]{1,0:T(8,128)(2,1)S(1)} %finish.1), channel_id=1, source_target_pairs={{0,8},{1,9},{2,10},{3,11},{4,12},{5,13},{6,14},{7,15},{8,0},{9,1},... | collective-permute-start | bytes 196616 | tf_op jit(solution)/shard_map/ppermute | solution.py:70
  62.7 6.4 %collective-permute-start.18 = (bf16[4,256,128]{2,1,0:T(8,128)(2,1)S(1)}, bf16[4,256,128]{2,1,0:T(8,128)(2,1)S(1)}, u32[]{:S(2)}, u32[]{:S(2)}) collective-permute-start(bf16[4,256,128]{2,1,0:T(8,128)(2,1)S(1)} %pad_maximum_fusion.1.a0), channel_id=1, source_target_pairs={{0,2},{1,5},{2,0},{3,7},{4,6},{5,1},{6,4},{7,3},{8,10},{9,13},{10,... | collective-permute-start | bytes 786440 | tf_op jit(solution)/shard_map/ppermute | solution.py:70
  63.6 9.2 %collective-permute-start.19 = (bf16[4,256,128]{2,1,0:T(8,128)(2,1)S(1)}, bf16[4,256,128]{2,1,0:T(8,128)(2,1)S(1)}, u32[]{:S(2)}, u32[]{:S(2)}) collective-permute-start(bf16[4,256,128]{2,1,0:T(8,128)(2,1)S(1)} %pad_maximum_fusion.1.a0), channel_id=1, source_target_pairs={{0,4},{1,3},{2,6},{3,1},{4,0},{5,7},{6,2},{7,5},{8,12},{9,11},{10,... | collective-permute-start | bytes 786440 | tf_op jit(solution)/shard_map/ppermute | solution.py:70
  64.4 8.4 %collective-permute-start.20 = (bf16[4,256,128]{2,1,0:T(8,128)(2,1)S(1)}, bf16[4,256,128]{2,1,0:T(8,128)(2,1)S(1)}, u32[]{:S(2)}, u32[]{:S(2)}) collective-permute-start(bf16[4,256,128]{2,1,0:T(8,128)(2,1)S(1)} %pad_maximum_fusion.1.a0), channel_id=1, source_target_pairs={{0,6},{1,7},{2,4},{3,5},{4,2},{5,3},{6,0},{7,1},{8,14},{9,15},{10,... | collective-permute-start | bytes 786440 | tf_op jit(solution)/shard_map/ppermute | solution.py:70
  73.7 1.3 %collective-permute-start.21 = (bf16[4,16,512]{2,1,0:T(8,128)(2,1)S(1)}, bf16[4,16,512]{2,1,0:T(8,128)(2,1)S(1)}, u32[]{:S(2)}, u32[]{:S(2)}) collective-permute-start(bf16[4,16,512]{2,1,0:T(8,128)(2,1)S(1)} %get-tuple-element.52), channel_id=1, source_target_pairs={{0,1},{1,0},{2,3},{3,2},{4,5},{5,4},{6,7},{7,6},{8,9},{9,8},{10,11... | collective-permute-start | bytes 196616 | tf_op jit(solution)/shard_map/ppermute | solution.py:415

commit v6 on v5

--- a/solution.py
+++ b/solution.py
@@ -304,8 +304,9 @@
     )(*parts)
 
 
-def project_kernel(size, a0, a1, a2, a3, weight, kept, sent, whole_rows, product):
-    core = lax.axis_index("tp")
+def project_kernel(size, other, a0, a1, a2, a3, weight, out, whole_rows):
+    side = lax.axis_index("tp") ^ other
+    half = size.tokens // 2
     for index, ref in enumerate((a0, a1, a2, a3)):
         for line in range(size.lines):
             chip = place(size, line, index % 2, index // 2)
@@ -317,36 +318,37 @@
                 whole_rows[kv * size.group + g, pl.ds(at, size.group_tokens), :] = piece
     total = None
     for h in range(0, size.heads, 2):
-        pair = jnp.concatenate([whole_rows[h], whole_rows[h + 1]], axis=1)
+        pair = jnp.concatenate(
+            [
+                jnp.concatenate(
+                    [
+                        whole_rows[k, pl.ds(pl.multiple_of(j * size.tokens + side * half, half), half), :]
+                        for j in range(size.cand)
+                    ]
+                )
+                for k in (h, h + 1)
+            ],
+            axis=1,
+        )
         term = jnp.dot(
             pair,
             weight[pl.ds(h * size.width, 2 * size.width), :],
             preferred_element_type=jnp.float32,
         )
         total = term if total is None else total + term
-    product[...] = total
-    half = size.tokens // 2
     for j in range(size.cand):
-        near = pl.multiple_of(j * size.tokens + core * half, half)
-        far = pl.multiple_of(j * size.tokens + (1 - core) * half, half)
-        kept[j] = product[pl.ds(near, half), :]
-        sent[j] = product[pl.ds(far, half), :].astype(jnp.bfloat16)
-
-
-def project(size, gathered, weight):
+        out[j] = total[j * half : (j + 1) * half].astype(out.dtype)
+
+
+def project(size, other, dtype, gathered, weight):
     columns = weight.shape[1]
-    shape = (size.cand, size.tokens // 2, columns)
     return pl.pallas_call(
-        functools.partial(project_kernel, size),
-        out_shape=[
-            jax.ShapeDtypeStruct(shape, jnp.float32),
-            jax.ShapeDtypeStruct(shape, jnp.bfloat16),
-        ],
+        functools.partial(project_kernel, size, other),
+        out_shape=jax.ShapeDtypeStruct((size.cand, size.tokens // 2, columns), dtype),
         in_specs=[whole()] * 5,
-        out_specs=[whole()] * 2,
+        out_specs=whole(),
         scratch_shapes=[
             pltpu.VMEM((size.heads, size.cand * size.tokens, size.width), jnp.bfloat16),
-            pltpu.VMEM((size.cand * size.tokens, columns), jnp.float32),
         ],
         compiler_params=pltpu.CompilerParams(vmem_limit_bytes=LIMIT),
         name="project",
@@ -410,7 +412,9 @@
     parts = split_merge(size, (near, near_a, far_b, far_ab), (far, far_a, near_b, near_ab))
     parts = [parts[0]] + [hop(size, parts[k], k) for k in range(1, lines)]
     attention = finish(size, parts)
-    kept, sent = project(size, gather_all(size, attention), out_weight)
+    gathered = gather_all(size, attention)
+    sent = project(size, 1, jnp.bfloat16, gathered, out_weight)
+    kept = project(size, 0, jnp.float32, gathered, out_weight)
     cores = lax.axis_size("tp")
     sent = lax.ppermute(sent, "tp", [(i, cores - 1 - i) for i in range(cores)])
     return (kept + sent.astype(jnp.float32)).astype(jnp.bfloat16)

time: 76.3 us -> 76.5 us (level)
  starting transfers between devices: 27.7 us -> 28.8 us
  Pallas kernels: 11.7 us -> 10.8 us
    pallas_call x2, Pallas kernels: 10.2 us -> 8.22 us  [attention_part(): pl.pallas_call(functools.partial(attention_kernel, size, far, places), ou...]
    ppermute x21, waiting for transfers between devices: 28.3 us -> 29.7 us  [hop(): return lax.ppermute(value, ('ctx', 'tp'), pairs)]
    pallas_call x1 -> x2, Pallas kernels: 0.93 us -> 2.05 us  [project(): pl.pallas_call(functools.partial(project_kernel, size, other), out_shape=...]
    ppermute x21, starting transfers between devices: 27.6 us -> 28.7 us  [hop(): return lax.ppermute(value, ('ctx', 'tp'), pairs)]
    ppermute x1, waiting for transfers between devices: 1.24 us -> 0.21 us  [on_device(): sent = lax.ppermute(sent, 'tp', [(i, cores - 1 - i) for i in range(cores)])]
  transfers between devices with their start and end apart: 22 -> 22, of which waited for: 12 -> 13; matrix products, arithmetic and copies ran while one was open for 8% -> 8% of each run, Pallas kernels for 13% -> 12%
where the time goes in v6:
time: 76.5 us; the launch traced here: 76.3 us
  waiting for transfers between devices  29.9 us (39%)
  starting transfers between devices  28.8 us (38%)
  Pallas kernels  10.8 us (14%)
  local copies, waits for them, and re-layouts  4.73 us (6%)
  other arithmetic  1.91 us (2%)
    ppermute x21, waiting for transfers between devices, hop(): return lax.ppermute(value, ('ctx', 'tp'), pairs)  29.7 us
    ppermute x21, starting transfers between devices, hop(): return lax.ppermute(value, ('ctx', 'tp'), pairs)  28.7 us
    pallas_call x2, Pallas kernels, attention_part(): pl.pallas_call(functools.partial(attention_kernel, size, far, places), ou...  8.22 us
    transpose x1, local copies, waits for them, and re-layouts, on_device(): values = jnp.transpose(cached_prompt_values, (2, 0, 1, 3))  3.28 us
    pallas_call x2, Pallas kernels, project(): pl.pallas_call(functools.partial(project_kernel, size, other), out_shape=...  2.05 us
  transfers between devices with their start and end apart: 22, of which 13 were waited for; matrix products, arithmetic and copies ran while one was open for 8% of the time, Pallas kernels for 12%

profile of v6, /device:TPU:0, one launch (start us, length us, event | category | flops | bytes accessed | tf_op | source)
XLA Modules:
  0.0 76.3 jit_solution(11167859229184558848)
XLA Ops:
  0.0 3.0 %collective-permute-start = (bf16[4,2,32,128]{3,2,1,0:T(8,128)(2,1)}, bf16[4,2,32,128]{3,2,1,0:T(8,128)(2,1)S(1)}, u32[]{:S(2)}, u32[]{:S(2)}) collective-permute-start(bf16[4,2,32,128]{3,2,1,0:T(8,128)(2,1)} %param.7), channel_id=1, source_target_pairs={{0,8},{1,9},{2,10},{3,11},{4,12},{5,13},{6,14},{7,15},{8,0},{9,1},... | collective-permute-start | bytes 196616 | tf_op jit(solution)/shard_map/ppermute | solution.py:70
  3.0 2.6 %collective-permute-start.1 = (bf16[4,2,32,128]{3,2,1,0:T(8,128)(2,1)}, bf16[4,2,32,128]{3,2,1,0:T(8,128)(2,1)S(1)}, u32[]{:S(2)}, u32[]{:S(2)}) collective-permute-start(bf16[4,2,32,128]{3,2,1,0:T(8,128)(2,1)} %param.7), channel_id=1, source_target_pairs={{0,16},{1,17},{2,18},{3,19},{4,20},{5,21},{6,22},{7,23},{8,24},{9,... | collective-permute-start | bytes 196616 | tf_op jit(solution)/shard_map/ppermute | solution.py:70
  5.6 0.0 collective-permute-start.2
  5.6 0.8 %convert_reduce_fusion = (s32[4]{0:T(128)S(1)}, s32[4]{0:T(128)S(1)}, s32[4,128]{1,0:T(4,128)S(1)}) fusion(s32[4,128]{1,0:T(4,128)} %param.12, s32[]{:T(128)S(6)} %mul.3), kind=kLoop, calls=%fused_computation.10 | loop fusion | flops 3576 | bytes 4132 | tf_op jit(solution)/shard_map/reduce_sum | solution.py:370
  6.4 0.1 iota_add_fusion
  6.5 0.1 iota_compare_fusion.1
  6.6 0.7 copy.21
  7.3 0.7 copy.20
  8.0 0.0 copy-start.1
  8.1 3.3 %copy_bitcast_fusion = (bf16[4,16,128,128]{3,2,1,0:T(8,128)(2,1)S(1)}, bf16[4,16,128,128]{3,2,1,0:T(8,128)(2,1)S(1)}) fusion(bf16[16,128,4,128]{3,2,1,0:T(4,128)(2,1)} %param.11, bf16[16,128,4,128]{3,2,1,0:T(4,128)(2,1)} %param.10), kind=kLoop, calls=%fused_computation | loop fusion | bytes 8388608 | tf_op jit(solution)/shard_map/transpose | solution.py:392
  11.4 0.2 select_reduce_fusion.lists
  11.6 0.0 collective-permute-done
  11.6 0.0 collective-permute-done.1
  11.6 0.3 collective-permute-done.2
  11.9 0.0 copy-done.1
  12.0 1.6 %collective-permute-start.3 = (bf16[4,4,2,32,128]{4,3,2,1,0:T(8,128)(2,1)S(1)}, bf16[4,4,2,32,128]{4,3,2,1,0:T(8,128)(2,1)S(1)}, u32[]{:S(2)}, u32[]{:S(2)}) collective-permute-start(bf16[4,4,2,32,128]{4,3,2,1,0:T(8,128)(2,1)S(1)} %pad_maximum_fusion.qa), channel_id=1, source_target_pairs={{0,2},{1,5},{2,0},{3,7},{4,6},{5,1},{6,4},{7,3},{8,10},{9,13},{10,... | collective-permute-start | bytes 786440 | tf_op jit(solution)/shard_map/ppermute | solution.py:70
  13.5 1.5 %collective-permute-start.5 = (bf16[4,4,2,32,128]{4,3,2,1,0:T(8,128)(2,1)S(1)}, bf16[4,4,2,32,128]{4,3,2,1,0:T(8,128)(2,1)S(1)}, u32[]{:S(2)}, u32[]{:S(2)}) collective-permute-start(bf16[4,4,2,32,128]{4,3,2,1,0:T(8,128)(2,1)S(1)} %pad_maximum_fusion.qa), channel_id=1, source_target_pairs={{0,4},{1,3},{2,6},{3,1},{4,0},{5,7},{6,2},{7,5},{8,12},{9,11},{10,... | collective-permute-start | bytes 786440 | tf_op jit(solution)/shard_map/ppermute | solution.py:70
  15.0 6.1 %collective-permute-done.3.qb = bf16[4,4,2,32,128]{4,3,2,1,0:T(8,128)(2,1)S(1)} collective-permute-done((bf16[4,4,2,32,128]{4,3,2,1,0:T(8,128)(2,1)S(1)}, bf16[4,4,2,32,128]{4,3,2,1,0:T(8,128)(2,1)S(1)}, u32[]{:S(2)}, u32[]{:S(2)}) %collective-permute-start.3) | collective-permute-done | bytes 262176 | tf_op jit(solution)/shard_map/ppermute | solution.py:70
  21.2 0.1 collective-permute-start.6
  21.2 4.1 %attention.2 = (bf16[528,128]{1,0:T(8,128)(2,1)S(1)}, bf16[528,128]{1,0:T(8,128)(2,1)S(1)}, bf16[528,128]{1,0:T(8,128)(2,1)S(1)}, bf16[528,128]{1,0:T(8,128)(2,1)S(1)}) custom-call(s32[4,16]{1,0:T(4,128)S(1)} %select_reduce_fusion.lists, s32[4]{0:T(128)S(1)} %sub.15.counts, bf16[4,4,2,32,128]{4,3,2,1,0:T(8,128)(2,1)S(1)} %pad_maximum_fusion.qa, ...), custom_call_target="tpu_custom_call" | custom-call | tf_op jit(solution)/shard_map/attention/pallas_call | solution.py:207
  25.3 2.0 %collective-permute-start.10 = (bf16[528,128]{1,0:T(8,128)(2,1)S(1)}, bf16[528,128]{1,0:T(8,128)(2,1)S(1)}, u32[]{:S(2)}, u32[]{:S(2)}) collective-permute-start(bf16[528,128]{1,0:T(8,128)(2,1)S(1)} %get-tuple-element.43), channel_id=1, source_target_pairs={{0,4},{1,3},{2,6},{3,1},{4,0},{5,7},{6,2},{7,5},{8,12},{9,11},{10,... | collective-permute-start | bytes 405512 | tf_op jit(solution)/shard_map/ppermute | solution.py:70
  27.4 1.0 %collective-permute-start.11 = (bf16[528,128]{1,0:T(8,128)(2,1)S(1)}, bf16[528,128]{1,0:T(8,128)(2,1)S(1)}, u32[]{:S(2)}, u32[]{:S(2)}) collective-permute-start(bf16[528,128]{1,0:T(8,128)(2,1)S(1)} %get-tuple-element.44), channel_id=1, source_target_pairs={{0,6},{1,7},{2,4},{3,5},{4,2},{5,3},{6,0},{7,1},{8,14},{9,15},{10,... | collective-permute-start | bytes 405512 | tf_op jit(solution)/shard_map/ppermute | solution.py:70
  28.4 0.5 collective-permute-start.4
  28.9 0.0 collective-permute-done.5.qa
  28.9 0.4 collective-permute-done.6.qb
  29.3 0.0 copy-start
  29.3 4.1 %attention.3 = (bf16[528,128]{1,0:T(8,128)(2,1)S(1)}, bf16[528,128]{1,0:T(8,128)(2,1)S(1)}, bf16[528,128]{1,0:T(8,128)(2,1)S(1)}, bf16[528,128]{1,0:T(8,128)(2,1)S(1)}) custom-call(s32[4,16]{1,0:T(4,128)S(1)} %select_reduce_fusion.lists, s32[4]{0:T(128)S(1)} %sub.15.counts, bf16[4,4,2,32,128]{4,3,2,1,0:T(8,128)(2,1)S(1)} %collective-permute-done.5.qa, ...), custom_call_target="tpu_custom_call" | custom-call | tf_op jit(solution)/shard_map/attention/pallas_call | solution.py:207
  33.4 1.6 %collective-permute-start.7 = (bf16[528,128]{1,0:T(8,128)(2,1)S(1)}, bf16[528,128]{1,0:T(8,128)(2,1)S(1)}, u32[]{:S(2)}, u32[]{:S(2)}) collective-permute-start(bf16[528,128]{1,0:T(8,128)(2,1)S(1)} %get-tuple-element.39), channel_id=1, source_target_pairs={{0,4},{1,3},{2,6},{3,1},{4,0},{5,7},{6,2},{7,5},{8,12},{9,11},{10,... | collective-permute-start | bytes 405512 | tf_op jit(solution)/shard_map/ppermute | solution.py:70
  35.1 2.5 %collective-permute-start.8 = (bf16[528,128]{1,0:T(8,128)(2,1)S(1)}, bf16[528,128]{1,0:T(8,128)(2,1)S(1)}, u32[]{:S(2)}, u32[]{:S(2)}) collective-permute-start(bf16[528,128]{1,0:T(8,128)(2,1)S(1)} %get-tuple-element.40), channel_id=1, source_target_pairs={{0,6},{1,7},{2,4},{3,5},{4,2},{5,3},{6,0},{7,1},{8,14},{9,15},{10,... | collective-permute-start | bytes 405512 | tf_op jit(solution)/shard_map/ppermute | solution.py:70
  37.6 0.0 collective-permute-done.10.refs_6_
  37.6 0.0 collective-permute-start.9
  37.6 0.0 collective-permute-done.11.refs_7_
  37.6 0.0 collective-permute-done.4.refs_1_
  37.6 1.5 %collective-permute-done.7.refs_2_ = bf16[528,128]{1,0:T(8,128)(2,1)S(1)} collective-permute-done((bf16[528,128]{1,0:T(8,128)(2,1)S(1)}, bf16[528,128]{1,0:T(8,128)(2,1)S(1)}, u32[]{:S(2)}, u32[]{:S(2)}) %collective-permute-start.7) | collective-permute-done | bytes 135200 | tf_op jit(solution)/shard_map/ppermute | solution.py:70
  39.1 1.9 %collective-permute-done.8.refs_3_ = bf16[528,128]{1,0:T(8,128)(2,1)S(1)} collective-permute-done((bf16[528,128]{1,0:T(8,128)(2,1)S(1)}, bf16[528,128]{1,0:T(8,128)(2,1)S(1)}, u32[]{:S(2)}, u32[]{:S(2)}) %collective-permute-start.8) | collective-permute-done | bytes 135200 | tf_op jit(solution)/shard_map/ppermute | solution.py:70
  41.0 1.6 %collective-permute-done.9.refs_5_ = bf16[528,128]{1,0:T(8,128)(2,1)S(1)} collective-permute-done((bf16[528,128]{1,0:T(8,128)(2,1)S(1)}, bf16[528,128]{1,0:T(8,128)(2,1)S(1)}, u32[]{:S(2)}, u32[]{:S(2)}) %collective-permute-start.9) | collective-permute-done | bytes 135200 | tf_op jit(solution)/shard_map/ppermute | solution.py:70
  42.6 0.4 split.1
  43.0 1.1 %collective-permute-start.12 = (bf16[272,128]{1,0:T(8,128)(2,1)S(1)}, bf16[272,128]{1,0:T(8,128)(2,1)S(1)}, u32[]{:S(2)}, u32[]{:S(2)}) collective-permute-start(bf16[272,128]{1,0:T(8,128)(2,1)S(1)} %get-tuple-element.46), channel_id=1, source_target_pairs={{0,8},{1,9},{2,10},{3,11},{4,12},{5,13},{6,14},{7,15},{8,0},{9,1},... | collective-permute-start | bytes 208904 | tf_op jit(solution)/shard_map/ppermute | solution.py:70
  44.1 4.0 %collective-permute-start.13 = (bf16[272,128]{1,0:T(8,128)(2,1)S(1)}, bf16[272,128]{1,0:T(8,128)(2,1)S(1)}, u32[]{:S(2)}, u32[]{:S(2)}) collective-permute-start(bf16[272,128]{1,0:T(8,128)(2,1)S(1)} %get-tuple-element.47), channel_id=1, source_target_pairs={{0,16},{1,17},{2,18},{3,19},{4,20},{5,21},{6,22},{7,23},{8,24},{9,... | collective-permute-start | bytes 208904 | tf_op jit(solution)/shard_map/ppermute | solution.py:70
  48.1 0.0 collective-permute-start.14
  48.1 0.0 collective-permute-done.12.refs_1_
  48.1 4.2 %collective-permute-done.13.refs_2_ = bf16[272,128]{1,0:T(8,128)(2,1)S(1)} collective-permute-done((bf16[272,128]{1,0:T(8,128)(2,1)S(1)}, bf16[272,128]{1,0:T(8,128)(2,1)S(1)}, u32[]{:S(2)}, u32[]{:S(2)}) %collective-permute-start.13) | collective-permute-done | bytes 69664 | tf_op jit(solution)/shard_map/ppermute | solution.py:70
  52.3 2.0 %collective-permute-done.14.refs_3_ = bf16[272,128]{1,0:T(8,128)(2,1)S(1)} collective-permute-done((bf16[272,128]{1,0:T(8,128)(2,1)S(1)}, bf16[272,128]{1,0:T(8,128)(2,1)S(1)}, u32[]{:S(2)}, u32[]{:S(2)}) %collective-permute-start.14) | collective-permute-done | bytes 69664 | tf_op jit(solution)/shard_map/ppermute | solution.py:70
  54.3 0.2 finish.1
  54.5 1.9 %collective-permute-start.16 = (bf16[256,128]{1,0:T(8,128)(2,1)S(1)}, bf16[256,128]{1,0:T(8,128)(2,1)S(1)}, u32[]{:S(2)}, u32[]{:S(2)}) collective-permute-start(bf16[256,128]{1,0:T(8,128)(2,1)S(1)} %finish.1), channel_id=1, source_target_pairs={{0,16},{1,17},{2,18},{3,19},{4,20},{5,21},{6,22},{7,23},{8,24},{9,... | collective-permute-start | bytes 196616 | tf_op jit(solution)/shard_map/ppermute | solution.py:70
  56.4 1.2 %collective-permute-start.17 = (bf16[256,128]{1,0:T(8,128)(2,1)S(1)}, bf16[256,128]{1,0:T(8,128)(2,1)S(1)}, u32[]{:S(2)}, u32[]{:S(2)}) collective-permute-start(bf16[256,128]{1,0:T(8,128)(2,1)S(1)} %finish.1), channel_id=1, source_target_pairs={{0,24},{1,25},{2,26},{3,27},{4,28},{5,29},{6,30},{7,31},{8,16},{9,... | collective-permute-start | bytes 196616 | tf_op jit(solution)/shard_map/ppermute | solution.py:70
  57.7 0.4 collective-permute-start.15
  58.0 2.4 %collective-permute-done.16 = bf16[256,128]{1,0:T(8,128)(2,1)S(1)} collective-permute-done((bf16[256,128]{1,0:T(8,128)(2,1)S(1)}, bf16[256,128]{1,0:T(8,128)(2,1)S(1)}, u32[]{:S(2)}, u32[]{:S(2)}) %collective-permute-start.16) | collective-permute-done | bytes 65568 | tf_op jit(solution)/shard_map/ppermute | solution.py:70
  60.4 2.2 %collective-permute-done.17 = bf16[256,128]{1,0:T(8,128)(2,1)S(1)} collective-permute-done((bf16[256,128]{1,0:T(8,128)(2,1)S(1)}, bf16[256,128]{1,0:T(8,128)(2,1)S(1)}, u32[]{:S(2)}, u32[]{:S(2)}) %collective-permute-start.17) | collective-permute-done | bytes 65568 | tf_op jit(solution)/shard_map/ppermute | solution.py:70
  62.6 0.0 collective-permute-done.15
  62.7 1.4 %collective-permute-start.18 = (bf16[4,256,128]{2,1,0:T(8,128)(2,1)S(1)}, bf16[4,256,128]{2,1,0:T(8,128)(2,1)S(1)}, u32[]{:S(2)}, u32[]{:S(2)}) collective-permute-start(bf16[4,256,128]{2,1,0:T(8,128)(2,1)S(1)} %pad_maximum_fusion.1.a0), channel_id=1, source_target_pairs={{0,2},{1,5},{2,0},{3,7},{4,6},{5,1},{6,4},{7,3},{8,10},{9,13},{10,... | collective-permute-start | bytes 786440 | tf_op jit(solution)/shard_map/ppermute | solution.py:70
  64.1 1.4 %collective-permute-start.19 = (bf16[4,256,128]{2,1,0:T(8,128)(2,1)S(1)}, bf16[4,256,128]{2,1,0:T(8,128)(2,1)S(1)}, u32[]{:S(2)}, u32[]{:S(2)}) collective-permute-start(bf16[4,256,128]{2,1,0:T(8,128)(2,1)S(1)} %pad_maximum_fusion.1.a0), channel_id=1, source_target_pairs={{0,4},{1,3},{2,6},{3,1},{4,0},{5,7},{6,2},{7,5},{8,12},{9,11},{10,... | collective-permute-start | bytes 786440 | tf_op jit(solution)/shard_map/ppermute | solution.py:70
  65.5 0.8 collective-permute-start.20
  66.2 2.9 %collective-permute-done.18.a1 = bf16[4,256,128]{2,1,0:T(8,128)(2,1)S(1)} collective-permute-done((bf16[4,256,128]{2,1,0:T(8,128)(2,1)S(1)}, bf16[4,256,128]{2,1,0:T(8,128)(2,1)S(1)}, u32[]{:S(2)}, u32[]{:S(2)}) %collective-permute-start.18) | collective-permute-done | bytes 262176 | tf_op jit(solution)/shard_map/ppermute | solution.py:70
  69.1 4.2 %collective-permute-done.19.a2 = bf16[4,256,128]{2,1,0:T(8,128)(2,1)S(1)} collective-permute-done((bf16[4,256,128]{2,1,0:T(8,128)(2,1)S(1)}, bf16[4,256,128]{2,1,0:T(8,128)(2,1)S(1)}, u32[]{:S(2)}, u32[]{:S(2)}) %collective-permute-start.19) | collective-permute-done | bytes 262176 | tf_op jit(solution)/shard_map/ppermute | solution.py:70
  73.3 0.0 collective-permute-done.20.a3
  73.3 0.0 copy-done
  73.3 1.0 %project.3 = bf16[4,16,512]{2,1,0:T(8,128)(2,1)S(1)} custom-call(bf16[4,256,128]{2,1,0:T(8,128)(2,1)S(1)} %pad_maximum_fusion.1.a0, bf16[4,256,128]{2,1,0:T(8,128)(2,1)S(1)} %collective-permute-done.18.a1, bf16[4,256,128]{2,1,0:T(8,128)(2,1)S(1)} %collective-permute-done.19.a2, bf16[4,256,128]{2,1,0:T(8,128)(2,1)S(1)} %collective-permute-done.20.a3, ...), custom_call_target="tpu_custom_call" | custom-call | tf_op jit(solution)/shard_map/project/pallas_call | solution.py:345
  74.3 0.1 collective-permute-start.21
  74.4 1.0 %project.2 = f32[4,16,512]{2,1,0:T(8,128)S(1)} custom-call(bf16[4,256,128]{2,1,0:T(8,128)(2,1)S(1)} %pad_maximum_fusion.1.a0, bf16[4,256,128]{2,1,0:T(8,128)(2,1)S(1)} %collective-permute-done.18.a1, bf16[4,256,128]{2,1,0:T(8,128)(2,1)S(1)} %collective-permute-done.19.a2, bf16[4,256,128]{2,1,0:T(8,128)(2,1)S(1)} %collective-permute-done.20.a3, ...), custom_call_target="tpu_custom_call" | custom-call | tf_op jit(solution)/shard_map/project/pallas_call | solution.py:345
  75.4 0.2 collective-permute-done.21
  75.7 0.6 add_convert_fusion
  (5 shorter events, 0.1 us)
Async XLA Ops:
  0.0 11.6 %collective-permute-start = (bf16[4,2,32,128]{3,2,1,0:T(8,128)(2,1)}, bf16[4,2,32,128]{3,2,1,0:T(8,128)(2,1)S(1)}, u32[]{:S(2)}, u32[]{:S(2)}) collective-permute-start(bf16[4,2,32,128]{3,2,1,0:T(8,128)(2,1)} %param.7), channel_id=1, source_target_pairs={{0,8},{1,9},{2,10},{3,11},{4,12},{5,13},{6,14},{7,15},{8,0},{9,1},... | collective-permute-start | bytes 196616 | tf_op jit(solution)/shard_map/ppermute | solution.py:70
  3.0 8.6 %collective-permute-start.1 = (bf16[4,2,32,128]{3,2,1,0:T(8,128)(2,1)}, bf16[4,2,32,128]{3,2,1,0:T(8,128)(2,1)S(1)}, u32[]{:S(2)}, u32[]{:S(2)}) collective-permute-start(bf16[4,2,32,128]{3,2,1,0:T(8,128)(2,1)} %param.7), channel_id=1, source_target_pairs={{0,16},{1,17},{2,18},{3,19},{4,20},{5,21},{6,22},{7,23},{8,24},{9,... | collective-permute-start | bytes 196616 | tf_op jit(solution)/shard_map/ppermute | solution.py:70
  5.6 6.3 %collective-permute-start.2 = (bf16[4,2,32,128]{3,2,1,0:T(8,128)(2,1)}, bf16[4,2,32,128]{3,2,1,0:T(8,128)(2,1)S(1)}, u32[]{:S(2)}, u32[]{:S(2)}) collective-permute-start(bf16[4,2,32,128]{3,2,1,0:T(8,128)(2,1)} %param.7), channel_id=1, source_target_pairs={{0,24},{1,25},{2,26},{3,27},{4,28},{5,29},{6,30},{7,31},{8,16},{9,... | collective-permute-start | bytes 196616 | tf_op jit(solution)/shard_map/ppermute | solution.py:70
  8.0 3.9 %copy-start.1 = (bf16[4,2,32,128]{3,2,1,0:T(8,128)(2,1)S(1)}, bf16[4,2,32,128]{3,2,1,0:T(8,128)(2,1)}, u32[]{:S(2)}) copy-start(bf16[4,2,32,128]{3,2,1,0:T(8,128)(2,1)} %param.7) | copy-start | bytes 196612
  12.0 9.2 %collective-permute-start.3 = (bf16[4,4,2,32,128]{4,3,2,1,0:T(8,128)(2,1)S(1)}, bf16[4,4,2,32,128]{4,3,2,1,0:T(8,128)(2,1)S(1)}, u32[]{:S(2)}, u32[]{:S(2)}) collective-permute-start(bf16[4,4,2,32,128]{4,3,2,1,0:T(8,128)(2,1)S(1)} %pad_maximum_fusion.qa), channel_id=1, source_target_pairs={{0,2},{1,5},{2,0},{3,7},{4,6},{5,1},{6,4},{7,3},{8,10},{9,13},{10,... | collective-permute-start | bytes 786440 | tf_op jit(solution)/shard_map/ppermute | solution.py:70
  13.5 15.4 %collective-permute-start.5 = (bf16[4,4,2,32,128]{4,3,2,1,0:T(8,128)(2,1)S(1)}, bf16[4,4,2,32,128]{4,3,2,1,0:T(8,128)(2,1)S(1)}, u32[]{:S(2)}, u32[]{:S(2)}) collective-permute-start(bf16[4,4,2,32,128]{4,3,2,1,0:T(8,128)(2,1)S(1)} %pad_maximum_fusion.qa), channel_id=1, source_target_pairs={{0,4},{1,3},{2,6},{3,1},{4,0},{5,7},{6,2},{7,5},{8,12},{9,11},{10,... | collective-permute-start | bytes 786440 | tf_op jit(solution)/shard_map/ppermute | solution.py:70
  21.2 8.2 %collective-permute-start.6 = (bf16[4,4,2,32,128]{4,3,2,1,0:T(8,128)(2,1)S(1)}, bf16[4,4,2,32,128]{4,3,2,1,0:T(8,128)(2,1)S(1)}, u32[]{:S(2)}, u32[]{:S(2)}) collective-permute-start(bf16[4,4,2,32,128]{4,3,2,1,0:T(8,128)(2,1)S(1)} %collective-permute-done.3.qb), channel_id=1, source_target_pairs={{0,4},{1,3},{2,6},{3,1},{4,0},{5,7},{6,2},{7,5},{8,12},{9,11},{10,... | collective-permute-start | bytes 786440 | tf_op jit(solution)/shard_map/ppermute | solution.py:70
  25.3 12.2 %collective-permute-start.10 = (bf16[528,128]{1,0:T(8,128)(2,1)S(1)}, bf16[528,128]{1,0:T(8,128)(2,1)S(1)}, u32[]{:S(2)}, u32[]{:S(2)}) collective-permute-start(bf16[528,128]{1,0:T(8,128)(2,1)S(1)} %get-tuple-element.43), channel_id=1, source_target_pairs={{0,4},{1,3},{2,6},{3,1},{4,0},{5,7},{6,2},{7,5},{8,12},{9,11},{10,... | collective-permute-start | bytes 405512 | tf_op jit(solution)/shard_map/ppermute | solution.py:70
  27.4 10.2 %collective-permute-start.11 = (bf16[528,128]{1,0:T(8,128)(2,1)S(1)}, bf16[528,128]{1,0:T(8,128)(2,1)S(1)}, u32[]{:S(2)}, u32[]{:S(2)}) collective-permute-start(bf16[528,128]{1,0:T(8,128)(2,1)S(1)} %get-tuple-element.44), channel_id=1, source_target_pairs={{0,6},{1,7},{2,4},{3,5},{4,2},{5,3},{6,0},{7,1},{8,14},{9,15},{10,... | collective-permute-start | bytes 405512 | tf_op jit(solution)/shard_map/ppermute | solution.py:70
  28.4 9.2 %collective-permute-start.4 = (bf16[528,128]{1,0:T(8,128)(2,1)S(1)}, bf16[528,128]{1,0:T(8,128)(2,1)S(1)}, u32[]{:S(2)}, u32[]{:S(2)}) collective-permute-start(bf16[528,128]{1,0:T(8,128)(2,1)S(1)} %get-tuple-element.38), channel_id=1, source_target_pairs={{0,2},{1,5},{2,0},{3,7},{4,6},{5,1},{6,4},{7,3},{8,10},{9,13},{10,... | collective-permute-start | bytes 405512 | tf_op jit(solution)/shard_map/ppermute | solution.py:70
  29.3 44.0 %copy-start = (bf16[4096,512]{1,0:T(8,128)(2,1)S(1)}, bf16[4096,512]{1,0:T(8,128)(2,1)}, u32[]{:S(2)}) copy-start(bf16[4096,512]{1,0:T(8,128)(2,1)} %weight.3) | copy-start | bytes 12582916
  33.4 5.6 %collective-permute-start.7 = (bf16[528,128]{1,0:T(8,128)(2,1)S(1)}, bf16[528,128]{1,0:T(8,128)(2,1)S(1)}, u32[]{:S(2)}, u32[]{:S(2)}) collective-permute-start(bf16[528,128]{1,0:T(8,128)(2,1)S(1)} %get-tuple-element.39), channel_id=1, source_target_pairs={{0,4},{1,3},{2,6},{3,1},{4,0},{5,7},{6,2},{7,5},{8,12},{9,11},{10,... | collective-permute-start | bytes 405512 | tf_op jit(solution)/shard_map/ppermute | solution.py:70
  35.1 5.9 %collective-permute-start.8 = (bf16[528,128]{1,0:T(8,128)(2,1)S(1)}, bf16[528,128]{1,0:T(8,128)(2,1)S(1)}, u32[]{:S(2)}, u32[]{:S(2)}) collective-permute-start(bf16[528,128]{1,0:T(8,128)(2,1)S(1)} %get-tuple-element.40), channel_id=1, source_target_pairs={{0,6},{1,7},{2,4},{3,5},{4,2},{5,3},{6,0},{7,1},{8,14},{9,15},{10,... | collective-permute-start | bytes 405512 | tf_op jit(solution)/shard_map/ppermute | solution.py:70
  37.6 5.0 %collective-permute-start.9 = (bf16[528,128]{1,0:T(8,128)(2,1)S(1)}, bf16[528,128]{1,0:T(8,128)(2,1)S(1)}, u32[]{:S(2)}, u32[]{:S(2)}) collective-permute-start(bf16[528,128]{1,0:T(8,128)(2,1)S(1)} %get-tuple-element.42), channel_id=1, source_target_pairs={{0,2},{1,5},{2,0},{3,7},{4,6},{5,1},{6,4},{7,3},{8,10},{9,13},{10,... | collective-permute-start | bytes 405512 | tf_op jit(solution)/shard_map/ppermute | solution.py:70
  43.0 5.1 %collective-permute-start.12 = (bf16[272,128]{1,0:T(8,128)(2,1)S(1)}, bf16[272,128]{1,0:T(8,128)(2,1)S(1)}, u32[]{:S(2)}, u32[]{:S(2)}) collective-permute-start(bf16[272,128]{1,0:T(8,128)(2,1)S(1)} %get-tuple-element.46), channel_id=1, source_target_pairs={{0,8},{1,9},{2,10},{3,11},{4,12},{5,13},{6,14},{7,15},{8,0},{9,1},... | collective-permute-start | bytes 208904 | tf_op jit(solution)/shard_map/ppermute | solution.py:70
  44.1 8.2 %collective-permute-start.13 = (bf16[272,128]{1,0:T(8,128)(2,1)S(1)}, bf16[272,128]{1,0:T(8,128)(2,1)S(1)}, u32[]{:S(2)}, u32[]{:S(2)}) collective-permute-start(bf16[272,128]{1,0:T(8,128)(2,1)S(1)} %get-tuple-element.47), channel_id=1, source_target_pairs={{0,16},{1,17},{2,18},{3,19},{4,20},{5,21},{6,22},{7,23},{8,24},{9,... | collective-permute-start | bytes 208904 | tf_op jit(solution)/shard_map/ppermute | solution.py:70
  48.1 6.2 %collective-permute-start.14 = (bf16[272,128]{1,0:T(8,128)(2,1)S(1)}, bf16[272,128]{1,0:T(8,128)(2,1)S(1)}, u32[]{:S(2)}, u32[]{:S(2)}) collective-permute-start(bf16[272,128]{1,0:T(8,128)(2,1)S(1)} %get-tuple-element.48), channel_id=1, source_target_pairs={{0,24},{1,25},{2,26},{3,27},{4,28},{5,29},{6,30},{7,31},{8,16},{9,... | collective-permute-start | bytes 208904 | tf_op jit(solution)/shard_map/ppermute | solution.py:70
  54.5 5.9 %collective-permute-start.16 = (bf16[256,128]{1,0:T(8,128)(2,1)S(1)}, bf16[256,128]{1,0:T(8,128)(2,1)S(1)}, u32[]{:S(2)}, u32[]{:S(2)}) collective-permute-start(bf16[256,128]{1,0:T(8,128)(2,1)S(1)} %finish.1), channel_id=1, source_target_pairs={{0,16},{1,17},{2,18},{3,19},{4,20},{5,21},{6,22},{7,23},{8,24},{9,... | collective-permute-start | bytes 196616 | tf_op jit(solution)/shard_map/ppermute | solution.py:70
  56.4 6.2 %collective-permute-start.17 = (bf16[256,128]{1,0:T(8,128)(2,1)S(1)}, bf16[256,128]{1,0:T(8,128)(2,1)S(1)}, u32[]{:S(2)}, u32[]{:S(2)}) collective-permute-start(bf16[256,128]{1,0:T(8,128)(2,1)S(1)} %finish.1), channel_id=1, source_target_pairs={{0,24},{1,25},{2,26},{3,27},{4,28},{5,29},{6,30},{7,31},{8,16},{9,... | collective-permute-start | bytes 196616 | tf_op jit(solution)/shard_map/ppermute | solution.py:70
  57.7 5.0 %collective-permute-start.15 = (bf16[256,128]{1,0:T(8,128)(2,1)S(1)}, bf16[256,128]{1,0:T(8,128)(2,1)S(1)}, u32[]{:S(2)}, u32[]{:S(2)}) collective-permute-start(bf16[256,128]{1,0:T(8,128)(2,1)S(1)} %finish.1), channel_id=1, source_target_pairs={{0,8},{1,9},{2,10},{3,11},{4,12},{5,13},{6,14},{7,15},{8,0},{9,1},... | collective-permute-start | bytes 196616 | tf_op jit(solution)/shard_map/ppermute | solution.py:70
  62.7 6.4 %collective-permute-start.18 = (bf16[4,256,128]{2,1,0:T(8,128)(2,1)S(1)}, bf16[4,256,128]{2,1,0:T(8,128)(2,1)S(1)}, u32[]{:S(2)}, u32[]{:S(2)}) collective-permute-start(bf16[4,256,128]{2,1,0:T(8,128)(2,1)S(1)} %pad_maximum_fusion.1.a0), channel_id=1, source_target_pairs={{0,2},{1,5},{2,0},{3,7},{4,6},{5,1},{6,4},{7,3},{8,10},{9,13},{10,... | collective-permute-start | bytes 786440 | tf_op jit(solution)/shard_map/ppermute | solution.py:70
  64.1 9.2 %collective-permute-start.19 = (bf16[4,256,128]{2,1,0:T(8,128)(2,1)S(1)}, bf16[4,256,128]{2,1,0:T(8,128)(2,1)S(1)}, u32[]{:S(2)}, u32[]{:S(2)}) collective-permute-start(bf16[4,256,128]{2,1,0:T(8,128)(2,1)S(1)} %pad_maximum_fusion.1.a0), channel_id=1, source_target_pairs={{0,4},{1,3},{2,6},{3,1},{4,0},{5,7},{6,2},{7,5},{8,12},{9,11},{10,... | collective-permute-start | bytes 786440 | tf_op jit(solution)/shard_map/ppermute | solution.py:70
  65.5 7.8 %collective-permute-start.20 = (bf16[4,256,128]{2,1,0:T(8,128)(2,1)S(1)}, bf16[4,256,128]{2,1,0:T(8,128)(2,1)S(1)}, u32[]{:S(2)}, u32[]{:S(2)}) collective-permute-start(bf16[4,256,128]{2,1,0:T(8,128)(2,1)S(1)} %pad_maximum_fusion.1.a0), channel_id=1, source_target_pairs={{0,6},{1,7},{2,4},{3,5},{4,2},{5,3},{6,0},{7,1},{8,14},{9,15},{10,... | collective-permute-start | bytes 786440 | tf_op jit(solution)/shard_map/ppermute | solution.py:70
  74.3 1.3 %collective-permute-start.21 = (bf16[4,16,512]{2,1,0:T(8,128)(2,1)S(1)}, bf16[4,16,512]{2,1,0:T(8,128)(2,1)S(1)}, u32[]{:S(2)}, u32[]{:S(2)}) collective-permute-start(bf16[4,16,512]{2,1,0:T(8,128)(2,1)S(1)} %project.3), channel_id=1, source_target_pairs={{0,1},{1,0},{2,3},{3,2},{4,5},{5,4},{6,7},{7,6},{8,9},{9,8},{10,11... | collective-permute-start | bytes 196616 | tf_op jit(solution)/shard_map/ppermute | solution.py:419
